TPU v7x, 32 devices: a whole 2x2x4 slice. The times are simulated.
32 devices in a mesh: leaf: 8 (over z, x), grid: 4 (over y, core).
Axes of the slice: x: 2, y: 2, z: 4, core: 2. Of those that a mesh axis runs over, the one named last changes fastest.
Arguments:
- rhs_rows: float32 [16384, 256], P(('leaf', 'grid')), may hold values from -6 to 6
- order: int32 [16384], P(('leaf', 'grid')), may hold values from 0 to 511, as said below
- leaf_inverse: float32 [16384, 2048], P('leaf', 'grid'), as said below
- leaf_panels: float32 [8, 4, 1024, 2048], P('leaf', None, None, 'grid'), may hold values from -0.046875 to 0.046875
- panel_mask: int32 [8, 4, 16], P('leaf', None, 'grid'), may hold values 0 or 1
- sep_rhs: float32 [8, 1024, 256], P('leaf', None, 'grid'), may hold values from -6 to 6
- sep_inverse: float32 [8, 1024, 1024], P('leaf'), as said below
- sep_panels: float32 [8, 3, 1024, 1024], P('leaf'), may hold values from -0.0625 to 0.0625
Outputs:
- leaf_solution: float32 [16384, 256], P(('leaf', 'grid'))
- sep_solution: float32 [8, 1024, 256], P('leaf', None, 'grid')
- widths: float32 [256], P('grid')
Inputs may be any that keep to these rules, and one draw needn't show every extreme that they name: Each row block of 512 entries of order is a permutation of 0 .. 511. Each leaf's block of leaf_inverse is lower triangular. Each separator's block of sep_inverse is lower triangular.
All inputs are finite; a program needn't handle non-finite values. No bound on the sum of `panel_mask` on one device may be relied on, other than what follows from the above.
Results may differ from a plain program's by a relative error of at most 0.0001.
Values sent between devices are 32-bit elements; how exact they have to be, the bound alone decides.
No kernel may reach another device: no remote copies, remote signals or barrier semaphores. Data moves between devices by JAX's collectives and lax.ppermute only.
A program may use at most 192 MiB of HBM per device.

v0:
```python
import functools

import jax
import jax.numpy as jnp
from jax import lax
from jax.experimental import pallas as pl
from jax.experimental.pallas import tpu as pltpu
from jax.sharding import PartitionSpec as P

HIGH = lax.Precision.HIGH
SMEM = pl.BlockSpec(memory_space=pltpu.SMEM)
VMEM = pl.BlockSpec(memory_space=pltpu.VMEM)
HBM = pl.BlockSpec(memory_space=pl.ANY)
PIECE = 128
MIB = 2**20


def shaped(*shape, dtype=jnp.float32):
    return jax.ShapeDtypeStruct(shape, dtype)


def cost(products):
    return pl.CostEstimate(flops=24 * products, bytes_accessed=4 * 2**20, transcendentals=0)


def limit(mebibytes):
    return pltpu.CompilerParams(vmem_limit_bytes=mebibytes * MIB)


def split(value):
    high = value.astype(jnp.bfloat16)
    return high, (value - high.astype(jnp.float32)).astype(jnp.bfloat16)


def split_wide(value):
    high = value.astype(jnp.bfloat16)
    return high, value - high.astype(jnp.float32)


def in_hbm(value):
    return pltpu.with_memory_space_constraint(value, pltpu.HBM)


def in_vmem(value):
    return pltpu.with_memory_space_constraint(value, pltpu.VMEM)


def pieces(source, held, arrived):
    copies = []
    for step in range(held.shape[0] // PIECE):
        at = pl.ds(step * PIECE, PIECE)
        copies.append(pltpu.make_async_copy(source.at[at], held.at[at], arrived.at[step]))
        copies[step].start()
    return copies


def wait(copies, rows):
    for copy in copies[rows.start // PIECE : rows.stop // PIECE]:
        copy.wait()


def whole(*shape):
    return pl.BlockSpec(shape, lambda *step: (0,) * len(shape))


def pick_kernel(order, rows, out):
    size = rows.shape[0]
    place = lax.broadcasted_iota(jnp.int32, (size, size), 0)
    chosen = jnp.where(place == order[...], 1.0, 0.0).T.astype(jnp.bfloat16)
    high, rest = split_wide(rows[...])
    middle, low = split(rest)
    value = jnp.dot(chosen, high, preferred_element_type=jnp.float32)
    value = value + jnp.dot(chosen, middle, preferred_element_type=jnp.float32)
    out[...] = value + jnp.dot(chosen, low, preferred_element_type=jnp.float32)


def pick(rows, order):
    size, columns = rows.shape
    return pl.pallas_call(
        pick_kernel,
        out_shape=shaped(size, columns),
        grid=(1,),
        in_specs=[whole(1, size), whole(size, columns)],
        out_specs=whole(size, columns),
        cost_estimate=cost(size * size * columns),
        compiler_params=limit(12),
    )(in_hbm(order.reshape(1, size)), in_hbm(rows))


def product_kernel(last_two, place, matrix, rows, *outs):
    size = rows.shape[0]
    for step in range(2):
        block = 2 + ((place[0] & 1) ^ (1 - step)) if last_two else 1 - step
        at = pl.ds(pl.multiple_of(block * size, size), size)
        value = jnp.dot(
            matrix[at], rows[...], precision=HIGH, preferred_element_type=jnp.float32
        )
        if last_two:
            outs[step][...] = value
        elif step == 0:
            outs[0][...] = value[: size // 2]
            outs[1][...] = value[size // 2 :]
        else:
            outs[2][...] = value


def two_products(place, matrix, rows, last_two):
    size, columns = rows.shape
    shapes = [size, size] if last_two else [size // 2, size // 2, size]
    return pl.pallas_call(
        functools.partial(product_kernel, last_two),
        out_shape=[shaped(count, columns) for count in shapes],
        in_specs=[SMEM, VMEM, VMEM],
        out_specs=[VMEM] * len(shapes),
        cost_estimate=cost(2 * size * size * columns),
        compiler_params=limit(8),
    )(place, in_vmem(matrix), rows)


def update_of(turned, scale, panel):
    return lax.dot_general(
        turned * scale,
        panel,
        (((1,), (1,)), ((), ())),
        precision=HIGH,
        preferred_element_type=jnp.float32,
    )


def hand_out(value, core, rows, lanes, width, given, kept):
    for mine in range(2):

        @pl.when(core == mine)
        def _(mine=mine):
            for half in range(2):
                at = (2 * half + mine) * width
                other = (2 * half + 1 - mine) * width
                kept[half, rows, lanes] = value[at : at + width]
                given[half, rows, lanes] = value[other : other + width]


def first_update_kernel(
    width, where, kept_in, in_chip, between, lowest, top, bottom, pair_top, pair_bottom, scale, panels,
    leaf_y, turned, squares, given, kept
):
    place = where[0]

    @pl.when(place == 0)
    def _():
        leaf_y[...] = lowest[...]

    @pl.when(place == 1)
    def _():
        middle = leaf_y.shape[0] // 2
        leaf_y[:middle] = top[...] + pair_top[...]
        leaf_y[middle:] = bottom[...] + pair_bottom[...]

    @pl.when(place == 2)
    def _():
        leaf_y[...] = kept_in[...] + between[...]

    @pl.when(place == 3)
    def _():
        leaf_y[...] = (kept_in[...] + in_chip[...]) + between[...]

    turned[...] = leaf_y[...].T
    value = update_of(turned[...], scale[0:1], panels[0])
    hand_out(value, place & 1, slice(None), slice(None), width, given, kept)
    own = jnp.sum(leaf_y[...] * leaf_y[...], axis=0, keepdims=True)
    squares[...] = jnp.broadcast_to(own, squares.shape)


def first_update(where, parts, scale, panels):
    size, columns = parts[0].shape
    rows = panels.shape[1]
    width = columns // 4
    halves = shaped(2, width, rows)
    return pl.pallas_call(
        functools.partial(first_update_kernel, width),
        out_shape=(
            shaped(size, columns), shaped(columns, size), shaped(8, columns), halves, halves
        ),
        in_specs=[SMEM] + [VMEM] * (len(parts) + 2),
        out_specs=(VMEM,) * 5,
        cost_estimate=cost(size * rows * columns),
        compiler_params=limit(12),
    )(where, *parts, scale, in_vmem(panels))


def second_update_kernel(width, where, turned, scale, panels, given, kept):
    every = slice(None)
    value = update_of(turned[...], scale[1:2], panels[1])
    hand_out(value, where[0] & 1, every, every, width, given, kept)


def second_update(where, turned, scale, panels):
    columns, size = turned.shape
    rows = panels.shape[1]
    width = columns // 4
    halves = shaped(2, width, rows)
    return pl.pallas_call(
        functools.partial(second_update_kernel, width),
        out_shape=(halves, halves),
        in_specs=[SMEM] + [VMEM] * 3,
        out_specs=(VMEM, VMEM),
        cost_estimate=cost(size * rows * columns),
        compiler_params=limit(8),
    )(where, turned, scale, in_vmem(panels))


def later_update_kernel(width, where, squares, turned, scale, panels, given, kept):
    core = where[0] & 1
    tiers = panels.shape[0]
    for tier in range(2, tiers):
        value = update_of(turned[...], scale[tier : tier + 1], panels[tier])
        rows = slice((tier - 2) * width, (tier - 1) * width)
        hand_out(value, core, rows, slice(None), width, given, kept)
    at = (tiers - 2) * width
    for refs, of in ((given, 1 - core), (kept, core)):
        refs[:, at:, :] = jnp.zeros((2, 8, refs.shape[2]), jnp.float32)
        for half in range(2):
            pair = squares[:, 2 * width * half : 2 * width * (half + 1)]
            pair = jnp.where(of == 0, pair, pltpu.roll(pair, width, 1))
            refs[half, at:, 0 : 2 * width] = pair


def later_updates(where, squares, turned, scale, panels):
    columns, size = turned.shape
    tiers, rows = panels.shape[:2]
    width = columns // 4
    halves = shaped(2, (tiers - 2) * width + 8, rows)
    return pl.pallas_call(
        functools.partial(later_update_kernel, width),
        out_shape=(halves, halves),
        in_specs=[SMEM] + [VMEM] * 4,
        out_specs=(VMEM, VMEM),
        cost_estimate=cost(1),
        compiler_params=limit(12),
    )(where, squares, turned, scale, in_vmem(panels))


def chip_sum_kernel(where, kept, got, own, away):
    half = where[0] >> 1
    own[...] = kept[half] + got[half]
    away[...] = kept[1 - half] + got[1 - half]


def chip_sum(where, kept, got):
    shape = shaped(*kept.shape[1:])
    return pl.pallas_call(
        chip_sum_kernel,
        out_shape=(shape, shape),
        in_specs=[SMEM, VMEM, VMEM],
        out_specs=(VMEM, VMEM),
        cost_estimate=cost(1),
        compiler_params=limit(6),
    )(where, kept, got)


def prepare_kernel(
    inverse, panels, out, wide, direct_high, direct_low, high, low, inverse_arrived, panel_arrived, gone
):
    rows = high.shape[0]
    block = rows // 4
    copies = pieces(inverse.at[0], wide.at[0], inverse_arrived)
    pieces(panels.at[0, 0], wide.at[1], panel_arrived)
    for at in range(0, rows, block):
        part = slice(at, at + block)
        wait(copies, part)
        high[part], low[part] = split(wide[0, part])
    sent = [
        pltpu.make_async_copy(source, out.at[2 + step], gone.at[step])
        for step, source in enumerate((high, low))
    ]
    for copy in sent:
        copy.start()

    def part_sent(step):
        part = pl.ds(pl.multiple_of(step * block, block), block)
        return [
            pltpu.make_async_copy(source.at[part], out.at[which, part], gone.at[2 + which])
            for which, source in enumerate((direct_high, direct_low))
        ]

    @pl.loop(0, 4)
    def _(step):
        part = pl.ds(pl.multiple_of(step * block, block), block)
        for piece in range(block // PIECE):
            at = pl.ds(pl.multiple_of(step * block + piece * PIECE, PIECE), PIECE)
            pltpu.make_async_copy(
                panels.at[0, 0, at], wide.at[1, at], panel_arrived.at[step * (block // PIECE) + piece]
            ).wait()
        panel_high, panel_low = split(wide[1, part])
        for at in range(0, rows, block):
            lanes = slice(at, at + block)
            both = high[at:, lanes]
            value = jnp.dot(panel_high[:, at:], both, preferred_element_type=jnp.float32)
            value = value + jnp.dot(panel_low[:, at:], both, preferred_element_type=jnp.float32)
            value = value + jnp.dot(
                panel_high[:, at:], low[at:, lanes], preferred_element_type=jnp.float32
            )
            direct_high[part, lanes], direct_low[part, lanes] = split(value)

        @pl.when(step > 0)
        def _():
            for copy in part_sent(step - 1):
                copy.wait()

        for copy in part_sent(step):
            copy.start()

    for copy in sent + part_sent(3):
        copy.wait()


def prepared(sep_inverse, sep_panels):
    rows = sep_inverse.shape[1]
    return pl.pallas_call(
        prepare_kernel,
        out_shape=pltpu.HBM((4, rows, rows), jnp.bfloat16),
        in_specs=[HBM] * 2,
        out_specs=HBM,
        scratch_shapes=[pltpu.VMEM((2, rows, rows), jnp.float32)]
        + [pltpu.VMEM((rows, rows), jnp.bfloat16)] * 4
        + [
            pltpu.SemaphoreType.DMA((rows // PIECE,)),
            pltpu.SemaphoreType.DMA((rows // PIECE,)),
            pltpu.SemaphoreType.DMA((4,)),
        ],
        cost_estimate=cost(rows**3),
        compiler_params=limit(24),
    )(in_hbm(sep_inverse), in_hbm(sep_panels))


def load_kernel(halves, panels, halves_out, panels_out, arrived):
    copies = [(panels.at[0, step], panels_out.at[step]) for step in range(panels_out.shape[0])]
    copies += [(halves.at[step], halves_out.at[step]) for step in range(4)]
    copies = [
        pltpu.make_async_copy(source, target, arrived.at[step])
        for step, (source, target) in enumerate(copies)
    ]
    for copy in copies:
        copy.start()
    for copy in copies:
        copy.wait()


def loaded(halves, leaf_panels):
    return pl.pallas_call(
        load_kernel,
        out_shape=(
            pltpu.VMEM(halves.shape, jnp.bfloat16),
            pltpu.VMEM(leaf_panels.shape[1:], jnp.float32),
        ),
        in_specs=[HBM] * 2,
        out_specs=(VMEM,) * 2,
        scratch_shapes=[pltpu.SemaphoreType.DMA((4 + leaf_panels.shape[1],))],
        cost_estimate=cost(1),
        compiler_params=limit(4),
    )(in_hbm(halves), in_hbm(leaf_panels))


def load_panel_kernel(panels, out, arrived):
    copies = pieces(panels.at[0, 1], out, arrived)
    wait(copies, slice(0, out.shape[0]))


def loaded_panel(panels):
    rows = panels.shape[2]
    return pl.pallas_call(
        load_panel_kernel,
        out_shape=pltpu.VMEM(panels.shape[2:], jnp.float32),
        in_specs=[HBM],
        out_specs=VMEM,
        scratch_shapes=[pltpu.SemaphoreType.DMA((rows // PIECE,))],
        cost_estimate=cost(1),
        compiler_params=limit(4),
    )(in_hbm(panels))


def operands(value):
    width = value.shape[1] // 2
    lane = lax.broadcasted_iota(jnp.int32, value.shape, 1)
    high = value.astype(jnp.bfloat16)
    as_wide = high.astype(jnp.float32)
    return jnp.where(lane < width, as_wide, value - as_wide).astype(jnp.bfloat16), high


def applied(matrix_high, matrix_low, both, high):
    first = jnp.dot(matrix_high, both, preferred_element_type=jnp.float32)
    second = jnp.dot(matrix_low, high, preferred_element_type=jnp.float32)
    return (first + pltpu.roll(first, first.shape[1] // 2, 1)) + second


def doubled(value):
    return jnp.concatenate([value, value], axis=0).T


def left_of(own_rhs, parts):
    whole_parts = [part[...] for part in parts if part.shape == own_rhs.shape]
    halves = [part[...] for part in parts if part.shape != own_rhs.shape]
    total = whole_parts[0]
    for part in whole_parts[1:]:
        total = total + part
    if halves:
        total = total + jnp.concatenate(halves, axis=0)
    return own_rhs[...] - total


def direct_kernel(count, own_rhs, halves, *refs):
    parts, (left, term) = refs[:count], refs[count:]
    left[...] = left_of(own_rhs, parts)
    value = applied(halves[0], halves[1], *operands(doubled(left[...])))
    term[...] = value.T[: term.shape[0]]


def direct(own_rhs, halves, parts):
    width, rows = own_rhs.shape
    return pl.pallas_call(
        functools.partial(direct_kernel, len(parts)),
        out_shape=(shaped(width, rows), shaped(width, rows)),
        in_specs=[VMEM] * (2 + len(parts)),
        out_specs=(VMEM, VMEM),
        cost_estimate=cost(rows**2 * 4096),
        compiler_params=limit(8),
    )(own_rhs, in_vmem(halves), *parts)


def tail_of(copies, held, both, high, width, out):
    rows = held.shape[0]
    block = rows // 4
    for at in range(0, rows, block):
        part = slice(at, at + block)
        if copies:
            wait(copies, part)
        out[:width, part] = applied(*split(held[part]), both, high).T[:width]


def with_squares(out, width, squares):
    out[width:, :] = jnp.zeros((8, out.shape[1]), jnp.float32)
    out[width:, : squares.shape[1]] = squares[...]


def solve_kernel(tier, last, with_tail, where, left, halves, solved, *refs):
    panel, refs = refs[0] if with_tail else None, refs[with_tail:]
    out, squares, kept, *sent = refs
    width = left.shape[0]
    value = applied(halves[2], halves[3], *operands(doubled(left[...])))
    mine = value.T[:width]
    kept[...] = value

    @pl.when(where[2] == tier)
    def _():
        out[...] = mine

    @pl.when(where[2] != tier)
    def _():
        out[...] = solved[...]

    own = jnp.sum(value * value, axis=0, keepdims=True)
    squares[...] = jnp.broadcast_to(own, squares.shape)
    if sent:
        tail_of(None, panel, *operands(value), width, sent[0])
        if last:
            with_squares(sent[0], width, squares)


def solve(where, tier, left, halves, solved, panel=None, last=False):
    width, rows = left.shape
    with_tail = panel is not None
    return pl.pallas_call(
        functools.partial(solve_kernel, tier, last, with_tail),
        out_shape=[shaped(width, rows), shaped(8, 2 * width), shaped(rows, 2 * width)]
        + [shaped(width + 8 * last, rows)] * with_tail,
        in_specs=[SMEM] + [VMEM] * (3 + with_tail),
        out_specs=[VMEM] * (3 + with_tail),
        cost_estimate=cost(1),
        compiler_params=limit(8),
    )(where, left, in_vmem(halves), solved, *([in_vmem(panel)] if with_tail else []))


def tails_kernel(value, squares, panels, *refs):
    sent, (held, arrived) = refs[:-2], refs[-2:]
    width = squares.shape[1] // 2
    copies = [
        pieces(panels.at[0, 2 + step], held.at[step], arrived.at[step])
        for step in range(held.shape[0])
    ]
    both, high = operands(value[...])
    for step, out in enumerate(sent):
        tail_of(copies[step], held.at[step], both, high, width, out)
    with_squares(sent[-1], width, squares)


def more_tails(value, squares, panels, count):
    rows = value.shape[0]
    width = squares.shape[1] // 2
    shapes = [(width + 8 * (step == count - 1), rows) for step in range(count)]
    return pl.pallas_call(
        tails_kernel,
        out_shape=[shaped(*shape) for shape in shapes],
        in_specs=[VMEM, VMEM, HBM],
        out_specs=[VMEM] * count,
        scratch_shapes=[
            pltpu.VMEM((count, rows, rows), jnp.float32),
            pltpu.SemaphoreType.DMA((count, rows // PIECE)),
        ],
        cost_estimate=cost(1),
        compiler_params=limit(8 + 4 * count),
    )(value, squares, in_hbm(panels))


def last_kernel(leaves, count, where, own_rhs, halves, squares, got, first, second, kept, widths):
    left = left_of(own_rhs, (first, second))
    value = applied(halves[2], halves[3], *operands(doubled(left)))
    kept[...] = value
    total = (squares[...] + got[...]) + jnp.sum(value * value, axis=0, keepdims=True)
    value = jnp.sqrt(total / count + 1e-06)
    widths[...] = jnp.where(where[1] == leaves - 1, value, 0.0)


def last(leaves, count, where, own_rhs, halves, squares, got, parts):
    width, rows = own_rhs.shape
    return pl.pallas_call(
        functools.partial(last_kernel, leaves, count),
        out_shape=(shaped(rows, 2 * width), shaped(*squares.shape)),
        in_specs=[SMEM] + [VMEM] * 6,
        out_specs=(VMEM, VMEM),
        cost_estimate=cost(1),
        compiler_params=limit(8),
    )(where, own_rhs, in_vmem(halves), squares, got, *parts)


def settle_kernel(tiers, where, solved, value, out):
    width = out.shape[0]

    @pl.when(where[2] == tiers)
    def _():
        out[...] = value[...].T[:width]

    @pl.when(where[2] != tiers)
    def _():
        out[...] = solved[...]


def settled(tiers, where, solved, value):
    return pl.pallas_call(
        functools.partial(settle_kernel, tiers),
        out_shape=shaped(*solved.shape),
        in_specs=[SMEM, VMEM, VMEM],
        out_specs=VMEM,
        cost_estimate=cost(1),
        compiler_params=limit(6),
    )(where, solved, value)


def local(rhs_rows, order, leaf_inverse, leaf_panels, panel_mask, sep_rhs, sep_inverse, sep_panels):
    n_leaf = lax.axis_size("leaf")
    n_grid = lax.axis_size("grid")
    tiers = leaf_panels.shape[1]
    block_rows, columns = rhs_rows.shape
    block_count = n_leaf * n_grid
    sep_rows = sep_rhs.shape[1]
    width = columns // n_grid
    leaf = lax.axis_index("leaf").astype(jnp.int32)
    grid = lax.axis_index("grid").astype(jnp.int32)
    level = jnp.ones((), jnp.int32)
    for bit in range(1, tiers):
        level = level + ((leaf + 1) & (2**bit - 1) == 0).astype(jnp.int32)
    where = jnp.stack([grid, leaf, level])
    scale = jnp.repeat(panel_mask[0].astype(jnp.float32), 128, axis=1)

    picked = pick(rhs_rows, order)
    picked, where = lax.optimization_barrier((picked, where))
    moved = lax.all_to_all(
        picked.reshape(block_count, block_rows // block_count, columns),
        ("leaf", "grid"),
        split_axis=0,
        concat_axis=0,
        tiled=True,
    )
    permuted = moved.reshape(block_rows, columns)

    _, inverse, own_panels = lax.optimization_barrier((picked, sep_inverse, sep_panels))
    halves = prepared(inverse, own_panels)
    permuted, halves = lax.optimization_barrier((permuted, halves))

    given, kept = two_products(where, leaf_inverse, permuted, True)
    in_chip = lax.ppermute(given, "grid", [(0, 1), (1, 0), (2, 3)])
    onward = kept + in_chip
    onward, permuted, halves = lax.optimization_barrier((onward, permuted, halves))
    between = lax.ppermute(onward, "grid", [(0, 2), (1, 3)])
    *low_block, lowest = two_products(where, leaf_inverse, permuted, False)
    from_pair = [lax.ppermute(part, "grid", [(0, 1)]) for part in low_block]
    halves, panels = loaded(halves, leaf_panels)

    leaf_y, turned, squares, given, kept = first_update(
        where, (kept, in_chip, between, lowest, *low_block, *from_pair), scale, panels
    )
    swap = [(0, 1), (1, 0), (2, 3), (3, 2)]
    over = [(0, 2), (1, 3), (2, 0), (3, 1)]
    got = lax.ppermute(given, "grid", swap)
    given, other = second_update(where, turned, scale, panels)
    own, away = chip_sum(where, kept, got)
    away, given, turned = lax.optimization_barrier((away, given, turned))
    got = lax.ppermute(away, "grid", over)
    second, away = chip_sum(where, other, lax.ppermute(given, "grid", swap))
    given, kept = later_updates(where, squares, turned, scale, panels)
    got, away, given = lax.optimization_barrier((got, away, given))
    mine = own + got
    following = second + lax.ppermute(away, "grid", over)
    own, away = chip_sum(where, kept, lax.ppermute(given, "grid", swap))
    pairs = [(base + 1, base) for base in range(0, n_leaf, 2)]
    own, own_panels = lax.optimization_barrier((own, sep_panels))
    next_panel = loaded_panel(own_panels)
    got, own, next_panel = lax.optimization_barrier(
        (lax.ppermute(mine, "leaf", pairs), own, next_panel)
    )
    parts = [mine, got]
    edges = [(step * width, (step + 1) * width) for step in range(tiers - 2)]
    edges[-1] = (edges[-1][0], own.shape[0])
    rest = [
        own[start:stop] + lax.ppermute(away[start:stop], "grid", over) for start, stop in edges
    ]

    own_rhs = sep_rhs[0].T
    solved = jnp.zeros_like(own_rhs)
    waiting = []
    for tier in range(1, tiers):
        size = 2**tier
        direct_left, direct_right, early, onward, aside = [], [], [], [], []
        for base in range(0, n_leaf, size):
            host, end = (base + size // 2 - 1, base + size - 1)
            parent = base // (2 * size) * 2 * size + size - 1
            onward.append((host, end))
            if end == parent:
                direct_left.append((host, parent))
            else:
                direct_right.append((host, parent))
                early.append((end, parent))
                aside.append((host, end))
        left, term = direct(own_rhs, halves, parts)
        count = len(rest)
        solved, own, *more = solve(
            where, tier, left, halves, solved, next_panel if count else None, count == 1
        )
        if waiting:
            _, following, *waiting = lax.optimization_barrier((left, following, *waiting))
            rest = [
                other + lax.ppermute(other + tail, "leaf", before)
                for other, tail in zip(rest, waiting)
            ]
        if count:
            value, tail = more
            next_early = lax.ppermute(following, "leaf", early)
            term = following + term
            from_left = lax.ppermute(term, "leaf", direct_left)
            parts = [following, next_early, from_left]
            if tier == 1:
                turn = lax.ppermute(term[width // 2 :], "leaf", aside)
                parts.append(lax.ppermute(term[: width // 2], "leaf", direct_right))
                parts.append(lax.ppermute(turn, "leaf", early))
            else:
                parts.append(lax.ppermute(term, "leaf", direct_right))
            following = rest[0] + lax.ppermute(rest[0] + tail, "leaf", onward)
            rest = rest[1:]
            waiting = []
            if count > 1:
                value, _ = lax.optimization_barrier((value, from_left))
                waiting = more_tails(value, own, sep_panels, count - 1)
                parts[1], *waiting = lax.optimization_barrier((parts[1], *waiting))
            before = onward
        else:
            squares = following[width:, : 2 * width]
            following = following[:width]
            parts = [following, lax.ppermute(following + term, "leaf", direct_left)]
            got = lax.ppermute(squares + own, "leaf", direct_left)
    value, widths = last(
        n_leaf,
        n_leaf * (block_rows * n_grid + sep_rows),
        where,
        own_rhs,
        halves,
        squares,
        got,
        parts,
    )
    solved = settled(tiers, where, solved, value)
    step = n_leaf
    while step > 1:
        half_step = step // 2
        steps = [(end, end - half_step) for end in range(step - 1, n_leaf, step)]
        widths = widths + lax.ppermute(widths, "leaf", steps)
        step = half_step
    return (leaf_y, solved.T[None], widths[0, :width])


def solution(mesh):
    placed = (
        P(("leaf", "grid"), None),
        P(("leaf", "grid")),
        P("leaf", "grid"),
        P("leaf", None, None, "grid"),
        P("leaf", None, "grid"),
        P("leaf", None, "grid"),
        P("leaf", None, None),
        P("leaf", None, None, None),
    )
    return jax.shard_map(
        local,
        mesh=mesh,
        in_specs=placed,
        out_specs=(P(("leaf", "grid"), None), P("leaf", None, "grid"), P("grid")),
        check_vma=False,
    )
```

profile of v0, /device:TPU:0, one launch (start us, length us, event | category | flops | bytes accessed | tf_op | source)
XLA Modules:
  0.0 142.7 jit_solution(6596659104861790109)
XLA Ops:
  0.6 2.5 %shard_map.103 = f32[512,256]{1,0:T(8,128)} custom-call(s32[1,512]{1,0:T(1,128)} %bitcast.31, f32[512,256]{1,0:T(8,128)} %rows.1), custom_call_target="tpu_custom_call" | custom-call | flops 1610612736 | bytes 4194304 | tf_op jit(solution)/shard_map/pallas_call | solution.py:79
  3.3 7.3 %all-to-all-start = ((f32[32,16,256]{2,1,0:T(8,128)}), f32[32,16,256]{2,1,0:T(8,128)S(1)}, u32[]{:S(2)}, u32[]{:S(2)}) async-start(f32[32,16,256]{2,1,0:T(8,128)} %bitcast.4), calls=%async_computation | async-start | bytes 1048576 | tf_op jit(solution)/shard_map/all_to_all | solution.py:575
  10.6 8.4 %shard_map.104.halves = bf16[4,1024,1024]{2,1,0:T(8,128)(2,1)} custom-call(f32[1,1024,1024]{2,1,0:T(8,128)} %inverse, f32[1,3,1024,1024]{3,2,1,0:T(8,128)} %panels.5), custom_call_target="tpu_custom_call" | custom-call | flops 25769803776 | bytes 4194304 | tf_op jit(solution)/shard_map/pallas_call | solution.py:318
  19.0 7.1 %all-to-all-done = f32[32,16,256]{2,1,0:T(8,128)S(1)} async-done(((f32[32,16,256]{2,1,0:T(8,128)}), f32[32,16,256]{2,1,0:T(8,128)S(1)}, u32[]{:S(2)}, u32[]{:S(2)}) %all-to-all-start) | async-done | bytes 524320 | tf_op jit(solution)/shard_map/all_to_all | solution.py:575
  26.1 2.2 %copy-done.1 = f32[2048,512]{1,0:T(8,128)S(1)} copy-done((f32[2048,512]{1,0:T(8,128)S(1)}, f32[2048,512]{1,0:T(8,128)}, u32[]{:S(2)}) %copy-start.1) | copy-done | bytes 4194328
  29.8 1.9 %collective-permute-start = (f32[512,256]{1,0:T(8,128)S(1)}, f32[512,256]{1,0:T(8,128)S(1)}, u32[]{:S(2)}, u32[]{:S(2)}) collective-permute-start(f32[512,256]{1,0:T(8,128)S(1)} %get-tuple-element.72), channel_id=1, source_target_pairs={{0,1},{1,0},{2,3},{4,5},{5,4},{6,7},{8,9},{9,8},{10,11},{12,13},{1... | collective-permute-start | bytes 1572872 | tf_op jit(solution)/shard_map/ppermute | solution.py:589
  31.8 1.9 %collective-permute-done.in_chip = f32[512,256]{1,0:T(8,128)S(1)} collective-permute-done((f32[512,256]{1,0:T(8,128)S(1)}, f32[512,256]{1,0:T(8,128)S(1)}, u32[]{:S(2)}, u32[]{:S(2)}) %collective-permute-start) | collective-permute-done | bytes 524320 | tf_op jit(solution)/shard_map/ppermute | solution.py:589
  33.7 2.9 %collective-permute-start.1 = (f32[512,256]{1,0:T(8,128)S(1)}, f32[512,256]{1,0:T(8,128)S(1)}, u32[]{:S(2)}, u32[]{:S(2)}) collective-permute-start(f32[512,256]{1,0:T(8,128)S(1)} %add.72), channel_id=1, source_target_pairs={{0,2},{1,3},{4,6},{5,7},{8,10},{9,11},{12,14},{13,15},{16,18},{17,... | collective-permute-start | bytes 1572872 | tf_op jit(solution)/shard_map/ppermute | solution.py:592
  38.2 2.0 %collective-permute-start.2 = (f32[256,256]{1,0:T(8,128)S(1)}, f32[256,256]{1,0:T(8,128)S(1)}, u32[]{:S(2)}, u32[]{:S(2)}) collective-permute-start(f32[256,256]{1,0:T(8,128)S(1)} %get-tuple-element.77.top), channel_id=1, source_target_pairs={{0,1},{4,5},{8,9},{12,13},{16,17},{20,21},{24,25},{28,29}} | collective-permute-start | bytes 786440 | tf_op jit(solution)/shard_map/ppermute | solution.py:594
  41.6 5.9 %shard_map.107 = (bf16[4,1024,1024]{2,1,0:T(8,128)(2,1)S(1)}, f32[4,1024,512]{2,1,0:T(8,128)S(1)}) custom-call(bf16[4,1024,1024]{2,1,0:T(8,128)(2,1)} %shard_map.104.halves, f32[1,4,1024,512]{3,2,1,0:T(8,128)} %panels.3), custom_call_target="tpu_custom_call" | custom-call | flops 24 | bytes 4194304 | tf_op jit(solution)/shard_map/pallas_call | solution.py:349
  48.3 2.5 %shard_map.108 = (f32[512,256]{1,0:T(8,128)}, f32[256,512]{1,0:T(8,128)S(1)}, f32[8,256]{1,0:T(8,128)S(1)}, f32[2,64,1024]{2,1,0:T(8,128)S(1)}, f32[2,64,1024]{2,1,0:T(8,128)S(1)}) custom-call(s32[3]{0:T(128)S(1)} %pad_add_fusion.place.where, f32[512,256]{1,0:T(8,128)S(1)} %get-tuple-element.71.kept_in, f32[512,256]{1,0:T(8,128)S(1)} %collective-permute-done.in_chip, ...), custom_call_target="tpu_custom_call" | custom-call | flops 3221225472 | bytes 4194304 | tf_op jit(solution)/shard_map/pallas_call | solution.py:178
  53.7 2.5 %collective-permute-start.6 = (f32[64,1024]{1,0:T(8,128)S(1)}, f32[64,1024]{1,0:T(8,128)S(1)}, u32[]{:S(2)}, u32[]{:S(2)}) collective-permute-start(f32[64,1024]{1,0:T(8,128)S(1)} %get-tuple-element.91), channel_id=1, source_target_pairs={{0,2},{1,3},{2,0},{3,1},{4,6},{5,7},{6,4},{7,5},{8,10},{9,11},{10,... | collective-permute-start | bytes 786440 | tf_op jit(solution)/shard_map/ppermute | solution.py:606
  56.2 2.9 %shard_map.112 = (f32[2,136,1024]{2,1,0:T(8,128)S(1)}, f32[2,136,1024]{2,1,0:T(8,128)S(1)}) custom-call(s32[3]{0:T(128)S(1)} %pad_add_fusion.place.where, f32[8,256]{1,0:T(8,128)S(1)} %get-tuple-element.93.squares, f32[256,512]{1,0:T(8,128)S(1)} %get-tuple-element.94.turned, f32[4,512]{1,0:T(4,128)S(1)} %bitcast.29, f32[4,1024,512]{2,1,0:T(8,128)S(1)} %get-tuple-element.80.panels), custom_call_target="tpu_custom_call" | custom-call | flops 24 | bytes 4194304 | tf_op jit(solution)/shard_map/pallas_call | solution.py:232
  59.6 3.2 %collective-permute-done.6 = f32[64,1024]{1,0:T(8,128)S(1)} collective-permute-done((f32[64,1024]{1,0:T(8,128)S(1)}, f32[64,1024]{1,0:T(8,128)S(1)}, u32[]{:S(2)}, u32[]{:S(2)}) %collective-permute-start.6) | collective-permute-done | bytes 262176 | tf_op jit(solution)/shard_map/ppermute | solution.py:606
  66.9 2.3 %shard_map.114.refs_0_ = f32[1024,1024]{1,0:T(8,128)S(1)} custom-call(f32[1,3,1024,1024]{3,2,1,0:T(8,128)} %panels.5), custom_call_target="tpu_custom_call" | custom-call | flops 24 | bytes 4194304 | tf_op jit(solution)/shard_map/pallas_call | solution.py:370
  69.1 4.4 %collective-permute-done.9.refs_1_ = f32[64,1024]{1,0:T(8,128)S(1)} collective-permute-done((f32[64,1024]{1,0:T(8,128)S(1)}, f32[64,1024]{1,0:T(8,128)S(1)}, u32[]{:S(2)}, u32[]{:S(2)}) %collective-permute-start.9) | collective-permute-done | bytes 262176 | tf_op jit(solution)/shard_map/ppermute | solution.py:617
  80.6 3.6 %shard_map.116 = (f32[64,1024]{1,0:T(8,128)S(1)}, f32[8,128]{1,0:T(8,128)S(1)}, f32[1024,128]{1,0:T(8,128)S(1)}, f32[64,1024]{1,0:T(8,128)S(1)}) custom-call(s32[3]{0:T(128)S(1)} %pad_add_fusion.place.where, f32[64,1024]{1,0:T(8,128)S(1)} %get-tuple-element.105.left, bf16[4,1024,1024]{2,1,0:T(8,128)(2,1)S(1)} %get-tuple-element.82.halves, ...), custom_call_target="tpu_custom_call" | custom-call | flops 24 | bytes 4194304 | tf_op jit(solution)/shard_map/pallas_call | solution.py:471
  87.3 4.4 %collective-permute-start.16 = (f32[64,1024]{1,0:T(8,128)S(1)}, f32[64,1024]{1,0:T(8,128)S(1)}, u32[]{:S(2)}, u32[]{:S(2)}) collective-permute-start(f32[64,1024]{1,0:T(8,128)S(1)} %fusion.3), channel_id=1, source_target_pairs={{0,4},{8,12},{16,20},{24,28},{1,5},{9,13},{17,21},{25,29},{2,6},{1... | collective-permute-start | bytes 786440 | tf_op jit(solution)/shard_map/ppermute | solution.py:665
  91.7 3.2 %shard_map.117 = f32[72,1024]{1,0:T(8,128)S(1)} custom-call(f32[1024,128]{1,0:T(8,128)S(1)} %get-tuple-element.109.value, f32[8,128]{1,0:T(8,128)S(1)} %get-tuple-element.110.squares, f32[1,3,1024,1024]{3,2,1,0:T(8,128)} %panels.5), custom_call_target="tpu_custom_call" | custom-call | flops 24 | bytes 4194304 | tf_op jit(solution)/shard_map/pallas_call | solution.py:499
  96.7 3.9 %collective-permute-start.21 = (f32[72,1024]{1,0:T(8,128)S(1)}, f32[72,1024]{1,0:T(8,128)S(1)}, u32[]{:S(2)}, u32[]{:S(2)}) collective-permute-start(f32[72,1024]{1,0:T(8,128)S(1)} %fusion.1), channel_id=1, source_target_pairs={{0,4},{8,12},{16,20},{24,28},{1,5},{9,13},{17,21},{25,29},{2,6},{1... | collective-permute-start | bytes 884744 | tf_op jit(solution)/shard_map/ppermute | solution.py:650
  102.7 4.1 %shard_map.120 = (f32[64,1024]{1,0:T(8,128)S(1)}, f32[8,128]{1,0:T(8,128)}, f32[1024,128]{1,0:T(8,128)}, f32[72,1024]{1,0:T(8,128)S(1)}) custom-call(s32[3]{0:T(128)S(1)} %pad_add_fusion.place.where, f32[64,1024]{1,0:T(8,128)S(1)} %get-tuple-element.112.left, bf16[4,1024,1024]{2,1,0:T(8,128)(2,1)S(1)} %get-tuple-element.82.halves, ...), custom_call_target="tpu_custom_call" | custom-call | flops 24 | bytes 4194304 | tf_op jit(solution)/shard_map/pallas_call | solution.py:471
  110.3 3.0 %shard_map.121 = (f32[64,1024]{1,0:T(8,128)S(1)}, f32[8,128]{1,0:T(8,128)S(1)}, f32[1024,128]{1,0:T(8,128)}) custom-call(s32[3]{0:T(128)S(1)} %pad_add_fusion.place.where, f32[64,1024]{1,0:T(8,128)S(1)} %get-tuple-element.119.left, bf16[4,1024,1024]{2,1,0:T(8,128)(2,1)S(1)} %get-tuple-element.82.halves, f32[64,1024]{1,0:T(8,128)S(1)} %get-tuple-element.121.solved), custom_call_target="tpu_custom_call" | custom-call | flops 24 | bytes 4194304 | tf_op jit(solution)/shard_map/pallas_call | solution.py:471
  113.9 2.0 %shard_map.122 = (f32[1024,128]{1,0:T(8,128)S(1)}, f32[8,128]{1,0:T(8,128)S(1)}) custom-call(s32[3]{0:T(128)S(1)} %pad_add_fusion.place.where, f32[64,1024]{1,0:T(8,128)S(1)} %bitcast.26, bf16[4,1024,1024]{2,1,0:T(8,128)(2,1)S(1)} %get-tuple-element.82.halves, f32[8,128]{1,0:T(8,128)S(1)} %get-tuple-element.134.squares, ...), custom_call_target="tpu_custom_call" | custom-call | flops 24 | bytes 4194304 | tf_op jit(solution)/shard_map/pallas_call | solution.py:524
  119.9 22.3 %collective-permute-done.27 = f32[8,128]{1,0:T(8,128)S(1)} collective-permute-done((f32[8,128]{1,0:T(8,128)S(1)}, f32[8,128]{1,0:T(8,128)S(1)}, u32[]{:S(2)}, u32[]{:S(2)}) %collective-permute-start.27) | collective-permute-done | bytes 4128 | tf_op jit(solution)/shard_map/ppermute | solution.py:693
  (86 shorter events, 35.1 us)
Async XLA Ops:
  3.3 22.9 %all-to-all-start = ((f32[32,16,256]{2,1,0:T(8,128)}), f32[32,16,256]{2,1,0:T(8,128)S(1)}, u32[]{:S(2)}, u32[]{:S(2)}) async-start(f32[32,16,256]{2,1,0:T(8,128)} %bitcast.4), calls=%async_computation | async-start | bytes 1048576 | tf_op jit(solution)/shard_map/all_to_all | solution.py:575
  29.8 3.8 %collective-permute-start = (f32[512,256]{1,0:T(8,128)S(1)}, f32[512,256]{1,0:T(8,128)S(1)}, u32[]{:S(2)}, u32[]{:S(2)}) collective-permute-start(f32[512,256]{1,0:T(8,128)S(1)} %get-tuple-element.72), channel_id=1, source_target_pairs={{0,1},{1,0},{2,3},{4,5},{5,4},{6,7},{8,9},{9,8},{10,11},{12,13},{1... | collective-permute-start | bytes 1572872 | tf_op jit(solution)/shard_map/ppermute | solution.py:589
  33.7 14.6 %collective-permute-start.1 = (f32[512,256]{1,0:T(8,128)S(1)}, f32[512,256]{1,0:T(8,128)S(1)}, u32[]{:S(2)}, u32[]{:S(2)}) collective-permute-start(f32[512,256]{1,0:T(8,128)S(1)} %add.72), channel_id=1, source_target_pairs={{0,2},{1,3},{4,6},{5,7},{8,10},{9,11},{12,14},{13,15},{16,18},{17,... | collective-permute-start | bytes 1572872 | tf_op jit(solution)/shard_map/ppermute | solution.py:592
  38.2 9.3 %collective-permute-start.2 = (f32[256,256]{1,0:T(8,128)S(1)}, f32[256,256]{1,0:T(8,128)S(1)}, u32[]{:S(2)}, u32[]{:S(2)}) collective-permute-start(f32[256,256]{1,0:T(8,128)S(1)} %get-tuple-element.77.top), channel_id=1, source_target_pairs={{0,1},{4,5},{8,9},{12,13},{16,17},{20,21},{24,25},{28,29}} | collective-permute-start | bytes 786440 | tf_op jit(solution)/shard_map/ppermute | solution.py:594
  40.2 7.4 %collective-permute-start.3 = (f32[256,256]{1,0:T(8,128)S(1)}, f32[256,256]{1,0:T(8,128)S(1)}, u32[]{:S(2)}, u32[]{:S(2)}) collective-permute-start(f32[256,256]{1,0:T(8,128)S(1)} %get-tuple-element.78.bottom), channel_id=1, source_target_pairs={{0,1},{4,5},{8,9},{12,13},{16,17},{20,21},{24,25},{28,29}} | collective-permute-start | bytes 786440 | tf_op jit(solution)/shard_map/ppermute | solution.py:594
  53.3 5.7 %collective-permute-start.5 = (f32[2,64,1024]{2,1,0:T(8,128)S(1)}, f32[2,64,1024]{2,1,0:T(8,128)S(1)}, u32[]{:S(2)}, u32[]{:S(2)}) collective-permute-start(f32[2,64,1024]{2,1,0:T(8,128)S(1)} %get-tuple-element.89), channel_id=1, source_target_pairs={{0,1},{1,0},{2,3},{3,2},{4,5},{5,4},{6,7},{7,6},{8,9},{9,8},{10,11... | collective-permute-start | bytes 1572872 | tf_op jit(solution)/shard_map/ppermute | solution.py:607
  53.7 9.2 %collective-permute-start.6 = (f32[64,1024]{1,0:T(8,128)S(1)}, f32[64,1024]{1,0:T(8,128)S(1)}, u32[]{:S(2)}, u32[]{:S(2)}) collective-permute-start(f32[64,1024]{1,0:T(8,128)S(1)} %get-tuple-element.91), channel_id=1, source_target_pairs={{0,2},{1,3},{2,0},{3,1},{4,6},{5,7},{6,4},{7,5},{8,10},{9,11},{10,... | collective-permute-start | bytes 786440 | tf_op jit(solution)/shard_map/ppermute | solution.py:606
  62.9 3.3 %collective-permute-start.10 = (f32[2,136,1024]{2,1,0:T(8,128)S(1)}, f32[2,136,1024]{2,1,0:T(8,128)S(1)}, u32[]{:S(2)}, u32[]{:S(2)}) collective-permute-start(f32[2,136,1024]{2,1,0:T(8,128)S(1)} %get-tuple-element.100), channel_id=1, source_target_pairs={{0,1},{1,0},{2,3},{3,2},{4,5},{5,4},{6,7},{7,6},{8,9},{9,8},{10,11... | collective-permute-start | bytes 3342344 | tf_op jit(solution)/shard_map/ppermute | solution.py:612
  62.9 10.6 %collective-permute-start.9 = (f32[64,1024]{1,0:T(8,128)S(1)}, f32[64,1024]{1,0:T(8,128)S(1)}, u32[]{:S(2)}, u32[]{:S(2)}) collective-permute-start(f32[64,1024]{1,0:T(8,128)S(1)} %add.74.refs_0_), channel_id=1, source_target_pairs={{4,0},{12,8},{20,16},{28,24},{5,1},{13,9},{21,17},{29,25},{6,2},{1... | collective-permute-start | bytes 786440 | tf_op jit(solution)/shard_map/ppermute | solution.py:617
  64.4 12.6 %collective-permute-start.7 = (f32[64,1024]{1,0:T(8,128)S(1)}, f32[64,1024]{1,0:T(8,128)S(1)}, u32[]{:S(2)}, u32[]{:S(2)}) collective-permute-start(f32[64,1024]{1,0:T(8,128)S(1)} %get-tuple-element.96), channel_id=1, source_target_pairs={{0,2},{1,3},{2,0},{3,1},{4,6},{5,7},{6,4},{7,5},{8,10},{9,11},{10,... | collective-permute-start | bytes 786440 | tf_op jit(solution)/shard_map/ppermute | solution.py:611
  73.5 11.6 %collective-permute-start.15 = (f32[64,1024]{1,0:T(8,128)S(1)}, f32[64,1024]{1,0:T(8,128)S(1)}, u32[]{:S(2)}, u32[]{:S(2)}) collective-permute-start(f32[64,1024]{1,0:T(8,128)S(1)} %slice.30), channel_id=1, source_target_pairs={{0,2},{1,3},{2,0},{3,1},{4,6},{5,7},{6,4},{7,5},{8,10},{9,11},{10,... | collective-permute-start | bytes 786440 | tf_op jit(solution)/shard_map/ppermute | solution.py:623
  77.1 7.2 %collective-permute-start.13 = (f32[32,1024]{1,0:T(8,128)S(1)}, f32[32,1024]{1,0:T(8,128)S(1)}, u32[]{:S(2)}, u32[]{:S(2)}) collective-permute-start(f32[32,1024]{1,0:T(8,128)S(1)} %get-tuple-element.135), channel_id=1, source_target_pairs={{8,12},{24,28},{9,13},{25,29},{10,14},{26,30},{11,15},{27,31}} | collective-permute-start | bytes 393224 | tf_op jit(solution)/shard_map/ppermute | solution.py:660
  77.8 9.5 %collective-permute-start.11 = (f32[64,1024]{1,0:T(8,128)S(1)}, f32[64,1024]{1,0:T(8,128)S(1)}, u32[]{:S(2)}, u32[]{:S(2)}) collective-permute-start(f32[64,1024]{1,0:T(8,128)S(1)} %get-tuple-element.129), channel_id=1, source_target_pairs={{0,4},{16,20},{1,5},{17,21},{2,6},{18,22},{3,7},{19,23}} | collective-permute-start | bytes 786440 | tf_op jit(solution)/shard_map/ppermute | solution.py:657
  79.2 15.7 %collective-permute-start.8 = (f32[64,1024]{1,0:T(8,128)S(1)}, f32[64,1024]{1,0:T(8,128)S(1)}, u32[]{:S(2)}, u32[]{:S(2)}) collective-permute-start(f32[64,1024]{1,0:T(8,128)S(1)} %get-tuple-element.130.refs_0_), channel_id=1, source_target_pairs={{12,4},{28,20},{13,5},{29,21},{14,6},{30,22},{15,7},{31,23}} | collective-permute-start | bytes 786440 | tf_op jit(solution)/shard_map/ppermute | solution.py:655
  79.9 15.0 %collective-permute-start.12 = (f32[32,1024]{1,0:T(8,128)S(1)}, f32[32,1024]{1,0:T(8,128)S(1)}, u32[]{:S(2)}, u32[]{:S(2)}) collective-permute-start(f32[32,1024]{1,0:T(8,128)S(1)} %get-tuple-element.136), channel_id=1, source_target_pairs={{8,4},{24,20},{9,5},{25,21},{10,6},{26,22},{11,7},{27,23}} | collective-permute-start | bytes 393224 | tf_op jit(solution)/shard_map/ppermute | solution.py:661
  84.3 12.3 %collective-permute-start.20 = (f32[72,1024]{1,0:T(8,128)S(1)}, f32[72,1024]{1,0:T(8,128)S(1)}, u32[]{:S(2)}, u32[]{:S(2)}) collective-permute-start(f32[72,1024]{1,0:T(8,128)S(1)} %slice.32), channel_id=1, source_target_pairs={{0,2},{1,3},{2,0},{3,1},{4,6},{5,7},{6,4},{7,5},{8,10},{9,11},{10,... | collective-permute-start | bytes 884744 | tf_op jit(solution)/shard_map/ppermute | solution.py:623
  85.1 9.8 %collective-permute-start.14 = (f32[32,1024]{1,0:T(8,128)S(1)}, f32[32,1024]{1,0:T(8,128)S(1)}, u32[]{:S(2)}, u32[]{:S(2)}) collective-permute-start(f32[32,1024]{1,0:T(8,128)S(1)} %collective-permute-done.13), channel_id=1, source_target_pairs={{12,4},{28,20},{13,5},{29,21},{14,6},{30,22},{15,7},{31,23}} | collective-permute-start | bytes 393224 | tf_op jit(solution)/shard_map/ppermute | solution.py:662
  87.3 9.3 %collective-permute-start.16 = (f32[64,1024]{1,0:T(8,128)S(1)}, f32[64,1024]{1,0:T(8,128)S(1)}, u32[]{:S(2)}, u32[]{:S(2)}) collective-permute-start(f32[64,1024]{1,0:T(8,128)S(1)} %fusion.3), channel_id=1, source_target_pairs={{0,4},{8,12},{16,20},{24,28},{1,5},{9,13},{17,21},{25,29},{2,6},{1... | collective-permute-start | bytes 786440 | tf_op jit(solution)/shard_map/ppermute | solution.py:665
  96.7 10.1 %collective-permute-start.21 = (f32[72,1024]{1,0:T(8,128)S(1)}, f32[72,1024]{1,0:T(8,128)S(1)}, u32[]{:S(2)}, u32[]{:S(2)}) collective-permute-start(f32[72,1024]{1,0:T(8,128)S(1)} %fusion.1), channel_id=1, source_target_pairs={{0,4},{8,12},{16,20},{24,28},{1,5},{9,13},{17,21},{25,29},{2,6},{1... | collective-permute-start | bytes 884744 | tf_op jit(solution)/shard_map/ppermute | solution.py:650
  100.6 7.2 %collective-permute-start.18 = (f32[64,1024]{1,0:T(8,128)S(1)}, f32[64,1024]{1,0:T(8,128)S(1)}, u32[]{:S(2)}, u32[]{:S(2)}) collective-permute-start(f32[64,1024]{1,0:T(8,128)S(1)} %add.79), channel_id=1, source_target_pairs={{4,12},{5,13},{6,14},{7,15}} | collective-permute-start | bytes 786440 | tf_op jit(solution)/shard_map/ppermute | solution.py:657
  101.3 6.5 %collective-permute-start.19 = (f32[64,1024]{1,0:T(8,128)S(1)}, f32[64,1024]{1,0:T(8,128)S(1)}, u32[]{:S(2)}, u32[]{:S(2)}) collective-permute-start(f32[64,1024]{1,0:T(8,128)S(1)} %add.79), channel_id=1, source_target_pairs={{20,12},{21,13},{22,14},{23,15}} | collective-permute-start | bytes 786440 | tf_op jit(solution)/shard_map/ppermute | solution.py:664
  102.0 5.8 %collective-permute-start.17 = (f32[64,1024]{1,0:T(8,128)S(1)}, f32[64,1024]{1,0:T(8,128)S(1)}, u32[]{:S(2)}, u32[]{:S(2)}) collective-permute-start(f32[64,1024]{1,0:T(8,128)S(1)} %fusion.2.refs_0_), channel_id=1, source_target_pairs={{28,12},{29,13},{30,14},{31,15}} | collective-permute-start | bytes 786440 | tf_op jit(solution)/shard_map/ppermute | solution.py:655
  109.6 4.3 %collective-permute-start.24 = (f32[64,1024]{1,0:T(8,128)S(1)}, f32[64,1024]{1,0:T(8,128)S(1)}, u32[]{:S(2)}, u32[]{:S(2)}) collective-permute-start(f32[64,1024]{1,0:T(8,128)S(1)} %get-tuple-element.131), channel_id=1, source_target_pairs={{12,28},{13,29},{14,30},{15,31}} | collective-permute-start | bytes 786440 | tf_op jit(solution)/shard_map/ppermute | solution.py:676
  117.3 24.8 %collective-permute-start.27 = (f32[8,128]{1,0:T(8,128)S(1)}, f32[8,128]{1,0:T(8,128)S(1)}, u32[]{:S(2)}, u32[]{:S(2)}) collective-permute-start(f32[8,128]{1,0:T(8,128)S(1)} %add.88), channel_id=1, source_target_pairs={{4,0},{12,8},{20,16},{28,24},{5,1},{13,9},{21,17},{29,25},{6,2},{1... | collective-permute-start | bytes 12296 | tf_op jit(solution)/shard_map/ppermute | solution.py:693
  (9 other events, 33.3 us)
where the time goes:
time: 143 us
  Pallas kernels  53.2 us (37%)
  starting transfers between devices  43.5 us (30%)
  waiting for transfers between devices  41.3 us (29%)
  local copies, waits for them, and re-layouts  2.87 us (2%)
    ppermute x3, waiting for transfers between devices, local(): widths = widths + lax.ppermute(widths, 'leaf', steps)  22.3 us
    pallas_call x3, Pallas kernels, solve(): pl.pallas_call(functools.partial(solve_kernel, tier, last, with_tail), ou...  10.8 us
    pallas_call x1, Pallas kernels, prepared(): pl.pallas_call(prepare_kernel, out_shape=pltpu.HBM((4, rows, rows), jnp.b...  8.43 us
    all_to_all x1, starting transfers between devices, local(): lax.all_to_all(picked.reshape(block_count, block_rows // block_count, col...  7.3 us
    all_to_all x1, waiting for transfers between devices, local(): lax.all_to_all(picked.reshape(block_count, block_rows // block_count, col...  7.11 us
    pallas_call x1, Pallas kernels, loaded(): pl.pallas_call(load_kernel, out_shape=(pltpu.VMEM(halves.shape, jnp.bfloa...  5.92 us
    ppermute x2, starting transfers between devices, local(): following = rest[0] + lax.ppermute(rest[0] + tail, 'leaf', onward)  5.29 us
    pallas_call x3, Pallas kernels, direct(): pl.pallas_call(functools.partial(direct_kernel, len(parts)), out_shape=(s...  4.9 us
  transfers between devices with their start and end apart: 29, of which 8 were waited for; matrix products, arithmetic and copies ran while one was open for 0% of the time, Pallas kernels for 31%

commit v1 on v0

--- a/solution.py
+++ b/solution.py
@@ -397,13 +397,9 @@
 
 
 def left_of(own_rhs, parts):
-    whole_parts = [part[...] for part in parts if part.shape == own_rhs.shape]
-    halves = [part[...] for part in parts if part.shape != own_rhs.shape]
-    total = whole_parts[0]
-    for part in whole_parts[1:]:
-        total = total + part
-    if halves:
-        total = total + jnp.concatenate(halves, axis=0)
+    total = parts[0][...]
+    for part in parts[1:]:
+        total = total + part[...]
     return own_rhs[...] - total
 
 
@@ -652,16 +648,15 @@
             ]
         if count:
             value, tail = more
-            next_early = lax.ppermute(following, "leaf", early)
             term = following + term
             from_left = lax.ppermute(term, "leaf", direct_left)
-            parts = [following, next_early, from_left]
             if tier == 1:
-                turn = lax.ppermute(term[width // 2 :], "leaf", aside)
-                parts.append(lax.ppermute(term[: width // 2], "leaf", direct_right))
-                parts.append(lax.ppermute(turn, "leaf", early))
+                turn, tail = lax.optimization_barrier((lax.ppermute(term, "leaf", aside), tail))
+                parts = [following, lax.ppermute(following + turn, "leaf", early), from_left]
             else:
-                parts.append(lax.ppermute(term, "leaf", direct_right))
+                next_early = lax.ppermute(following, "leaf", early)
+                from_right = lax.ppermute(term, "leaf", direct_right)
+                parts = [following, next_early, from_left, from_right]
             following = rest[0] + lax.ppermute(rest[0] + tail, "leaf", onward)
             rest = rest[1:]
             waiting = []

time: 143 us -> 142 us (level)
  starting transfers between devices: 43.5 us -> 39.7 us
  waiting for transfers between devices: 41.3 us -> 43.9 us
    ppermute x3, waiting for transfers between devices: 22.3 us -> 25.5 us  [local(): widths = widths + lax.ppermute(widths, 'leaf', steps)]
    ppermute x2, starting transfers between devices: 5.29 us -> 2.61 us  [local(): following = rest[0] + lax.ppermute(rest[0] + tail, 'leaf', onward)]
    ppermute x2, waiting for transfers between devices: 1.45 us -> 0.01 us  [local(): from_left = lax.ppermute(term, 'leaf', direct_left)]
  transfers between devices with their start and end apart: 29 -> 27, of which waited for: 8 -> 8; matrix products, arithmetic and copies ran while one was open for 0% -> 0% of each run, Pallas kernels for 31% -> 31%
where the time goes in v1:
time: 142 us; the launch traced here: 141 us
  Pallas kernels  53.2 us (37%)
  waiting for transfers between devices  43.9 us (31%)
  starting transfers between devices  39.7 us (28%)
  local copies, waits for them, and re-layouts  2.85 us (2%)
    ppermute x3, waiting for transfers between devices, local(): widths = widths + lax.ppermute(widths, 'leaf', steps)  25.5 us
    pallas_call x3, Pallas kernels, solve(): pl.pallas_call(functools.partial(solve_kernel, tier, last, with_tail), ou...  10.8 us
    pallas_call x1, Pallas kernels, prepared(): pl.pallas_call(prepare_kernel, out_shape=pltpu.HBM((4, rows, rows), jnp.b...  8.44 us
    all_to_all x1, starting transfers between devices, local(): lax.all_to_all(picked.reshape(block_count, block_rows // block_count, col...  7.3 us
    all_to_all x1, waiting for transfers between devices, local(): lax.all_to_all(picked.reshape(block_count, block_rows // block_count, col...  7.1 us
    pallas_call x1, Pallas kernels, loaded(): pl.pallas_call(load_kernel, out_shape=(pltpu.VMEM(halves.shape, jnp.bfloa...  5.92 us
    pallas_call x3, Pallas kernels, direct(): pl.pallas_call(functools.partial(direct_kernel, len(parts)), out_shape=(s...  4.89 us
    ppermute x1, waiting for transfers between devices, local(): lax.ppermute(mine, 'leaf', pairs)  4.55 us
  transfers between devices with their start and end apart: 27, of which 8 were waited for; matrix products, arithmetic and copies ran while one was open for 0% of the time, Pallas kernels for 31%

profile of v1, /device:TPU:0, one launch (start us, length us, event | category | flops | bytes accessed | tf_op | source)
XLA Modules:
  0.0 141.4 jit_solution(7152009706481583197)
XLA Ops:
  0.6 2.5 %shard_map.103 = f32[512,256]{1,0:T(8,128)} custom-call(s32[1,512]{1,0:T(1,128)} %bitcast.31, f32[512,256]{1,0:T(8,128)} %rows.1), custom_call_target="tpu_custom_call" | custom-call | flops 1610612736 | bytes 4194304 | tf_op jit(solution)/shard_map/pallas_call | solution.py:79
  3.3 7.3 %all-to-all-start = ((f32[32,16,256]{2,1,0:T(8,128)}), f32[32,16,256]{2,1,0:T(8,128)S(1)}, u32[]{:S(2)}, u32[]{:S(2)}) async-start(f32[32,16,256]{2,1,0:T(8,128)} %bitcast.4), calls=%async_computation | async-start | bytes 1048576 | tf_op jit(solution)/shard_map/all_to_all | solution.py:571
  10.6 8.4 %shard_map.104.halves = bf16[4,1024,1024]{2,1,0:T(8,128)(2,1)} custom-call(f32[1,1024,1024]{2,1,0:T(8,128)} %inverse, f32[1,3,1024,1024]{3,2,1,0:T(8,128)} %panels.5), custom_call_target="tpu_custom_call" | custom-call | flops 25769803776 | bytes 4194304 | tf_op jit(solution)/shard_map/pallas_call | solution.py:318
  19.0 7.1 %all-to-all-done = f32[32,16,256]{2,1,0:T(8,128)S(1)} async-done(((f32[32,16,256]{2,1,0:T(8,128)}), f32[32,16,256]{2,1,0:T(8,128)S(1)}, u32[]{:S(2)}, u32[]{:S(2)}) %all-to-all-start) | async-done | bytes 524320 | tf_op jit(solution)/shard_map/all_to_all | solution.py:571
  26.1 2.2 %copy-done.1 = f32[2048,512]{1,0:T(8,128)S(1)} copy-done((f32[2048,512]{1,0:T(8,128)S(1)}, f32[2048,512]{1,0:T(8,128)}, u32[]{:S(2)}) %copy-start.1) | copy-done | bytes 4194328
  29.8 1.9 %collective-permute-start = (f32[512,256]{1,0:T(8,128)S(1)}, f32[512,256]{1,0:T(8,128)S(1)}, u32[]{:S(2)}, u32[]{:S(2)}) collective-permute-start(f32[512,256]{1,0:T(8,128)S(1)} %get-tuple-element.74), channel_id=1, source_target_pairs={{0,1},{1,0},{2,3},{4,5},{5,4},{6,7},{8,9},{9,8},{10,11},{12,13},{1... | collective-permute-start | bytes 1572872 | tf_op jit(solution)/shard_map/ppermute | solution.py:585
  33.7 2.9 %collective-permute-start.1 = (f32[512,256]{1,0:T(8,128)S(1)}, f32[512,256]{1,0:T(8,128)S(1)}, u32[]{:S(2)}, u32[]{:S(2)}) collective-permute-start(f32[512,256]{1,0:T(8,128)S(1)} %add.75), channel_id=1, source_target_pairs={{0,2},{1,3},{4,6},{5,7},{8,10},{9,11},{12,14},{13,15},{16,18},{17,... | collective-permute-start | bytes 1572872 | tf_op jit(solution)/shard_map/ppermute | solution.py:588
  38.2 2.0 %collective-permute-start.2 = (f32[256,256]{1,0:T(8,128)S(1)}, f32[256,256]{1,0:T(8,128)S(1)}, u32[]{:S(2)}, u32[]{:S(2)}) collective-permute-start(f32[256,256]{1,0:T(8,128)S(1)} %get-tuple-element.79.top), channel_id=1, source_target_pairs={{0,1},{4,5},{8,9},{12,13},{16,17},{20,21},{24,25},{28,29}} | collective-permute-start | bytes 786440 | tf_op jit(solution)/shard_map/ppermute | solution.py:590
  41.6 5.9 %shard_map.107 = (bf16[4,1024,1024]{2,1,0:T(8,128)(2,1)S(1)}, f32[4,1024,512]{2,1,0:T(8,128)S(1)}) custom-call(bf16[4,1024,1024]{2,1,0:T(8,128)(2,1)} %shard_map.104.halves, f32[1,4,1024,512]{3,2,1,0:T(8,128)} %panels.3), custom_call_target="tpu_custom_call" | custom-call | flops 24 | bytes 4194304 | tf_op jit(solution)/shard_map/pallas_call | solution.py:349
  48.3 2.5 %shard_map.108 = (f32[512,256]{1,0:T(8,128)}, f32[256,512]{1,0:T(8,128)S(1)}, f32[8,256]{1,0:T(8,128)S(1)}, f32[2,64,1024]{2,1,0:T(8,128)S(1)}, f32[2,64,1024]{2,1,0:T(8,128)S(1)}) custom-call(s32[3]{0:T(128)S(1)} %pad_add_fusion.place.where, f32[512,256]{1,0:T(8,128)S(1)} %get-tuple-element.73.kept_in, f32[512,256]{1,0:T(8,128)S(1)} %collective-permute-done.in_chip, ...), custom_call_target="tpu_custom_call" | custom-call | flops 3221225472 | bytes 4194304 | tf_op jit(solution)/shard_map/pallas_call | solution.py:178
  53.7 2.5 %collective-permute-start.6 = (f32[64,1024]{1,0:T(8,128)S(1)}, f32[64,1024]{1,0:T(8,128)S(1)}, u32[]{:S(2)}, u32[]{:S(2)}) collective-permute-start(f32[64,1024]{1,0:T(8,128)S(1)} %get-tuple-element.93), channel_id=1, source_target_pairs={{0,2},{1,3},{2,0},{3,1},{4,6},{5,7},{6,4},{7,5},{8,10},{9,11},{10,... | collective-permute-start | bytes 786440 | tf_op jit(solution)/shard_map/ppermute | solution.py:602
  56.2 2.9 %shard_map.112 = (f32[2,136,1024]{2,1,0:T(8,128)S(1)}, f32[2,136,1024]{2,1,0:T(8,128)S(1)}) custom-call(s32[3]{0:T(128)S(1)} %pad_add_fusion.place.where, f32[8,256]{1,0:T(8,128)S(1)} %get-tuple-element.95.squares, f32[256,512]{1,0:T(8,128)S(1)} %get-tuple-element.96.turned, f32[4,512]{1,0:T(4,128)S(1)} %bitcast.29, f32[4,1024,512]{2,1,0:T(8,128)S(1)} %get-tuple-element.82.panels), custom_call_target="tpu_custom_call" | custom-call | flops 24 | bytes 4194304 | tf_op jit(solution)/shard_map/pallas_call | solution.py:232
  59.6 3.2 %collective-permute-done.6 = f32[64,1024]{1,0:T(8,128)S(1)} collective-permute-done((f32[64,1024]{1,0:T(8,128)S(1)}, f32[64,1024]{1,0:T(8,128)S(1)}, u32[]{:S(2)}, u32[]{:S(2)}) %collective-permute-start.6) | collective-permute-done | bytes 262176 | tf_op jit(solution)/shard_map/ppermute | solution.py:602
  66.7 2.3 %shard_map.114.refs_0_ = f32[1024,1024]{1,0:T(8,128)S(1)} custom-call(f32[1,3,1024,1024]{3,2,1,0:T(8,128)} %panels.5), custom_call_target="tpu_custom_call" | custom-call | flops 24 | bytes 4194304 | tf_op jit(solution)/shard_map/pallas_call | solution.py:370
  69.0 4.6 %collective-permute-done.8.refs_1_ = f32[64,1024]{1,0:T(8,128)S(1)} collective-permute-done((f32[64,1024]{1,0:T(8,128)S(1)}, f32[64,1024]{1,0:T(8,128)S(1)}, u32[]{:S(2)}, u32[]{:S(2)}) %collective-permute-start.8) | collective-permute-done | bytes 262176 | tf_op jit(solution)/shard_map/ppermute | solution.py:613
  77.9 2.1 %collective-permute-start.12 = (f32[64,1024]{1,0:T(8,128)S(1)}, f32[64,1024]{1,0:T(8,128)S(1)}, u32[]{:S(2)}, u32[]{:S(2)}) collective-permute-start(f32[64,1024]{1,0:T(8,128)S(1)} %get-tuple-element.133), channel_id=1, source_target_pairs={{0,4},{16,20},{1,5},{17,21},{2,6},{18,22},{3,7},{19,23}} | collective-permute-start | bytes 786440 | tf_op jit(solution)/shard_map/ppermute | solution.py:652
  80.1 3.6 %shard_map.116 = (f32[64,1024]{1,0:T(8,128)S(1)}, f32[8,128]{1,0:T(8,128)S(1)}, f32[1024,128]{1,0:T(8,128)S(1)}, f32[64,1024]{1,0:T(8,128)S(1)}) custom-call(s32[3]{0:T(128)S(1)} %pad_add_fusion.place.where, f32[64,1024]{1,0:T(8,128)S(1)} %get-tuple-element.108.left, bf16[4,1024,1024]{2,1,0:T(8,128)(2,1)S(1)} %get-tuple-element.84.halves, ...), custom_call_target="tpu_custom_call" | custom-call | flops 24 | bytes 4194304 | tf_op jit(solution)/shard_map/pallas_call | solution.py:467
  84.9 1.9 %collective-permute-start.14 = (f32[64,1024]{1,0:T(8,128)S(1)}, f32[64,1024]{1,0:T(8,128)S(1)}, u32[]{:S(2)}, u32[]{:S(2)}) collective-permute-start(f32[64,1024]{1,0:T(8,128)S(1)} %fusion.3), channel_id=1, source_target_pairs={{0,4},{8,12},{16,20},{24,28},{1,5},{9,13},{17,21},{25,29},{2,6},{1... | collective-permute-start | bytes 786440 | tf_op jit(solution)/shard_map/ppermute | solution.py:660
  86.8 3.2 %shard_map.117 = f32[72,1024]{1,0:T(8,128)S(1)} custom-call(f32[1024,128]{1,0:T(8,128)S(1)} %get-tuple-element.113.value, f32[8,128]{1,0:T(8,128)S(1)} %get-tuple-element.114.squares, f32[1,3,1024,1024]{3,2,1,0:T(8,128)} %panels.5), custom_call_target="tpu_custom_call" | custom-call | flops 24 | bytes 4194304 | tf_op jit(solution)/shard_map/pallas_call | solution.py:495
  92.4 3.7 %collective-permute-start.19 = (f32[72,1024]{1,0:T(8,128)S(1)}, f32[72,1024]{1,0:T(8,128)S(1)}, u32[]{:S(2)}, u32[]{:S(2)}) collective-permute-start(f32[72,1024]{1,0:T(8,128)S(1)} %fusion.1), channel_id=1, source_target_pairs={{0,4},{8,12},{16,20},{24,28},{1,5},{9,13},{17,21},{25,29},{2,6},{1... | collective-permute-start | bytes 884744 | tf_op jit(solution)/shard_map/ppermute | solution.py:646
  98.2 4.1 %shard_map.120 = (f32[64,1024]{1,0:T(8,128)S(1)}, f32[8,128]{1,0:T(8,128)}, f32[1024,128]{1,0:T(8,128)}, f32[72,1024]{1,0:T(8,128)S(1)}) custom-call(s32[3]{0:T(128)S(1)} %pad_add_fusion.place.where, f32[64,1024]{1,0:T(8,128)S(1)} %get-tuple-element.116.left, bf16[4,1024,1024]{2,1,0:T(8,128)(2,1)S(1)} %get-tuple-element.84.halves, ...), custom_call_target="tpu_custom_call" | custom-call | flops 24 | bytes 4194304 | tf_op jit(solution)/shard_map/pallas_call | solution.py:467
  105.8 3.0 %shard_map.121 = (f32[64,1024]{1,0:T(8,128)S(1)}, f32[8,128]{1,0:T(8,128)S(1)}, f32[1024,128]{1,0:T(8,128)}) custom-call(s32[3]{0:T(128)S(1)} %pad_add_fusion.place.where, f32[64,1024]{1,0:T(8,128)S(1)} %get-tuple-element.123.left, bf16[4,1024,1024]{2,1,0:T(8,128)(2,1)S(1)} %get-tuple-element.84.halves, f32[64,1024]{1,0:T(8,128)S(1)} %get-tuple-element.125.solved), custom_call_target="tpu_custom_call" | custom-call | flops 24 | bytes 4194304 | tf_op jit(solution)/shard_map/pallas_call | solution.py:467
  109.5 2.0 %shard_map.122 = (f32[1024,128]{1,0:T(8,128)S(1)}, f32[8,128]{1,0:T(8,128)S(1)}) custom-call(s32[3]{0:T(128)S(1)} %pad_add_fusion.place.where, f32[64,1024]{1,0:T(8,128)S(1)} %bitcast.26, bf16[4,1024,1024]{2,1,0:T(8,128)(2,1)S(1)} %get-tuple-element.84.halves, f32[8,128]{1,0:T(8,128)S(1)} %get-tuple-element.138.squares, ...), custom_call_target="tpu_custom_call" | custom-call | flops 24 | bytes 4194304 | tf_op jit(solution)/shard_map/pallas_call | solution.py:520
  115.4 25.5 %collective-permute-done.25 = f32[8,128]{1,0:T(8,128)S(1)} collective-permute-done((f32[8,128]{1,0:T(8,128)S(1)}, f32[8,128]{1,0:T(8,128)S(1)}, u32[]{:S(2)}, u32[]{:S(2)}) %collective-permute-start.25) | collective-permute-done | bytes 4128 | tf_op jit(solution)/shard_map/ppermute | solution.py:688
  (82 shorter events, 32.9 us)
Async XLA Ops:
  3.3 22.9 %all-to-all-start = ((f32[32,16,256]{2,1,0:T(8,128)}), f32[32,16,256]{2,1,0:T(8,128)S(1)}, u32[]{:S(2)}, u32[]{:S(2)}) async-start(f32[32,16,256]{2,1,0:T(8,128)} %bitcast.4), calls=%async_computation | async-start | bytes 1048576 | tf_op jit(solution)/shard_map/all_to_all | solution.py:571
  29.8 3.8 %collective-permute-start = (f32[512,256]{1,0:T(8,128)S(1)}, f32[512,256]{1,0:T(8,128)S(1)}, u32[]{:S(2)}, u32[]{:S(2)}) collective-permute-start(f32[512,256]{1,0:T(8,128)S(1)} %get-tuple-element.74), channel_id=1, source_target_pairs={{0,1},{1,0},{2,3},{4,5},{5,4},{6,7},{8,9},{9,8},{10,11},{12,13},{1... | collective-permute-start | bytes 1572872 | tf_op jit(solution)/shard_map/ppermute | solution.py:585
  33.7 14.6 %collective-permute-start.1 = (f32[512,256]{1,0:T(8,128)S(1)}, f32[512,256]{1,0:T(8,128)S(1)}, u32[]{:S(2)}, u32[]{:S(2)}) collective-permute-start(f32[512,256]{1,0:T(8,128)S(1)} %add.75), channel_id=1, source_target_pairs={{0,2},{1,3},{4,6},{5,7},{8,10},{9,11},{12,14},{13,15},{16,18},{17,... | collective-permute-start | bytes 1572872 | tf_op jit(solution)/shard_map/ppermute | solution.py:588
  38.2 9.3 %collective-permute-start.2 = (f32[256,256]{1,0:T(8,128)S(1)}, f32[256,256]{1,0:T(8,128)S(1)}, u32[]{:S(2)}, u32[]{:S(2)}) collective-permute-start(f32[256,256]{1,0:T(8,128)S(1)} %get-tuple-element.79.top), channel_id=1, source_target_pairs={{0,1},{4,5},{8,9},{12,13},{16,17},{20,21},{24,25},{28,29}} | collective-permute-start | bytes 786440 | tf_op jit(solution)/shard_map/ppermute | solution.py:590
  40.2 7.4 %collective-permute-start.3 = (f32[256,256]{1,0:T(8,128)S(1)}, f32[256,256]{1,0:T(8,128)S(1)}, u32[]{:S(2)}, u32[]{:S(2)}) collective-permute-start(f32[256,256]{1,0:T(8,128)S(1)} %get-tuple-element.80.bottom), channel_id=1, source_target_pairs={{0,1},{4,5},{8,9},{12,13},{16,17},{20,21},{24,25},{28,29}} | collective-permute-start | bytes 786440 | tf_op jit(solution)/shard_map/ppermute | solution.py:590
  50.8 1.9 %collective-permute-start.4 = (f32[2,64,1024]{2,1,0:T(8,128)S(1)}, f32[2,64,1024]{2,1,0:T(8,128)S(1)}, u32[]{:S(2)}, u32[]{:S(2)}) collective-permute-start(f32[2,64,1024]{2,1,0:T(8,128)S(1)} %get-tuple-element.88), channel_id=1, source_target_pairs={{0,1},{1,0},{2,3},{3,2},{4,5},{5,4},{6,7},{7,6},{8,9},{9,8},{10,11... | collective-permute-start | bytes 1572872 | tf_op jit(solution)/shard_map/ppermute | solution.py:598
  53.3 5.7 %collective-permute-start.5 = (f32[2,64,1024]{2,1,0:T(8,128)S(1)}, f32[2,64,1024]{2,1,0:T(8,128)S(1)}, u32[]{:S(2)}, u32[]{:S(2)}) collective-permute-start(f32[2,64,1024]{2,1,0:T(8,128)S(1)} %get-tuple-element.91), channel_id=1, source_target_pairs={{0,1},{1,0},{2,3},{3,2},{4,5},{5,4},{6,7},{7,6},{8,9},{9,8},{10,11... | collective-permute-start | bytes 1572872 | tf_op jit(solution)/shard_map/ppermute | solution.py:603
  53.7 9.2 %collective-permute-start.6 = (f32[64,1024]{1,0:T(8,128)S(1)}, f32[64,1024]{1,0:T(8,128)S(1)}, u32[]{:S(2)}, u32[]{:S(2)}) collective-permute-start(f32[64,1024]{1,0:T(8,128)S(1)} %get-tuple-element.93), channel_id=1, source_target_pairs={{0,2},{1,3},{2,0},{3,1},{4,6},{5,7},{6,4},{7,5},{8,10},{9,11},{10,... | collective-permute-start | bytes 786440 | tf_op jit(solution)/shard_map/ppermute | solution.py:602
  62.9 3.1 %collective-permute-start.9 = (f32[2,136,1024]{2,1,0:T(8,128)S(1)}, f32[2,136,1024]{2,1,0:T(8,128)S(1)}, u32[]{:S(2)}, u32[]{:S(2)}) collective-permute-start(f32[2,136,1024]{2,1,0:T(8,128)S(1)} %get-tuple-element.102), channel_id=1, source_target_pairs={{0,1},{1,0},{2,3},{3,2},{4,5},{5,4},{6,7},{7,6},{8,9},{9,8},{10,11... | collective-permute-start | bytes 3342344 | tf_op jit(solution)/shard_map/ppermute | solution.py:608
  62.9 10.6 %collective-permute-start.8 = (f32[64,1024]{1,0:T(8,128)S(1)}, f32[64,1024]{1,0:T(8,128)S(1)}, u32[]{:S(2)}, u32[]{:S(2)}) collective-permute-start(f32[64,1024]{1,0:T(8,128)S(1)} %add.77.refs_0_), channel_id=1, source_target_pairs={{4,0},{12,8},{20,16},{28,24},{5,1},{13,9},{21,17},{29,25},{6,2},{1... | collective-permute-start | bytes 786440 | tf_op jit(solution)/shard_map/ppermute | solution.py:613
  64.2 10.9 %collective-permute-start.7 = (f32[64,1024]{1,0:T(8,128)S(1)}, f32[64,1024]{1,0:T(8,128)S(1)}, u32[]{:S(2)}, u32[]{:S(2)}) collective-permute-start(f32[64,1024]{1,0:T(8,128)S(1)} %get-tuple-element.98), channel_id=1, source_target_pairs={{0,2},{1,3},{2,0},{3,1},{4,6},{5,7},{6,4},{7,5},{8,10},{9,11},{10,... | collective-permute-start | bytes 786440 | tf_op jit(solution)/shard_map/ppermute | solution.py:607
  75.2 8.5 %collective-permute-start.10 = (f32[64,1024]{1,0:T(8,128)S(1)}, f32[64,1024]{1,0:T(8,128)S(1)}, u32[]{:S(2)}, u32[]{:S(2)}) collective-permute-start(f32[64,1024]{1,0:T(8,128)S(1)} %get-tuple-element.133), channel_id=1, source_target_pairs={{8,12},{24,28},{9,13},{25,29},{10,14},{26,30},{11,15},{27,31}} | collective-permute-start | bytes 786440 | tf_op jit(solution)/shard_map/ppermute | solution.py:654
  76.1 8.7 %collective-permute-start.13 = (f32[64,1024]{1,0:T(8,128)S(1)}, f32[64,1024]{1,0:T(8,128)S(1)}, u32[]{:S(2)}, u32[]{:S(2)}) collective-permute-start(f32[64,1024]{1,0:T(8,128)S(1)} %slice.22), channel_id=1, source_target_pairs={{0,2},{1,3},{2,0},{3,1},{4,6},{5,7},{6,4},{7,5},{8,10},{9,11},{10,... | collective-permute-start | bytes 786440 | tf_op jit(solution)/shard_map/ppermute | solution.py:619
  77.9 8.9 %collective-permute-start.12 = (f32[64,1024]{1,0:T(8,128)S(1)}, f32[64,1024]{1,0:T(8,128)S(1)}, u32[]{:S(2)}, u32[]{:S(2)}) collective-permute-start(f32[64,1024]{1,0:T(8,128)S(1)} %get-tuple-element.133), channel_id=1, source_target_pairs={{0,4},{16,20},{1,5},{17,21},{2,6},{18,22},{3,7},{19,23}} | collective-permute-start | bytes 786440 | tf_op jit(solution)/shard_map/ppermute | solution.py:652
  83.7 6.3 %collective-permute-start.11 = (f32[64,1024]{1,0:T(8,128)S(1)}, f32[64,1024]{1,0:T(8,128)S(1)}, u32[]{:S(2)}, u32[]{:S(2)}) collective-permute-start(f32[64,1024]{1,0:T(8,128)S(1)} %add.79), channel_id=1, source_target_pairs={{12,4},{28,20},{13,5},{29,21},{14,6},{30,22},{15,7},{31,23}} | collective-permute-start | bytes 786440 | tf_op jit(solution)/shard_map/ppermute | solution.py:655
  84.5 7.8 %collective-permute-start.18 = (f32[72,1024]{1,0:T(8,128)S(1)}, f32[72,1024]{1,0:T(8,128)S(1)}, u32[]{:S(2)}, u32[]{:S(2)}) collective-permute-start(f32[72,1024]{1,0:T(8,128)S(1)} %slice.24), channel_id=1, source_target_pairs={{0,2},{1,3},{2,0},{3,1},{4,6},{5,7},{6,4},{7,5},{8,10},{9,11},{10,... | collective-permute-start | bytes 884744 | tf_op jit(solution)/shard_map/ppermute | solution.py:619
  84.9 6.8 %collective-permute-start.14 = (f32[64,1024]{1,0:T(8,128)S(1)}, f32[64,1024]{1,0:T(8,128)S(1)}, u32[]{:S(2)}, u32[]{:S(2)}) collective-permute-start(f32[64,1024]{1,0:T(8,128)S(1)} %fusion.3), channel_id=1, source_target_pairs={{0,4},{8,12},{16,20},{24,28},{1,5},{9,13},{17,21},{25,29},{2,6},{1... | collective-permute-start | bytes 786440 | tf_op jit(solution)/shard_map/ppermute | solution.py:660
  92.4 10.0 %collective-permute-start.19 = (f32[72,1024]{1,0:T(8,128)S(1)}, f32[72,1024]{1,0:T(8,128)S(1)}, u32[]{:S(2)}, u32[]{:S(2)}) collective-permute-start(f32[72,1024]{1,0:T(8,128)S(1)} %fusion.1), channel_id=1, source_target_pairs={{0,4},{8,12},{16,20},{24,28},{1,5},{9,13},{17,21},{25,29},{2,6},{1... | collective-permute-start | bytes 884744 | tf_op jit(solution)/shard_map/ppermute | solution.py:646
  96.1 7.0 %collective-permute-start.16 = (f32[64,1024]{1,0:T(8,128)S(1)}, f32[64,1024]{1,0:T(8,128)S(1)}, u32[]{:S(2)}, u32[]{:S(2)}) collective-permute-start(f32[64,1024]{1,0:T(8,128)S(1)} %add.83), channel_id=1, source_target_pairs={{4,12},{5,13},{6,14},{7,15}} | collective-permute-start | bytes 786440 | tf_op jit(solution)/shard_map/ppermute | solution.py:652
  96.8 6.3 %collective-permute-start.17 = (f32[64,1024]{1,0:T(8,128)S(1)}, f32[64,1024]{1,0:T(8,128)S(1)}, u32[]{:S(2)}, u32[]{:S(2)}) collective-permute-start(f32[64,1024]{1,0:T(8,128)S(1)} %add.83), channel_id=1, source_target_pairs={{20,12},{21,13},{22,14},{23,15}} | collective-permute-start | bytes 786440 | tf_op jit(solution)/shard_map/ppermute | solution.py:658
  97.5 5.6 %collective-permute-start.15 = (f32[64,1024]{1,0:T(8,128)S(1)}, f32[64,1024]{1,0:T(8,128)S(1)}, u32[]{:S(2)}, u32[]{:S(2)}) collective-permute-start(f32[64,1024]{1,0:T(8,128)S(1)} %fusion.2.refs_0_), channel_id=1, source_target_pairs={{28,12},{29,13},{30,14},{31,15}} | collective-permute-start | bytes 786440 | tf_op jit(solution)/shard_map/ppermute | solution.py:657
  102.4 2.4 %collective-permute-start.20 = (f32[72,1024]{1,0:T(8,128)S(1)}, f32[72,1024]{1,0:T(8,128)S(1)}, u32[]{:S(2)}, u32[]{:S(2)}) collective-permute-start(f32[72,1024]{1,0:T(8,128)S(1)} %fusion.5), channel_id=1, source_target_pairs={{4,12},{20,28},{5,13},{21,29},{6,14},{22,30},{7,15},{23,31}} | collective-permute-start | bytes 884744 | tf_op jit(solution)/shard_map/ppermute | solution.py:660
  104.9 4.6 %collective-permute-start.22 = (f32[64,1024]{1,0:T(8,128)S(1)}, f32[64,1024]{1,0:T(8,128)S(1)}, u32[]{:S(2)}, u32[]{:S(2)}) collective-permute-start(f32[64,1024]{1,0:T(8,128)S(1)} %get-tuple-element.135), channel_id=1, source_target_pairs={{12,28},{13,29},{14,30},{15,31}} | collective-permute-start | bytes 786440 | tf_op jit(solution)/shard_map/ppermute | solution.py:671
  112.8 28.1 %collective-permute-start.25 = (f32[8,128]{1,0:T(8,128)S(1)}, f32[8,128]{1,0:T(8,128)S(1)}, u32[]{:S(2)}, u32[]{:S(2)}) collective-permute-start(f32[8,128]{1,0:T(8,128)S(1)} %add.92), channel_id=1, source_target_pairs={{4,0},{12,8},{20,16},{28,24},{5,1},{13,9},{21,17},{29,25},{6,2},{1... | collective-permute-start | bytes 12296 | tf_op jit(solution)/shard_map/ppermute | solution.py:688
  (7 other events, 27.1 us)

commit v2 on v1

--- a/solution.py
+++ b/solution.py
@@ -403,23 +403,26 @@
     return own_rhs[...] - total
 
 
-def direct_kernel(count, own_rhs, halves, *refs):
+def direct_kernel(tier, count, where, own_rhs, halves, *refs):
     parts, (left, term) = refs[:count], refs[count:]
-    left[...] = left_of(own_rhs, parts)
-    value = applied(halves[0], halves[1], *operands(doubled(left[...])))
-    term[...] = value.T[: term.shape[0]]
-
-
-def direct(own_rhs, halves, parts):
+
+    @pl.when(where[2] == tier)
+    def _():
+        left[...] = left_of(own_rhs, parts)
+        value = applied(halves[0], halves[1], *operands(doubled(left[...])))
+        term[...] = value.T[: term.shape[0]]
+
+
+def direct(where, tier, own_rhs, halves, parts):
     width, rows = own_rhs.shape
     return pl.pallas_call(
-        functools.partial(direct_kernel, len(parts)),
+        functools.partial(direct_kernel, tier, len(parts)),
         out_shape=(shaped(width, rows), shaped(width, rows)),
-        in_specs=[VMEM] * (2 + len(parts)),
+        in_specs=[SMEM] + [VMEM] * (2 + len(parts)),
         out_specs=(VMEM, VMEM),
-        cost_estimate=cost(rows**2 * 4096),
+        cost_estimate=cost(rows**2 * 64),
         compiler_params=limit(8),
-    )(own_rhs, in_vmem(halves), *parts)
+    )(where, own_rhs, in_vmem(halves), *parts)
 
 
 def tail_of(copies, held, both, high, width, out):
@@ -441,24 +444,22 @@
     panel, refs = refs[0] if with_tail else None, refs[with_tail:]
     out, squares, kept, *sent = refs
     width = left.shape[0]
-    value = applied(halves[2], halves[3], *operands(doubled(left[...])))
-    mine = value.T[:width]
-    kept[...] = value
+
+    @pl.when(where[2] != tier)
+    def _():
+        out[...] = solved[...]
 
     @pl.when(where[2] == tier)
     def _():
-        out[...] = mine
-
-    @pl.when(where[2] != tier)
-    def _():
-        out[...] = solved[...]
-
-    own = jnp.sum(value * value, axis=0, keepdims=True)
-    squares[...] = jnp.broadcast_to(own, squares.shape)
-    if sent:
-        tail_of(None, panel, *operands(value), width, sent[0])
-        if last:
-            with_squares(sent[0], width, squares)
+        value = applied(halves[2], halves[3], *operands(doubled(left[...])))
+        out[...] = value.T[:width]
+        kept[...] = value
+        own = jnp.sum(value * value, axis=0, keepdims=True)
+        squares[...] = jnp.broadcast_to(own, squares.shape)
+        if sent:
+            tail_of(None, panel, *operands(value), width, sent[0])
+            if last:
+                with_squares(sent[0], width, squares)
 
 
 def solve(where, tier, left, halves, solved, panel=None, last=False):
@@ -475,27 +476,30 @@
     )(where, left, in_vmem(halves), solved, *([in_vmem(panel)] if with_tail else []))
 
 
-def tails_kernel(value, squares, panels, *refs):
+def tails_kernel(tier, where, value, squares, panels, *refs):
     sent, (held, arrived) = refs[:-2], refs[-2:]
     width = squares.shape[1] // 2
-    copies = [
-        pieces(panels.at[0, 2 + step], held.at[step], arrived.at[step])
-        for step in range(held.shape[0])
-    ]
-    both, high = operands(value[...])
-    for step, out in enumerate(sent):
-        tail_of(copies[step], held.at[step], both, high, width, out)
-    with_squares(sent[-1], width, squares)
-
-
-def more_tails(value, squares, panels, count):
+
+    @pl.when(where[2] == tier)
+    def _():
+        copies = [
+            pieces(panels.at[0, 2 + step], held.at[step], arrived.at[step])
+            for step in range(held.shape[0])
+        ]
+        both, high = operands(value[...])
+        for step, out in enumerate(sent):
+            tail_of(copies[step], held.at[step], both, high, width, out)
+        with_squares(sent[-1], width, squares)
+
+
+def more_tails(where, tier, value, squares, panels, count):
     rows = value.shape[0]
     width = squares.shape[1] // 2
     shapes = [(width + 8 * (step == count - 1), rows) for step in range(count)]
     return pl.pallas_call(
-        tails_kernel,
+        functools.partial(tails_kernel, tier),
         out_shape=[shaped(*shape) for shape in shapes],
-        in_specs=[VMEM, VMEM, HBM],
+        in_specs=[SMEM, VMEM, VMEM, HBM],
         out_specs=[VMEM] * count,
         scratch_shapes=[
             pltpu.VMEM((count, rows, rows), jnp.float32),
@@ -503,16 +507,22 @@
         ],
         cost_estimate=cost(1),
         compiler_params=limit(8 + 4 * count),
-    )(value, squares, in_hbm(panels))
+    )(where, value, squares, in_hbm(panels))
 
 
 def last_kernel(leaves, count, where, own_rhs, halves, squares, got, first, second, kept, widths):
-    left = left_of(own_rhs, (first, second))
-    value = applied(halves[2], halves[3], *operands(doubled(left)))
-    kept[...] = value
-    total = (squares[...] + got[...]) + jnp.sum(value * value, axis=0, keepdims=True)
-    value = jnp.sqrt(total / count + 1e-06)
-    widths[...] = jnp.where(where[1] == leaves - 1, value, 0.0)
+
+    @pl.when(where[1] != leaves - 1)
+    def _():
+        widths[...] = jnp.zeros_like(widths)
+
+    @pl.when(where[1] == leaves - 1)
+    def _():
+        left = left_of(own_rhs, (first, second))
+        value = applied(halves[2], halves[3], *operands(doubled(left)))
+        kept[...] = value
+        total = (squares[...] + got[...]) + jnp.sum(value * value, axis=0, keepdims=True)
+        widths[...] = jnp.sqrt(total / count + 1e-06)
 
 
 def last(leaves, count, where, own_rhs, halves, squares, got, parts):
@@ -635,7 +645,7 @@
                 direct_right.append((host, parent))
                 early.append((end, parent))
                 aside.append((host, end))
-        left, term = direct(own_rhs, halves, parts)
+        left, term = direct(where, tier, own_rhs, halves, parts)
         count = len(rest)
         solved, own, *more = solve(
             where, tier, left, halves, solved, next_panel if count else None, count == 1
@@ -648,6 +658,8 @@
             ]
         if count:
             value, tail = more
+            if tier > 1:
+                term, tail = lax.optimization_barrier((term, tail))
             term = following + term
             from_left = lax.ppermute(term, "leaf", direct_left)
             if tier == 1:
@@ -662,7 +674,7 @@
             waiting = []
             if count > 1:
                 value, _ = lax.optimization_barrier((value, from_left))
-                waiting = more_tails(value, own, sep_panels, count - 1)
+                waiting = more_tails(where, tier, value, own, sep_panels, count - 1)
                 parts[1], *waiting = lax.optimization_barrier((parts[1], *waiting))
             before = onward
         else:

time: 142 us -> 138 us (0.972)
  Pallas kernels: 53.2 us -> 46.2 us
  waiting for transfers between devices: 43.9 us -> 48.1 us
    pallas_call x3, Pallas kernels: 10.8 us -> 6.28 us  [solve(): pl.pallas_call(functools.partial(solve_kernel, tier, last, with_tail), ou...]
    ppermute x2, waiting for transfers between devices: 0.57 us -> 2.19 us  [local(): lax.ppermute(away[start:stop], 'grid', over)]
    ppermute x3, waiting for transfers between devices: 25.5 us -> 27 us  [local(): widths = widths + lax.ppermute(widths, 'leaf', steps)]
    ppermute x2, starting transfers between devices: 2.17 us -> 3.61 us  [local(): lax.ppermute(away[start:stop], 'grid', over)]
    pallas_call x1, Pallas kernels: 1.99 us -> 0.56 us  [last(): pl.pallas_call(functools.partial(last_kernel, leaves, count), out_shape=(...]
  transfers between devices with their start and end apart: 27 -> 27, of which waited for: 8 -> 10; matrix products, arithmetic and copies ran while one was open for 0% -> 0% of each run, Pallas kernels for 31% -> 28%
where the time goes in v2:
time: 138 us
  waiting for transfers between devices  48.1 us (35%)
  Pallas kernels  46.2 us (33%)
  starting transfers between devices  39 us (28%)
  local copies, waits for them, and re-layouts  2.85 us (2%)
    ppermute x3, waiting for transfers between devices, local(): widths = widths + lax.ppermute(widths, 'leaf', steps)  27 us
    pallas_call x1, Pallas kernels, prepared(): pl.pallas_call(prepare_kernel, out_shape=pltpu.HBM((4, rows, rows), jnp.b...  8.44 us
    all_to_all x1, starting transfers between devices, local(): lax.all_to_all(picked.reshape(block_count, block_rows // block_count, col...  7.3 us
    all_to_all x1, waiting for transfers between devices, local(): lax.all_to_all(picked.reshape(block_count, block_rows // block_count, col...  7.1 us
    pallas_call x3, Pallas kernels, solve(): pl.pallas_call(functools.partial(solve_kernel, tier, last, with_tail), ou...  6.28 us
    pallas_call x1, Pallas kernels, loaded(): pl.pallas_call(load_kernel, out_shape=(pltpu.VMEM(halves.shape, jnp.bfloa...  5.92 us
    ppermute x1, waiting for transfers between devices, local(): lax.ppermute(mine, 'leaf', pairs)  4.55 us
    pallas_call x1, Pallas kernels, more_tails(): pl.pallas_call(functools.partial(tails_kernel, tier), out_shape=[shaped(*...  3.72 us
  transfers between devices with their start and end apart: 27, of which 10 were waited for; matrix products, arithmetic and copies ran while one was open for 0% of the time, Pallas kernels for 28%

profile of v2, /device:TPU:0, one launch (start us, length us, event | category | flops | bytes accessed | tf_op | source)
XLA Modules:
  0.0 137.9 jit_solution(11728066222394057600)
XLA Ops:
  0.6 2.5 %shard_map.103 = f32[512,256]{1,0:T(8,128)} custom-call(s32[1,512]{1,0:T(1,128)} %bitcast.31, f32[512,256]{1,0:T(8,128)} %rows.1), custom_call_target="tpu_custom_call" | custom-call | flops 1610612736 | bytes 4194304 | tf_op jit(solution)/shard_map/pallas_call | solution.py:79
  3.3 7.3 %all-to-all-start = ((f32[32,16,256]{2,1,0:T(8,128)}), f32[32,16,256]{2,1,0:T(8,128)S(1)}, u32[]{:S(2)}, u32[]{:S(2)}) async-start(f32[32,16,256]{2,1,0:T(8,128)} %bitcast.4), calls=%async_computation | async-start | bytes 1048576 | tf_op jit(solution)/shard_map/all_to_all | solution.py:581
  10.6 8.4 %shard_map.104.halves = bf16[4,1024,1024]{2,1,0:T(8,128)(2,1)} custom-call(f32[1,1024,1024]{2,1,0:T(8,128)} %inverse, f32[1,3,1024,1024]{3,2,1,0:T(8,128)} %panels.5), custom_call_target="tpu_custom_call" | custom-call | flops 25769803776 | bytes 4194304 | tf_op jit(solution)/shard_map/pallas_call | solution.py:318
  19.0 7.1 %all-to-all-done = f32[32,16,256]{2,1,0:T(8,128)S(1)} async-done(((f32[32,16,256]{2,1,0:T(8,128)}), f32[32,16,256]{2,1,0:T(8,128)S(1)}, u32[]{:S(2)}, u32[]{:S(2)}) %all-to-all-start) | async-done | bytes 524320 | tf_op jit(solution)/shard_map/all_to_all | solution.py:581
  26.1 2.2 %copy-done.1 = f32[2048,512]{1,0:T(8,128)S(1)} copy-done((f32[2048,512]{1,0:T(8,128)S(1)}, f32[2048,512]{1,0:T(8,128)}, u32[]{:S(2)}) %copy-start.1) | copy-done | bytes 4194328
  29.8 1.9 %collective-permute-start = (f32[512,256]{1,0:T(8,128)S(1)}, f32[512,256]{1,0:T(8,128)S(1)}, u32[]{:S(2)}, u32[]{:S(2)}) collective-permute-start(f32[512,256]{1,0:T(8,128)S(1)} %get-tuple-element.76), channel_id=1, source_target_pairs={{0,1},{1,0},{2,3},{4,5},{5,4},{6,7},{8,9},{9,8},{10,11},{12,13},{1... | collective-permute-start | bytes 1572872 | tf_op jit(solution)/shard_map/ppermute | solution.py:595
  31.8 1.9 %collective-permute-done.in_chip = f32[512,256]{1,0:T(8,128)S(1)} collective-permute-done((f32[512,256]{1,0:T(8,128)S(1)}, f32[512,256]{1,0:T(8,128)S(1)}, u32[]{:S(2)}, u32[]{:S(2)}) %collective-permute-start) | collective-permute-done | bytes 524320 | tf_op jit(solution)/shard_map/ppermute | solution.py:595
  33.7 2.9 %collective-permute-start.1 = (f32[512,256]{1,0:T(8,128)S(1)}, f32[512,256]{1,0:T(8,128)S(1)}, u32[]{:S(2)}, u32[]{:S(2)}) collective-permute-start(f32[512,256]{1,0:T(8,128)S(1)} %add.75), channel_id=1, source_target_pairs={{0,2},{1,3},{4,6},{5,7},{8,10},{9,11},{12,14},{13,15},{16,18},{17,... | collective-permute-start | bytes 1572872 | tf_op jit(solution)/shard_map/ppermute | solution.py:598
  38.2 2.0 %collective-permute-start.2 = (f32[256,256]{1,0:T(8,128)S(1)}, f32[256,256]{1,0:T(8,128)S(1)}, u32[]{:S(2)}, u32[]{:S(2)}) collective-permute-start(f32[256,256]{1,0:T(8,128)S(1)} %get-tuple-element.81.top), channel_id=1, source_target_pairs={{0,1},{4,5},{8,9},{12,13},{16,17},{20,21},{24,25},{28,29}} | collective-permute-start | bytes 786440 | tf_op jit(solution)/shard_map/ppermute | solution.py:600
  41.6 5.9 %shard_map.107 = (bf16[4,1024,1024]{2,1,0:T(8,128)(2,1)S(1)}, f32[4,1024,512]{2,1,0:T(8,128)S(1)}) custom-call(bf16[4,1024,1024]{2,1,0:T(8,128)(2,1)} %shard_map.104.halves, f32[1,4,1024,512]{3,2,1,0:T(8,128)} %panels.3), custom_call_target="tpu_custom_call" | custom-call | flops 24 | bytes 4194304 | tf_op jit(solution)/shard_map/pallas_call | solution.py:349
  48.3 2.5 %shard_map.108 = (f32[512,256]{1,0:T(8,128)}, f32[256,512]{1,0:T(8,128)S(1)}, f32[8,256]{1,0:T(8,128)S(1)}, f32[2,64,1024]{2,1,0:T(8,128)S(1)}, f32[2,64,1024]{2,1,0:T(8,128)S(1)}) custom-call(s32[3]{0:T(128)S(1)} %pad_add_fusion.place.where, f32[512,256]{1,0:T(8,128)S(1)} %get-tuple-element.75.kept_in, f32[512,256]{1,0:T(8,128)S(1)} %collective-permute-done.in_chip, ...), custom_call_target="tpu_custom_call" | custom-call | flops 3221225472 | bytes 4194304 | tf_op jit(solution)/shard_map/pallas_call | solution.py:178
  53.7 2.5 %collective-permute-start.6 = (f32[64,1024]{1,0:T(8,128)S(1)}, f32[64,1024]{1,0:T(8,128)S(1)}, u32[]{:S(2)}, u32[]{:S(2)}) collective-permute-start(f32[64,1024]{1,0:T(8,128)S(1)} %get-tuple-element.95), channel_id=1, source_target_pairs={{0,2},{1,3},{2,0},{3,1},{4,6},{5,7},{6,4},{7,5},{8,10},{9,11},{10,... | collective-permute-start | bytes 786440 | tf_op jit(solution)/shard_map/ppermute | solution.py:612
  56.2 2.9 %shard_map.112 = (f32[2,136,1024]{2,1,0:T(8,128)S(1)}, f32[2,136,1024]{2,1,0:T(8,128)S(1)}) custom-call(s32[3]{0:T(128)S(1)} %pad_add_fusion.place.where, f32[8,256]{1,0:T(8,128)S(1)} %get-tuple-element.97.squares, f32[256,512]{1,0:T(8,128)S(1)} %get-tuple-element.98.turned, f32[4,512]{1,0:T(4,128)S(1)} %bitcast.29, f32[4,1024,512]{2,1,0:T(8,128)S(1)} %get-tuple-element.84.panels), custom_call_target="tpu_custom_call" | custom-call | flops 24 | bytes 4194304 | tf_op jit(solution)/shard_map/pallas_call | solution.py:232
  59.6 3.2 %collective-permute-done.6 = f32[64,1024]{1,0:T(8,128)S(1)} collective-permute-done((f32[64,1024]{1,0:T(8,128)S(1)}, f32[64,1024]{1,0:T(8,128)S(1)}, u32[]{:S(2)}, u32[]{:S(2)}) %collective-permute-start.6) | collective-permute-done | bytes 262176 | tf_op jit(solution)/shard_map/ppermute | solution.py:612
  64.2 1.8 %collective-permute-start.7 = (f32[64,1024]{1,0:T(8,128)S(1)}, f32[64,1024]{1,0:T(8,128)S(1)}, u32[]{:S(2)}, u32[]{:S(2)}) collective-permute-start(f32[64,1024]{1,0:T(8,128)S(1)} %get-tuple-element.100), channel_id=1, source_target_pairs={{0,2},{1,3},{2,0},{3,1},{4,6},{5,7},{6,4},{7,5},{8,10},{9,11},{10,... | collective-permute-start | bytes 786440 | tf_op jit(solution)/shard_map/ppermute | solution.py:617
  66.7 2.3 %shard_map.114.refs_0_ = f32[1024,1024]{1,0:T(8,128)S(1)} custom-call(f32[1,3,1024,1024]{3,2,1,0:T(8,128)} %panels.5), custom_call_target="tpu_custom_call" | custom-call | flops 24 | bytes 4194304 | tf_op jit(solution)/shard_map/pallas_call | solution.py:370
  69.0 4.6 %collective-permute-done.8.refs_1_ = f32[64,1024]{1,0:T(8,128)S(1)} collective-permute-done((f32[64,1024]{1,0:T(8,128)S(1)}, f32[64,1024]{1,0:T(8,128)S(1)}, u32[]{:S(2)}, u32[]{:S(2)}) %collective-permute-start.8) | collective-permute-done | bytes 262176 | tf_op jit(solution)/shard_map/ppermute | solution.py:623
  73.5 2.2 %shard_map.115 = (f32[64,1024]{1,0:T(8,128)S(1)}, f32[64,1024]{1,0:T(8,128)S(1)}) custom-call(s32[3]{0:T(128)S(1)} %pad_add_fusion.place.where, f32[64,1024]{1,0:T(8,128)S(1)} %bitcast.21, bf16[4,1024,1024]{2,1,0:T(8,128)(2,1)S(1)} %get-tuple-element.86.halves, f32[64,1024]{1,0:T(8,128)S(1)} %add.77.refs_0_, f32[64,1024]{1,0:T(8,128)S(1)} %collective-permute-done.8.refs_1_), custom_call_target="tpu_custom_call" | custom-call | flops 1610612736 | bytes 4194304 | tf_op jit(solution)/shard_map/pallas_call | solution.py:418
  76.6 1.8 %collective-permute-start.13 = (f32[64,1024]{1,0:T(8,128)S(1)}, f32[64,1024]{1,0:T(8,128)S(1)}, u32[]{:S(2)}, u32[]{:S(2)}) collective-permute-start(f32[64,1024]{1,0:T(8,128)S(1)} %slice.22), channel_id=1, source_target_pairs={{0,2},{1,3},{2,0},{3,1},{4,6},{5,7},{6,4},{7,5},{8,10},{9,11},{10,... | collective-permute-start | bytes 786440 | tf_op jit(solution)/shard_map/ppermute | solution.py:629
  80.1 3.3 %shard_map.116 = (f32[64,1024]{1,0:T(8,128)S(1)}, f32[8,128]{1,0:T(8,128)S(1)}, f32[1024,128]{1,0:T(8,128)S(1)}, f32[64,1024]{1,0:T(8,128)S(1)}) custom-call(s32[3]{0:T(128)S(1)} %pad_add_fusion.place.where, f32[64,1024]{1,0:T(8,128)S(1)} %get-tuple-element.110.left, bf16[4,1024,1024]{2,1,0:T(8,128)(2,1)S(1)} %get-tuple-element.86.halves, ...), custom_call_target="tpu_custom_call" | custom-call | flops 24 | bytes 4194304 | tf_op jit(solution)/shard_map/pallas_call | solution.py:468
  86.0 1.8 %collective-permute-start.18 = (f32[72,1024]{1,0:T(8,128)S(1)}, f32[72,1024]{1,0:T(8,128)S(1)}, u32[]{:S(2)}, u32[]{:S(2)}) collective-permute-start(f32[72,1024]{1,0:T(8,128)S(1)} %slice.24), channel_id=1, source_target_pairs={{0,2},{1,3},{2,0},{3,1},{4,6},{5,7},{6,4},{7,5},{8,10},{9,11},{10,... | collective-permute-start | bytes 884744 | tf_op jit(solution)/shard_map/ppermute | solution.py:629
  87.8 3.7 %shard_map.117 = f32[72,1024]{1,0:T(8,128)S(1)} custom-call(s32[3]{0:T(128)S(1)} %pad_add_fusion.place.where, f32[1024,128]{1,0:T(8,128)S(1)} %get-tuple-element.115.value, f32[8,128]{1,0:T(8,128)S(1)} %get-tuple-element.116.squares, f32[1,3,1024,1024]{3,2,1,0:T(8,128)} %panels.5), custom_call_target="tpu_custom_call" | custom-call | flops 24 | bytes 4194304 | tf_op jit(solution)/shard_map/pallas_call | solution.py:499
  93.9 2.9 %collective-permute-start.19 = (f32[72,1024]{1,0:T(8,128)S(1)}, f32[72,1024]{1,0:T(8,128)S(1)}, u32[]{:S(2)}, u32[]{:S(2)}) collective-permute-start(f32[72,1024]{1,0:T(8,128)S(1)} %fusion.1), channel_id=1, source_target_pairs={{0,4},{8,12},{16,20},{24,28},{1,5},{9,13},{17,21},{25,29},{2,6},{1... | collective-permute-start | bytes 884744 | tf_op jit(solution)/shard_map/ppermute | solution.py:656
  110.4 27.0 %collective-permute-done.25 = f32[8,128]{1,0:T(8,128)S(1)} collective-permute-done((f32[8,128]{1,0:T(8,128)S(1)}, f32[8,128]{1,0:T(8,128)S(1)}, u32[]{:S(2)}, u32[]{:S(2)}) %collective-permute-start.25) | collective-permute-done | bytes 4128 | tf_op jit(solution)/shard_map/ppermute | solution.py:700
  (82 shorter events, 32.2 us)
Async XLA Ops:
  3.3 22.9 %all-to-all-start = ((f32[32,16,256]{2,1,0:T(8,128)}), f32[32,16,256]{2,1,0:T(8,128)S(1)}, u32[]{:S(2)}, u32[]{:S(2)}) async-start(f32[32,16,256]{2,1,0:T(8,128)} %bitcast.4), calls=%async_computation | async-start | bytes 1048576 | tf_op jit(solution)/shard_map/all_to_all | solution.py:581
  29.8 3.8 %collective-permute-start = (f32[512,256]{1,0:T(8,128)S(1)}, f32[512,256]{1,0:T(8,128)S(1)}, u32[]{:S(2)}, u32[]{:S(2)}) collective-permute-start(f32[512,256]{1,0:T(8,128)S(1)} %get-tuple-element.76), channel_id=1, source_target_pairs={{0,1},{1,0},{2,3},{4,5},{5,4},{6,7},{8,9},{9,8},{10,11},{12,13},{1... | collective-permute-start | bytes 1572872 | tf_op jit(solution)/shard_map/ppermute | solution.py:595
  33.7 14.6 %collective-permute-start.1 = (f32[512,256]{1,0:T(8,128)S(1)}, f32[512,256]{1,0:T(8,128)S(1)}, u32[]{:S(2)}, u32[]{:S(2)}) collective-permute-start(f32[512,256]{1,0:T(8,128)S(1)} %add.75), channel_id=1, source_target_pairs={{0,2},{1,3},{4,6},{5,7},{8,10},{9,11},{12,14},{13,15},{16,18},{17,... | collective-permute-start | bytes 1572872 | tf_op jit(solution)/shard_map/ppermute | solution.py:598
  38.2 9.3 %collective-permute-start.2 = (f32[256,256]{1,0:T(8,128)S(1)}, f32[256,256]{1,0:T(8,128)S(1)}, u32[]{:S(2)}, u32[]{:S(2)}) collective-permute-start(f32[256,256]{1,0:T(8,128)S(1)} %get-tuple-element.81.top), channel_id=1, source_target_pairs={{0,1},{4,5},{8,9},{12,13},{16,17},{20,21},{24,25},{28,29}} | collective-permute-start | bytes 786440 | tf_op jit(solution)/shard_map/ppermute | solution.py:600
  40.2 7.4 %collective-permute-start.3 = (f32[256,256]{1,0:T(8,128)S(1)}, f32[256,256]{1,0:T(8,128)S(1)}, u32[]{:S(2)}, u32[]{:S(2)}) collective-permute-start(f32[256,256]{1,0:T(8,128)S(1)} %get-tuple-element.82.bottom), channel_id=1, source_target_pairs={{0,1},{4,5},{8,9},{12,13},{16,17},{20,21},{24,25},{28,29}} | collective-permute-start | bytes 786440 | tf_op jit(solution)/shard_map/ppermute | solution.py:600
  50.8 1.9 %collective-permute-start.4 = (f32[2,64,1024]{2,1,0:T(8,128)S(1)}, f32[2,64,1024]{2,1,0:T(8,128)S(1)}, u32[]{:S(2)}, u32[]{:S(2)}) collective-permute-start(f32[2,64,1024]{2,1,0:T(8,128)S(1)} %get-tuple-element.90), channel_id=1, source_target_pairs={{0,1},{1,0},{2,3},{3,2},{4,5},{5,4},{6,7},{7,6},{8,9},{9,8},{10,11... | collective-permute-start | bytes 1572872 | tf_op jit(solution)/shard_map/ppermute | solution.py:608
  53.3 5.7 %collective-permute-start.5 = (f32[2,64,1024]{2,1,0:T(8,128)S(1)}, f32[2,64,1024]{2,1,0:T(8,128)S(1)}, u32[]{:S(2)}, u32[]{:S(2)}) collective-permute-start(f32[2,64,1024]{2,1,0:T(8,128)S(1)} %get-tuple-element.93), channel_id=1, source_target_pairs={{0,1},{1,0},{2,3},{3,2},{4,5},{5,4},{6,7},{7,6},{8,9},{9,8},{10,11... | collective-permute-start | bytes 1572872 | tf_op jit(solution)/shard_map/ppermute | solution.py:613
  53.7 9.2 %collective-permute-start.6 = (f32[64,1024]{1,0:T(8,128)S(1)}, f32[64,1024]{1,0:T(8,128)S(1)}, u32[]{:S(2)}, u32[]{:S(2)}) collective-permute-start(f32[64,1024]{1,0:T(8,128)S(1)} %get-tuple-element.95), channel_id=1, source_target_pairs={{0,2},{1,3},{2,0},{3,1},{4,6},{5,7},{6,4},{7,5},{8,10},{9,11},{10,... | collective-permute-start | bytes 786440 | tf_op jit(solution)/shard_map/ppermute | solution.py:612
  62.9 3.2 %collective-permute-start.9 = (f32[2,136,1024]{2,1,0:T(8,128)S(1)}, f32[2,136,1024]{2,1,0:T(8,128)S(1)}, u32[]{:S(2)}, u32[]{:S(2)}) collective-permute-start(f32[2,136,1024]{2,1,0:T(8,128)S(1)} %get-tuple-element.104), channel_id=1, source_target_pairs={{0,1},{1,0},{2,3},{3,2},{4,5},{5,4},{6,7},{7,6},{8,9},{9,8},{10,11... | collective-permute-start | bytes 3342344 | tf_op jit(solution)/shard_map/ppermute | solution.py:618
  62.9 10.6 %collective-permute-start.8 = (f32[64,1024]{1,0:T(8,128)S(1)}, f32[64,1024]{1,0:T(8,128)S(1)}, u32[]{:S(2)}, u32[]{:S(2)}) collective-permute-start(f32[64,1024]{1,0:T(8,128)S(1)} %add.77.refs_0_), channel_id=1, source_target_pairs={{4,0},{12,8},{20,16},{28,24},{5,1},{13,9},{21,17},{29,25},{6,2},{1... | collective-permute-start | bytes 786440 | tf_op jit(solution)/shard_map/ppermute | solution.py:623
  64.2 11.5 %collective-permute-start.7 = (f32[64,1024]{1,0:T(8,128)S(1)}, f32[64,1024]{1,0:T(8,128)S(1)}, u32[]{:S(2)}, u32[]{:S(2)}) collective-permute-start(f32[64,1024]{1,0:T(8,128)S(1)} %get-tuple-element.100), channel_id=1, source_target_pairs={{0,2},{1,3},{2,0},{3,1},{4,6},{5,7},{6,4},{7,5},{8,10},{9,11},{10,... | collective-permute-start | bytes 786440 | tf_op jit(solution)/shard_map/ppermute | solution.py:617
  75.8 7.6 %collective-permute-start.10 = (f32[64,1024]{1,0:T(8,128)S(1)}, f32[64,1024]{1,0:T(8,128)S(1)}, u32[]{:S(2)}, u32[]{:S(2)}) collective-permute-start(f32[64,1024]{1,0:T(8,128)S(1)} %get-tuple-element.137), channel_id=1, source_target_pairs={{8,12},{24,28},{9,13},{25,29},{10,14},{26,30},{11,15},{27,31}} | collective-permute-start | bytes 786440 | tf_op jit(solution)/shard_map/ppermute | solution.py:666
  76.6 8.0 %collective-permute-start.13 = (f32[64,1024]{1,0:T(8,128)S(1)}, f32[64,1024]{1,0:T(8,128)S(1)}, u32[]{:S(2)}, u32[]{:S(2)}) collective-permute-start(f32[64,1024]{1,0:T(8,128)S(1)} %slice.22), channel_id=1, source_target_pairs={{0,2},{1,3},{2,0},{3,1},{4,6},{5,7},{6,4},{7,5},{8,10},{9,11},{10,... | collective-permute-start | bytes 786440 | tf_op jit(solution)/shard_map/ppermute | solution.py:629
  78.5 9.4 %collective-permute-start.12 = (f32[64,1024]{1,0:T(8,128)S(1)}, f32[64,1024]{1,0:T(8,128)S(1)}, u32[]{:S(2)}, u32[]{:S(2)}) collective-permute-start(f32[64,1024]{1,0:T(8,128)S(1)} %get-tuple-element.137), channel_id=1, source_target_pairs={{0,4},{16,20},{1,5},{17,21},{2,6},{18,22},{3,7},{19,23}} | collective-permute-start | bytes 786440 | tf_op jit(solution)/shard_map/ppermute | solution.py:664
  83.4 8.2 %collective-permute-start.11 = (f32[64,1024]{1,0:T(8,128)S(1)}, f32[64,1024]{1,0:T(8,128)S(1)}, u32[]{:S(2)}, u32[]{:S(2)}) collective-permute-start(f32[64,1024]{1,0:T(8,128)S(1)} %add.79), channel_id=1, source_target_pairs={{12,4},{28,20},{13,5},{29,21},{14,6},{30,22},{15,7},{31,23}} | collective-permute-start | bytes 786440 | tf_op jit(solution)/shard_map/ppermute | solution.py:667
  84.7 7.5 %collective-permute-start.14 = (f32[64,1024]{1,0:T(8,128)S(1)}, f32[64,1024]{1,0:T(8,128)S(1)}, u32[]{:S(2)}, u32[]{:S(2)}) collective-permute-start(f32[64,1024]{1,0:T(8,128)S(1)} %fusion.3), channel_id=1, source_target_pairs={{0,4},{8,12},{16,20},{24,28},{1,5},{9,13},{17,21},{25,29},{2,6},{1... | collective-permute-start | bytes 786440 | tf_op jit(solution)/shard_map/ppermute | solution.py:672
  86.0 7.8 %collective-permute-start.18 = (f32[72,1024]{1,0:T(8,128)S(1)}, f32[72,1024]{1,0:T(8,128)S(1)}, u32[]{:S(2)}, u32[]{:S(2)}) collective-permute-start(f32[72,1024]{1,0:T(8,128)S(1)} %slice.24), channel_id=1, source_target_pairs={{0,2},{1,3},{2,0},{3,1},{4,6},{5,7},{6,4},{7,5},{8,10},{9,11},{10,... | collective-permute-start | bytes 884744 | tf_op jit(solution)/shard_map/ppermute | solution.py:629
  93.9 7.5 %collective-permute-start.19 = (f32[72,1024]{1,0:T(8,128)S(1)}, f32[72,1024]{1,0:T(8,128)S(1)}, u32[]{:S(2)}, u32[]{:S(2)}) collective-permute-start(f32[72,1024]{1,0:T(8,128)S(1)} %fusion.1), channel_id=1, source_target_pairs={{0,4},{8,12},{16,20},{24,28},{1,5},{9,13},{17,21},{25,29},{2,6},{1... | collective-permute-start | bytes 884744 | tf_op jit(solution)/shard_map/ppermute | solution.py:656
  98.2 3.9 %collective-permute-start.16 = (f32[64,1024]{1,0:T(8,128)S(1)}, f32[64,1024]{1,0:T(8,128)S(1)}, u32[]{:S(2)}, u32[]{:S(2)}) collective-permute-start(f32[64,1024]{1,0:T(8,128)S(1)} %add.83), channel_id=1, source_target_pairs={{4,12},{5,13},{6,14},{7,15}} | collective-permute-start | bytes 786440 | tf_op jit(solution)/shard_map/ppermute | solution.py:664
  98.9 3.3 %collective-permute-start.17 = (f32[64,1024]{1,0:T(8,128)S(1)}, f32[64,1024]{1,0:T(8,128)S(1)}, u32[]{:S(2)}, u32[]{:S(2)}) collective-permute-start(f32[64,1024]{1,0:T(8,128)S(1)} %add.83), channel_id=1, source_target_pairs={{20,12},{21,13},{22,14},{23,15}} | collective-permute-start | bytes 786440 | tf_op jit(solution)/shard_map/ppermute | solution.py:670
  99.6 2.6 %collective-permute-start.15 = (f32[64,1024]{1,0:T(8,128)S(1)}, f32[64,1024]{1,0:T(8,128)S(1)}, u32[]{:S(2)}, u32[]{:S(2)}) collective-permute-start(f32[64,1024]{1,0:T(8,128)S(1)} %fusion.2.refs_0_), channel_id=1, source_target_pairs={{28,12},{29,13},{30,14},{31,15}} | collective-permute-start | bytes 786440 | tf_op jit(solution)/shard_map/ppermute | solution.py:669
  101.5 1.3 collective-permute-start.20
  102.9 3.0 %collective-permute-start.22 = (f32[64,1024]{1,0:T(8,128)S(1)}, f32[64,1024]{1,0:T(8,128)S(1)}, u32[]{:S(2)}, u32[]{:S(2)}) collective-permute-start(f32[64,1024]{1,0:T(8,128)S(1)} %get-tuple-element.139), channel_id=1, source_target_pairs={{12,28},{13,29},{14,30},{15,31}} | collective-permute-start | bytes 786440 | tf_op jit(solution)/shard_map/ppermute | solution.py:683
  107.8 29.6 %collective-permute-start.25 = (f32[8,128]{1,0:T(8,128)S(1)}, f32[8,128]{1,0:T(8,128)S(1)}, u32[]{:S(2)}, u32[]{:S(2)}) collective-permute-start(f32[8,128]{1,0:T(8,128)S(1)} %add.92), channel_id=1, source_target_pairs={{4,0},{12,8},{20,16},{28,24},{5,1},{13,9},{21,17},{29,25},{6,2},{1... | collective-permute-start | bytes 12296 | tf_op jit(solution)/shard_map/ppermute | solution.py:700
  (7 other events, 27.1 us)

commit v3 on v2

--- a/solution.py
+++ b/solution.py
@@ -667,6 +667,7 @@
                 parts = [following, lax.ppermute(following + turn, "leaf", early), from_left]
             else:
                 next_early = lax.ppermute(following, "leaf", early)
+                next_early, rest[0] = lax.optimization_barrier((next_early, rest[0]))
                 from_right = lax.ppermute(term, "leaf", direct_right)
                 parts = [following, next_early, from_left, from_right]
             following = rest[0] + lax.ppermute(rest[0] + tail, "leaf", onward)

time: 138 us -> 138 us (level)
  no operation moved by 1% of the time
where the time goes in v3:
time: 138 us; the launch traced here: 137 us
  waiting for transfers between devices  47.6 us (34%)
  Pallas kernels  46.2 us (33%)
  starting transfers between devices  39 us (28%)
  local copies, waits for them, and re-layouts  2.85 us (2%)
    ppermute x3, waiting for transfers between devices, local(): widths = widths + lax.ppermute(widths, 'leaf', steps)  26.5 us
    pallas_call x1, Pallas kernels, prepared(): pl.pallas_call(prepare_kernel, out_shape=pltpu.HBM((4, rows, rows), jnp.b...  8.44 us
    all_to_all x1, starting transfers between devices, local(): lax.all_to_all(picked.reshape(block_count, block_rows // block_count, col...  7.3 us
    all_to_all x1, waiting for transfers between devices, local(): lax.all_to_all(picked.reshape(block_count, block_rows // block_count, col...  7.1 us
    pallas_call x3, Pallas kernels, solve(): pl.pallas_call(functools.partial(solve_kernel, tier, last, with_tail), ou...  6.28 us
    pallas_call x1, Pallas kernels, loaded(): pl.pallas_call(load_kernel, out_shape=(pltpu.VMEM(halves.shape, jnp.bfloa...  5.92 us
    ppermute x1, waiting for transfers between devices, local(): lax.ppermute(mine, 'leaf', pairs)  4.55 us
    pallas_call x1, Pallas kernels, more_tails(): pl.pallas_call(functools.partial(tails_kernel, tier), out_shape=[shaped(*...  3.72 us
  transfers between devices with their start and end apart: 27, of which 10 were waited for; matrix products, arithmetic and copies ran while one was open for 0% of the time, Pallas kernels for 28%

profile of v3, /device:TPU:0, one launch (start us, length us, event | category | flops | bytes accessed | tf_op | source)
XLA Modules:
  0.0 137.4 jit_solution(16239900687192382627)
XLA Ops:
  0.6 2.5 %shard_map.103 = f32[512,256]{1,0:T(8,128)} custom-call(s32[1,512]{1,0:T(1,128)} %bitcast.31, f32[512,256]{1,0:T(8,128)} %rows.1), custom_call_target="tpu_custom_call" | custom-call | flops 1610612736 | bytes 4194304 | tf_op jit(solution)/shard_map/pallas_call | solution.py:79
  3.3 7.3 %all-to-all-start = ((f32[32,16,256]{2,1,0:T(8,128)}), f32[32,16,256]{2,1,0:T(8,128)S(1)}, u32[]{:S(2)}, u32[]{:S(2)}) async-start(f32[32,16,256]{2,1,0:T(8,128)} %bitcast.4), calls=%async_computation | async-start | bytes 1048576 | tf_op jit(solution)/shard_map/all_to_all | solution.py:581
  10.6 8.4 %shard_map.104.halves = bf16[4,1024,1024]{2,1,0:T(8,128)(2,1)} custom-call(f32[1,1024,1024]{2,1,0:T(8,128)} %inverse, f32[1,3,1024,1024]{3,2,1,0:T(8,128)} %panels.5), custom_call_target="tpu_custom_call" | custom-call | flops 25769803776 | bytes 4194304 | tf_op jit(solution)/shard_map/pallas_call | solution.py:318
  19.0 7.1 %all-to-all-done = f32[32,16,256]{2,1,0:T(8,128)S(1)} async-done(((f32[32,16,256]{2,1,0:T(8,128)}), f32[32,16,256]{2,1,0:T(8,128)S(1)}, u32[]{:S(2)}, u32[]{:S(2)}) %all-to-all-start) | async-done | bytes 524320 | tf_op jit(solution)/shard_map/all_to_all | solution.py:581
  26.1 2.2 %copy-done.1 = f32[2048,512]{1,0:T(8,128)S(1)} copy-done((f32[2048,512]{1,0:T(8,128)S(1)}, f32[2048,512]{1,0:T(8,128)}, u32[]{:S(2)}) %copy-start.1) | copy-done | bytes 4194328
  29.8 1.9 %collective-permute-start = (f32[512,256]{1,0:T(8,128)S(1)}, f32[512,256]{1,0:T(8,128)S(1)}, u32[]{:S(2)}, u32[]{:S(2)}) collective-permute-start(f32[512,256]{1,0:T(8,128)S(1)} %get-tuple-element.78), channel_id=1, source_target_pairs={{0,1},{1,0},{2,3},{4,5},{5,4},{6,7},{8,9},{9,8},{10,11},{12,13},{1... | collective-permute-start | bytes 1572872 | tf_op jit(solution)/shard_map/ppermute | solution.py:595
  31.8 1.9 %collective-permute-done.in_chip = f32[512,256]{1,0:T(8,128)S(1)} collective-permute-done((f32[512,256]{1,0:T(8,128)S(1)}, f32[512,256]{1,0:T(8,128)S(1)}, u32[]{:S(2)}, u32[]{:S(2)}) %collective-permute-start) | collective-permute-done | bytes 524320 | tf_op jit(solution)/shard_map/ppermute | solution.py:595
  33.7 2.9 %collective-permute-start.1 = (f32[512,256]{1,0:T(8,128)S(1)}, f32[512,256]{1,0:T(8,128)S(1)}, u32[]{:S(2)}, u32[]{:S(2)}) collective-permute-start(f32[512,256]{1,0:T(8,128)S(1)} %add.75), channel_id=1, source_target_pairs={{0,2},{1,3},{4,6},{5,7},{8,10},{9,11},{12,14},{13,15},{16,18},{17,... | collective-permute-start | bytes 1572872 | tf_op jit(solution)/shard_map/ppermute | solution.py:598
  38.2 2.0 %collective-permute-start.2 = (f32[256,256]{1,0:T(8,128)S(1)}, f32[256,256]{1,0:T(8,128)S(1)}, u32[]{:S(2)}, u32[]{:S(2)}) collective-permute-start(f32[256,256]{1,0:T(8,128)S(1)} %get-tuple-element.83.top), channel_id=1, source_target_pairs={{0,1},{4,5},{8,9},{12,13},{16,17},{20,21},{24,25},{28,29}} | collective-permute-start | bytes 786440 | tf_op jit(solution)/shard_map/ppermute | solution.py:600
  41.6 5.9 %shard_map.107 = (bf16[4,1024,1024]{2,1,0:T(8,128)(2,1)S(1)}, f32[4,1024,512]{2,1,0:T(8,128)S(1)}) custom-call(bf16[4,1024,1024]{2,1,0:T(8,128)(2,1)} %shard_map.104.halves, f32[1,4,1024,512]{3,2,1,0:T(8,128)} %panels.3), custom_call_target="tpu_custom_call" | custom-call | flops 24 | bytes 4194304 | tf_op jit(solution)/shard_map/pallas_call | solution.py:349
  48.3 2.5 %shard_map.108 = (f32[512,256]{1,0:T(8,128)}, f32[256,512]{1,0:T(8,128)S(1)}, f32[8,256]{1,0:T(8,128)S(1)}, f32[2,64,1024]{2,1,0:T(8,128)S(1)}, f32[2,64,1024]{2,1,0:T(8,128)S(1)}) custom-call(s32[3]{0:T(128)S(1)} %pad_add_fusion.place.where, f32[512,256]{1,0:T(8,128)S(1)} %get-tuple-element.77.kept_in, f32[512,256]{1,0:T(8,128)S(1)} %collective-permute-done.in_chip, ...), custom_call_target="tpu_custom_call" | custom-call | flops 3221225472 | bytes 4194304 | tf_op jit(solution)/shard_map/pallas_call | solution.py:178
  53.7 2.5 %collective-permute-start.6 = (f32[64,1024]{1,0:T(8,128)S(1)}, f32[64,1024]{1,0:T(8,128)S(1)}, u32[]{:S(2)}, u32[]{:S(2)}) collective-permute-start(f32[64,1024]{1,0:T(8,128)S(1)} %get-tuple-element.97), channel_id=1, source_target_pairs={{0,2},{1,3},{2,0},{3,1},{4,6},{5,7},{6,4},{7,5},{8,10},{9,11},{10,... | collective-permute-start | bytes 786440 | tf_op jit(solution)/shard_map/ppermute | solution.py:612
  56.2 2.9 %shard_map.112 = (f32[2,136,1024]{2,1,0:T(8,128)S(1)}, f32[2,136,1024]{2,1,0:T(8,128)S(1)}) custom-call(s32[3]{0:T(128)S(1)} %pad_add_fusion.place.where, f32[8,256]{1,0:T(8,128)S(1)} %get-tuple-element.99.squares, f32[256,512]{1,0:T(8,128)S(1)} %get-tuple-element.100.turned, f32[4,512]{1,0:T(4,128)S(1)} %bitcast.29, ...), custom_call_target="tpu_custom_call" | custom-call | flops 24 | bytes 4194304 | tf_op jit(solution)/shard_map/pallas_call | solution.py:232
  59.6 3.2 %collective-permute-done.6 = f32[64,1024]{1,0:T(8,128)S(1)} collective-permute-done((f32[64,1024]{1,0:T(8,128)S(1)}, f32[64,1024]{1,0:T(8,128)S(1)}, u32[]{:S(2)}, u32[]{:S(2)}) %collective-permute-start.6) | collective-permute-done | bytes 262176 | tf_op jit(solution)/shard_map/ppermute | solution.py:612
  64.2 1.8 %collective-permute-start.7 = (f32[64,1024]{1,0:T(8,128)S(1)}, f32[64,1024]{1,0:T(8,128)S(1)}, u32[]{:S(2)}, u32[]{:S(2)}) collective-permute-start(f32[64,1024]{1,0:T(8,128)S(1)} %get-tuple-element.102), channel_id=1, source_target_pairs={{0,2},{1,3},{2,0},{3,1},{4,6},{5,7},{6,4},{7,5},{8,10},{9,11},{10,... | collective-permute-start | bytes 786440 | tf_op jit(solution)/shard_map/ppermute | solution.py:617
  66.7 2.3 %shard_map.114.refs_0_ = f32[1024,1024]{1,0:T(8,128)S(1)} custom-call(f32[1,3,1024,1024]{3,2,1,0:T(8,128)} %panels.5), custom_call_target="tpu_custom_call" | custom-call | flops 24 | bytes 4194304 | tf_op jit(solution)/shard_map/pallas_call | solution.py:370
  69.0 4.6 %collective-permute-done.8.refs_1_ = f32[64,1024]{1,0:T(8,128)S(1)} collective-permute-done((f32[64,1024]{1,0:T(8,128)S(1)}, f32[64,1024]{1,0:T(8,128)S(1)}, u32[]{:S(2)}, u32[]{:S(2)}) %collective-permute-start.8) | collective-permute-done | bytes 262176 | tf_op jit(solution)/shard_map/ppermute | solution.py:623
  73.5 2.2 %shard_map.115 = (f32[64,1024]{1,0:T(8,128)S(1)}, f32[64,1024]{1,0:T(8,128)S(1)}) custom-call(s32[3]{0:T(128)S(1)} %pad_add_fusion.place.where, f32[64,1024]{1,0:T(8,128)S(1)} %bitcast.21, bf16[4,1024,1024]{2,1,0:T(8,128)(2,1)S(1)} %get-tuple-element.88.halves, f32[64,1024]{1,0:T(8,128)S(1)} %add.77.refs_0_, f32[64,1024]{1,0:T(8,128)S(1)} %collective-permute-done.8.refs_1_), custom_call_target="tpu_custom_call" | custom-call | flops 1610612736 | bytes 4194304 | tf_op jit(solution)/shard_map/pallas_call | solution.py:418
  76.6 1.8 %collective-permute-start.13 = (f32[64,1024]{1,0:T(8,128)S(1)}, f32[64,1024]{1,0:T(8,128)S(1)}, u32[]{:S(2)}, u32[]{:S(2)}) collective-permute-start(f32[64,1024]{1,0:T(8,128)S(1)} %slice.22), channel_id=1, source_target_pairs={{0,2},{1,3},{2,0},{3,1},{4,6},{5,7},{6,4},{7,5},{8,10},{9,11},{10,... | collective-permute-start | bytes 786440 | tf_op jit(solution)/shard_map/ppermute | solution.py:629
  80.1 3.3 %shard_map.116 = (f32[64,1024]{1,0:T(8,128)S(1)}, f32[8,128]{1,0:T(8,128)S(1)}, f32[1024,128]{1,0:T(8,128)S(1)}, f32[64,1024]{1,0:T(8,128)S(1)}) custom-call(s32[3]{0:T(128)S(1)} %pad_add_fusion.place.where, f32[64,1024]{1,0:T(8,128)S(1)} %get-tuple-element.112.left, bf16[4,1024,1024]{2,1,0:T(8,128)(2,1)S(1)} %get-tuple-element.88.halves, ...), custom_call_target="tpu_custom_call" | custom-call | flops 24 | bytes 4194304 | tf_op jit(solution)/shard_map/pallas_call | solution.py:468
  86.0 1.8 %collective-permute-start.16 = (f32[72,1024]{1,0:T(8,128)S(1)}, f32[72,1024]{1,0:T(8,128)S(1)}, u32[]{:S(2)}, u32[]{:S(2)}) collective-permute-start(f32[72,1024]{1,0:T(8,128)S(1)} %slice.24), channel_id=1, source_target_pairs={{0,2},{1,3},{2,0},{3,1},{4,6},{5,7},{6,4},{7,5},{8,10},{9,11},{10,... | collective-permute-start | bytes 884744 | tf_op jit(solution)/shard_map/ppermute | solution.py:629
  87.9 3.7 %shard_map.117 = f32[72,1024]{1,0:T(8,128)S(1)} custom-call(s32[3]{0:T(128)S(1)} %pad_add_fusion.place.where, f32[1024,128]{1,0:T(8,128)S(1)} %get-tuple-element.117.value, f32[8,128]{1,0:T(8,128)S(1)} %get-tuple-element.118.squares, f32[1,3,1024,1024]{3,2,1,0:T(8,128)} %panels.5), custom_call_target="tpu_custom_call" | custom-call | flops 24 | bytes 4194304 | tf_op jit(solution)/shard_map/pallas_call | solution.py:499
  93.9 2.9 %collective-permute-start.17 = (f32[72,1024]{1,0:T(8,128)S(1)}, f32[72,1024]{1,0:T(8,128)S(1)}, u32[]{:S(2)}, u32[]{:S(2)}) collective-permute-start(f32[72,1024]{1,0:T(8,128)S(1)} %fusion.1), channel_id=1, source_target_pairs={{0,4},{8,12},{16,20},{24,28},{1,5},{9,13},{17,21},{25,29},{2,6},{1... | collective-permute-start | bytes 884744 | tf_op jit(solution)/shard_map/ppermute | solution.py:656
  110.4 26.5 %collective-permute-done.25 = f32[8,128]{1,0:T(8,128)S(1)} collective-permute-done((f32[8,128]{1,0:T(8,128)S(1)}, f32[8,128]{1,0:T(8,128)S(1)}, u32[]{:S(2)}, u32[]{:S(2)}) %collective-permute-start.25) | collective-permute-done | bytes 4128 | tf_op jit(solution)/shard_map/ppermute | solution.py:701
  (83 shorter events, 32.2 us)
Async XLA Ops:
  3.3 22.9 %all-to-all-start = ((f32[32,16,256]{2,1,0:T(8,128)}), f32[32,16,256]{2,1,0:T(8,128)S(1)}, u32[]{:S(2)}, u32[]{:S(2)}) async-start(f32[32,16,256]{2,1,0:T(8,128)} %bitcast.4), calls=%async_computation | async-start | bytes 1048576 | tf_op jit(solution)/shard_map/all_to_all | solution.py:581
  29.8 3.8 %collective-permute-start = (f32[512,256]{1,0:T(8,128)S(1)}, f32[512,256]{1,0:T(8,128)S(1)}, u32[]{:S(2)}, u32[]{:S(2)}) collective-permute-start(f32[512,256]{1,0:T(8,128)S(1)} %get-tuple-element.78), channel_id=1, source_target_pairs={{0,1},{1,0},{2,3},{4,5},{5,4},{6,7},{8,9},{9,8},{10,11},{12,13},{1... | collective-permute-start | bytes 1572872 | tf_op jit(solution)/shard_map/ppermute | solution.py:595
  33.7 14.6 %collective-permute-start.1 = (f32[512,256]{1,0:T(8,128)S(1)}, f32[512,256]{1,0:T(8,128)S(1)}, u32[]{:S(2)}, u32[]{:S(2)}) collective-permute-start(f32[512,256]{1,0:T(8,128)S(1)} %add.75), channel_id=1, source_target_pairs={{0,2},{1,3},{4,6},{5,7},{8,10},{9,11},{12,14},{13,15},{16,18},{17,... | collective-permute-start | bytes 1572872 | tf_op jit(solution)/shard_map/ppermute | solution.py:598
  38.2 9.3 %collective-permute-start.2 = (f32[256,256]{1,0:T(8,128)S(1)}, f32[256,256]{1,0:T(8,128)S(1)}, u32[]{:S(2)}, u32[]{:S(2)}) collective-permute-start(f32[256,256]{1,0:T(8,128)S(1)} %get-tuple-element.83.top), channel_id=1, source_target_pairs={{0,1},{4,5},{8,9},{12,13},{16,17},{20,21},{24,25},{28,29}} | collective-permute-start | bytes 786440 | tf_op jit(solution)/shard_map/ppermute | solution.py:600
  40.2 7.4 %collective-permute-start.3 = (f32[256,256]{1,0:T(8,128)S(1)}, f32[256,256]{1,0:T(8,128)S(1)}, u32[]{:S(2)}, u32[]{:S(2)}) collective-permute-start(f32[256,256]{1,0:T(8,128)S(1)} %get-tuple-element.84.bottom), channel_id=1, source_target_pairs={{0,1},{4,5},{8,9},{12,13},{16,17},{20,21},{24,25},{28,29}} | collective-permute-start | bytes 786440 | tf_op jit(solution)/shard_map/ppermute | solution.py:600
  50.8 1.9 %collective-permute-start.4 = (f32[2,64,1024]{2,1,0:T(8,128)S(1)}, f32[2,64,1024]{2,1,0:T(8,128)S(1)}, u32[]{:S(2)}, u32[]{:S(2)}) collective-permute-start(f32[2,64,1024]{2,1,0:T(8,128)S(1)} %get-tuple-element.92), channel_id=1, source_target_pairs={{0,1},{1,0},{2,3},{3,2},{4,5},{5,4},{6,7},{7,6},{8,9},{9,8},{10,11... | collective-permute-start | bytes 1572872 | tf_op jit(solution)/shard_map/ppermute | solution.py:608
  53.3 5.7 %collective-permute-start.5 = (f32[2,64,1024]{2,1,0:T(8,128)S(1)}, f32[2,64,1024]{2,1,0:T(8,128)S(1)}, u32[]{:S(2)}, u32[]{:S(2)}) collective-permute-start(f32[2,64,1024]{2,1,0:T(8,128)S(1)} %get-tuple-element.95), channel_id=1, source_target_pairs={{0,1},{1,0},{2,3},{3,2},{4,5},{5,4},{6,7},{7,6},{8,9},{9,8},{10,11... | collective-permute-start | bytes 1572872 | tf_op jit(solution)/shard_map/ppermute | solution.py:613
  53.7 9.2 %collective-permute-start.6 = (f32[64,1024]{1,0:T(8,128)S(1)}, f32[64,1024]{1,0:T(8,128)S(1)}, u32[]{:S(2)}, u32[]{:S(2)}) collective-permute-start(f32[64,1024]{1,0:T(8,128)S(1)} %get-tuple-element.97), channel_id=1, source_target_pairs={{0,2},{1,3},{2,0},{3,1},{4,6},{5,7},{6,4},{7,5},{8,10},{9,11},{10,... | collective-permute-start | bytes 786440 | tf_op jit(solution)/shard_map/ppermute | solution.py:612
  62.9 3.1 %collective-permute-start.9 = (f32[2,136,1024]{2,1,0:T(8,128)S(1)}, f32[2,136,1024]{2,1,0:T(8,128)S(1)}, u32[]{:S(2)}, u32[]{:S(2)}) collective-permute-start(f32[2,136,1024]{2,1,0:T(8,128)S(1)} %get-tuple-element.106), channel_id=1, source_target_pairs={{0,1},{1,0},{2,3},{3,2},{4,5},{5,4},{6,7},{7,6},{8,9},{9,8},{10,11... | collective-permute-start | bytes 3342344 | tf_op jit(solution)/shard_map/ppermute | solution.py:618
  62.9 10.6 %collective-permute-start.8 = (f32[64,1024]{1,0:T(8,128)S(1)}, f32[64,1024]{1,0:T(8,128)S(1)}, u32[]{:S(2)}, u32[]{:S(2)}) collective-permute-start(f32[64,1024]{1,0:T(8,128)S(1)} %add.77.refs_0_), channel_id=1, source_target_pairs={{4,0},{12,8},{20,16},{28,24},{5,1},{13,9},{21,17},{29,25},{6,2},{1... | collective-permute-start | bytes 786440 | tf_op jit(solution)/shard_map/ppermute | solution.py:623
  64.2 11.5 %collective-permute-start.7 = (f32[64,1024]{1,0:T(8,128)S(1)}, f32[64,1024]{1,0:T(8,128)S(1)}, u32[]{:S(2)}, u32[]{:S(2)}) collective-permute-start(f32[64,1024]{1,0:T(8,128)S(1)} %get-tuple-element.102), channel_id=1, source_target_pairs={{0,2},{1,3},{2,0},{3,1},{4,6},{5,7},{6,4},{7,5},{8,10},{9,11},{10,... | collective-permute-start | bytes 786440 | tf_op jit(solution)/shard_map/ppermute | solution.py:617
  75.8 7.6 %collective-permute-start.10 = (f32[64,1024]{1,0:T(8,128)S(1)}, f32[64,1024]{1,0:T(8,128)S(1)}, u32[]{:S(2)}, u32[]{:S(2)}) collective-permute-start(f32[64,1024]{1,0:T(8,128)S(1)} %get-tuple-element.141), channel_id=1, source_target_pairs={{8,12},{24,28},{9,13},{25,29},{10,14},{26,30},{11,15},{27,31}} | collective-permute-start | bytes 786440 | tf_op jit(solution)/shard_map/ppermute | solution.py:666
  76.6 8.0 %collective-permute-start.13 = (f32[64,1024]{1,0:T(8,128)S(1)}, f32[64,1024]{1,0:T(8,128)S(1)}, u32[]{:S(2)}, u32[]{:S(2)}) collective-permute-start(f32[64,1024]{1,0:T(8,128)S(1)} %slice.22), channel_id=1, source_target_pairs={{0,2},{1,3},{2,0},{3,1},{4,6},{5,7},{6,4},{7,5},{8,10},{9,11},{10,... | collective-permute-start | bytes 786440 | tf_op jit(solution)/shard_map/ppermute | solution.py:629
  78.5 9.4 %collective-permute-start.12 = (f32[64,1024]{1,0:T(8,128)S(1)}, f32[64,1024]{1,0:T(8,128)S(1)}, u32[]{:S(2)}, u32[]{:S(2)}) collective-permute-start(f32[64,1024]{1,0:T(8,128)S(1)} %get-tuple-element.141), channel_id=1, source_target_pairs={{0,4},{16,20},{1,5},{17,21},{2,6},{18,22},{3,7},{19,23}} | collective-permute-start | bytes 786440 | tf_op jit(solution)/shard_map/ppermute | solution.py:664
  83.4 8.2 %collective-permute-start.11 = (f32[64,1024]{1,0:T(8,128)S(1)}, f32[64,1024]{1,0:T(8,128)S(1)}, u32[]{:S(2)}, u32[]{:S(2)}) collective-permute-start(f32[64,1024]{1,0:T(8,128)S(1)} %add.79), channel_id=1, source_target_pairs={{12,4},{28,20},{13,5},{29,21},{14,6},{30,22},{15,7},{31,23}} | collective-permute-start | bytes 786440 | tf_op jit(solution)/shard_map/ppermute | solution.py:667
  84.7 7.5 %collective-permute-start.14 = (f32[64,1024]{1,0:T(8,128)S(1)}, f32[64,1024]{1,0:T(8,128)S(1)}, u32[]{:S(2)}, u32[]{:S(2)}) collective-permute-start(f32[64,1024]{1,0:T(8,128)S(1)} %fusion.3), channel_id=1, source_target_pairs={{0,4},{8,12},{16,20},{24,28},{1,5},{9,13},{17,21},{25,29},{2,6},{1... | collective-permute-start | bytes 786440 | tf_op jit(solution)/shard_map/ppermute | solution.py:673
  86.0 7.8 %collective-permute-start.16 = (f32[72,1024]{1,0:T(8,128)S(1)}, f32[72,1024]{1,0:T(8,128)S(1)}, u32[]{:S(2)}, u32[]{:S(2)}) collective-permute-start(f32[72,1024]{1,0:T(8,128)S(1)} %slice.24), channel_id=1, source_target_pairs={{0,2},{1,3},{2,0},{3,1},{4,6},{5,7},{6,4},{7,5},{8,10},{9,11},{10,... | collective-permute-start | bytes 884744 | tf_op jit(solution)/shard_map/ppermute | solution.py:629
  93.9 7.5 %collective-permute-start.17 = (f32[72,1024]{1,0:T(8,128)S(1)}, f32[72,1024]{1,0:T(8,128)S(1)}, u32[]{:S(2)}, u32[]{:S(2)}) collective-permute-start(f32[72,1024]{1,0:T(8,128)S(1)} %fusion.1), channel_id=1, source_target_pairs={{0,4},{8,12},{16,20},{24,28},{1,5},{9,13},{17,21},{25,29},{2,6},{1... | collective-permute-start | bytes 884744 | tf_op jit(solution)/shard_map/ppermute | solution.py:656
  96.8 4.6 %collective-permute-start.15 = (f32[64,1024]{1,0:T(8,128)S(1)}, f32[64,1024]{1,0:T(8,128)S(1)}, u32[]{:S(2)}, u32[]{:S(2)}) collective-permute-start(f32[64,1024]{1,0:T(8,128)S(1)} %fusion.2.refs_0_), channel_id=1, source_target_pairs={{28,12},{29,13},{30,14},{31,15}} | collective-permute-start | bytes 786440 | tf_op jit(solution)/shard_map/ppermute | solution.py:669
  98.9 3.3 %collective-permute-start.18 = (f32[64,1024]{1,0:T(8,128)S(1)}, f32[64,1024]{1,0:T(8,128)S(1)}, u32[]{:S(2)}, u32[]{:S(2)}) collective-permute-start(f32[64,1024]{1,0:T(8,128)S(1)} %add.86), channel_id=1, source_target_pairs={{4,12},{5,13},{6,14},{7,15}} | collective-permute-start | bytes 786440 | tf_op jit(solution)/shard_map/ppermute | solution.py:664
  99.6 2.6 %collective-permute-start.19 = (f32[64,1024]{1,0:T(8,128)S(1)}, f32[64,1024]{1,0:T(8,128)S(1)}, u32[]{:S(2)}, u32[]{:S(2)}) collective-permute-start(f32[64,1024]{1,0:T(8,128)S(1)} %add.86), channel_id=1, source_target_pairs={{20,12},{21,13},{22,14},{23,15}} | collective-permute-start | bytes 786440 | tf_op jit(solution)/shard_map/ppermute | solution.py:671
  101.5 1.3 collective-permute-start.20
  102.9 3.0 %collective-permute-start.22 = (f32[64,1024]{1,0:T(8,128)S(1)}, f32[64,1024]{1,0:T(8,128)S(1)}, u32[]{:S(2)}, u32[]{:S(2)}) collective-permute-start(f32[64,1024]{1,0:T(8,128)S(1)} %get-tuple-element.143), channel_id=1, source_target_pairs={{12,28},{13,29},{14,30},{15,31}} | collective-permute-start | bytes 786440 | tf_op jit(solution)/shard_map/ppermute | solution.py:684
  107.8 29.1 %collective-permute-start.25 = (f32[8,128]{1,0:T(8,128)S(1)}, f32[8,128]{1,0:T(8,128)S(1)}, u32[]{:S(2)}, u32[]{:S(2)}) collective-permute-start(f32[8,128]{1,0:T(8,128)S(1)} %add.92), channel_id=1, source_target_pairs={{4,0},{12,8},{20,16},{28,24},{5,1},{13,9},{21,17},{29,25},{6,2},{1... | collective-permute-start | bytes 12296 | tf_op jit(solution)/shard_map/ppermute | solution.py:701
  (7 other events, 27.1 us)

commit v4 on v2

--- a/solution.py
+++ b/solution.py
@@ -658,8 +658,6 @@
             ]
         if count:
             value, tail = more
-            if tier > 1:
-                term, tail = lax.optimization_barrier((term, tail))
             term = following + term
             from_left = lax.ppermute(term, "leaf", direct_left)
             if tier == 1:

time: 138 us -> 138 us (level)
  no operation moved by 1% of the time
where the time goes in v4:
time: 138 us
  waiting for transfers between devices  47.9 us (35%)
  Pallas kernels  46.2 us (33%)
  starting transfers between devices  39 us (28%)
  local copies, waits for them, and re-layouts  2.85 us (2%)
    ppermute x3, waiting for transfers between devices, local(): widths = widths + lax.ppermute(widths, 'leaf', steps)  26.8 us
    pallas_call x1, Pallas kernels, prepared(): pl.pallas_call(prepare_kernel, out_shape=pltpu.HBM((4, rows, rows), jnp.b...  8.44 us
    all_to_all x1, starting transfers between devices, local(): lax.all_to_all(picked.reshape(block_count, block_rows // block_count, col...  7.3 us
    all_to_all x1, waiting for transfers between devices, local(): lax.all_to_all(picked.reshape(block_count, block_rows // block_count, col...  7.1 us
    pallas_call x3, Pallas kernels, solve(): pl.pallas_call(functools.partial(solve_kernel, tier, last, with_tail), ou...  6.28 us
    pallas_call x1, Pallas kernels, loaded(): pl.pallas_call(load_kernel, out_shape=(pltpu.VMEM(halves.shape, jnp.bfloa...  5.92 us
    ppermute x1, waiting for transfers between devices, local(): lax.ppermute(mine, 'leaf', pairs)  4.55 us
    pallas_call x1, Pallas kernels, more_tails(): pl.pallas_call(functools.partial(tails_kernel, tier), out_shape=[shaped(*...  3.72 us
  transfers between devices with their start and end apart: 27, of which 10 were waited for; matrix products, arithmetic and copies ran while one was open for 0% of the time, Pallas kernels for 28%

profile of v4, /device:TPU:0, one launch (start us, length us, event | category | flops | bytes accessed | tf_op | source)
XLA Modules:
  0.0 137.7 jit_solution(4576260183795425544)
XLA Ops:
  0.6 2.5 %shard_map.103 = f32[512,256]{1,0:T(8,128)} custom-call(s32[1,512]{1,0:T(1,128)} %bitcast.31, f32[512,256]{1,0:T(8,128)} %rows.1), custom_call_target="tpu_custom_call" | custom-call | flops 1610612736 | bytes 4194304 | tf_op jit(solution)/shard_map/pallas_call | solution.py:79
  3.3 7.3 %all-to-all-start = ((f32[32,16,256]{2,1,0:T(8,128)}), f32[32,16,256]{2,1,0:T(8,128)S(1)}, u32[]{:S(2)}, u32[]{:S(2)}) async-start(f32[32,16,256]{2,1,0:T(8,128)} %bitcast.4), calls=%async_computation | async-start | bytes 1048576 | tf_op jit(solution)/shard_map/all_to_all | solution.py:581
  10.6 8.4 %shard_map.104.halves = bf16[4,1024,1024]{2,1,0:T(8,128)(2,1)} custom-call(f32[1,1024,1024]{2,1,0:T(8,128)} %inverse, f32[1,3,1024,1024]{3,2,1,0:T(8,128)} %panels.5), custom_call_target="tpu_custom_call" | custom-call | flops 25769803776 | bytes 4194304 | tf_op jit(solution)/shard_map/pallas_call | solution.py:318
  19.0 7.1 %all-to-all-done = f32[32,16,256]{2,1,0:T(8,128)S(1)} async-done(((f32[32,16,256]{2,1,0:T(8,128)}), f32[32,16,256]{2,1,0:T(8,128)S(1)}, u32[]{:S(2)}, u32[]{:S(2)}) %all-to-all-start) | async-done | bytes 524320 | tf_op jit(solution)/shard_map/all_to_all | solution.py:581
  26.1 2.2 %copy-done.1 = f32[2048,512]{1,0:T(8,128)S(1)} copy-done((f32[2048,512]{1,0:T(8,128)S(1)}, f32[2048,512]{1,0:T(8,128)}, u32[]{:S(2)}) %copy-start.1) | copy-done | bytes 4194328
  29.8 1.9 %collective-permute-start = (f32[512,256]{1,0:T(8,128)S(1)}, f32[512,256]{1,0:T(8,128)S(1)}, u32[]{:S(2)}, u32[]{:S(2)}) collective-permute-start(f32[512,256]{1,0:T(8,128)S(1)} %get-tuple-element.74), channel_id=1, source_target_pairs={{0,1},{1,0},{2,3},{4,5},{5,4},{6,7},{8,9},{9,8},{10,11},{12,13},{1... | collective-permute-start | bytes 1572872 | tf_op jit(solution)/shard_map/ppermute | solution.py:595
  31.8 1.9 %collective-permute-done.in_chip = f32[512,256]{1,0:T(8,128)S(1)} collective-permute-done((f32[512,256]{1,0:T(8,128)S(1)}, f32[512,256]{1,0:T(8,128)S(1)}, u32[]{:S(2)}, u32[]{:S(2)}) %collective-permute-start) | collective-permute-done | bytes 524320 | tf_op jit(solution)/shard_map/ppermute | solution.py:595
  33.7 2.9 %collective-permute-start.1 = (f32[512,256]{1,0:T(8,128)S(1)}, f32[512,256]{1,0:T(8,128)S(1)}, u32[]{:S(2)}, u32[]{:S(2)}) collective-permute-start(f32[512,256]{1,0:T(8,128)S(1)} %add.75), channel_id=1, source_target_pairs={{0,2},{1,3},{4,6},{5,7},{8,10},{9,11},{12,14},{13,15},{16,18},{17,... | collective-permute-start | bytes 1572872 | tf_op jit(solution)/shard_map/ppermute | solution.py:598
  38.2 2.0 %collective-permute-start.2 = (f32[256,256]{1,0:T(8,128)S(1)}, f32[256,256]{1,0:T(8,128)S(1)}, u32[]{:S(2)}, u32[]{:S(2)}) collective-permute-start(f32[256,256]{1,0:T(8,128)S(1)} %get-tuple-element.79.top), channel_id=1, source_target_pairs={{0,1},{4,5},{8,9},{12,13},{16,17},{20,21},{24,25},{28,29}} | collective-permute-start | bytes 786440 | tf_op jit(solution)/shard_map/ppermute | solution.py:600
  41.6 5.9 %shard_map.107 = (bf16[4,1024,1024]{2,1,0:T(8,128)(2,1)S(1)}, f32[4,1024,512]{2,1,0:T(8,128)S(1)}) custom-call(bf16[4,1024,1024]{2,1,0:T(8,128)(2,1)} %shard_map.104.halves, f32[1,4,1024,512]{3,2,1,0:T(8,128)} %panels.3), custom_call_target="tpu_custom_call" | custom-call | flops 24 | bytes 4194304 | tf_op jit(solution)/shard_map/pallas_call | solution.py:349
  48.3 2.5 %shard_map.108 = (f32[512,256]{1,0:T(8,128)}, f32[256,512]{1,0:T(8,128)S(1)}, f32[8,256]{1,0:T(8,128)S(1)}, f32[2,64,1024]{2,1,0:T(8,128)S(1)}, f32[2,64,1024]{2,1,0:T(8,128)S(1)}) custom-call(s32[3]{0:T(128)S(1)} %pad_add_fusion.place.where, f32[512,256]{1,0:T(8,128)S(1)} %get-tuple-element.73.kept_in, f32[512,256]{1,0:T(8,128)S(1)} %collective-permute-done.in_chip, ...), custom_call_target="tpu_custom_call" | custom-call | flops 3221225472 | bytes 4194304 | tf_op jit(solution)/shard_map/pallas_call | solution.py:178
  53.7 2.5 %collective-permute-start.6 = (f32[64,1024]{1,0:T(8,128)S(1)}, f32[64,1024]{1,0:T(8,128)S(1)}, u32[]{:S(2)}, u32[]{:S(2)}) collective-permute-start(f32[64,1024]{1,0:T(8,128)S(1)} %get-tuple-element.93), channel_id=1, source_target_pairs={{0,2},{1,3},{2,0},{3,1},{4,6},{5,7},{6,4},{7,5},{8,10},{9,11},{10,... | collective-permute-start | bytes 786440 | tf_op jit(solution)/shard_map/ppermute | solution.py:612
  56.2 2.9 %shard_map.112 = (f32[2,136,1024]{2,1,0:T(8,128)S(1)}, f32[2,136,1024]{2,1,0:T(8,128)S(1)}) custom-call(s32[3]{0:T(128)S(1)} %pad_add_fusion.place.where, f32[8,256]{1,0:T(8,128)S(1)} %get-tuple-element.95.squares, f32[256,512]{1,0:T(8,128)S(1)} %get-tuple-element.96.turned, f32[4,512]{1,0:T(4,128)S(1)} %bitcast.29, f32[4,1024,512]{2,1,0:T(8,128)S(1)} %get-tuple-element.82.panels), custom_call_target="tpu_custom_call" | custom-call | flops 24 | bytes 4194304 | tf_op jit(solution)/shard_map/pallas_call | solution.py:232
  59.6 3.2 %collective-permute-done.6 = f32[64,1024]{1,0:T(8,128)S(1)} collective-permute-done((f32[64,1024]{1,0:T(8,128)S(1)}, f32[64,1024]{1,0:T(8,128)S(1)}, u32[]{:S(2)}, u32[]{:S(2)}) %collective-permute-start.6) | collective-permute-done | bytes 262176 | tf_op jit(solution)/shard_map/ppermute | solution.py:612
  64.2 1.8 %collective-permute-start.7 = (f32[64,1024]{1,0:T(8,128)S(1)}, f32[64,1024]{1,0:T(8,128)S(1)}, u32[]{:S(2)}, u32[]{:S(2)}) collective-permute-start(f32[64,1024]{1,0:T(8,128)S(1)} %get-tuple-element.98), channel_id=1, source_target_pairs={{0,2},{1,3},{2,0},{3,1},{4,6},{5,7},{6,4},{7,5},{8,10},{9,11},{10,... | collective-permute-start | bytes 786440 | tf_op jit(solution)/shard_map/ppermute | solution.py:617
  66.7 2.3 %shard_map.114.refs_0_ = f32[1024,1024]{1,0:T(8,128)S(1)} custom-call(f32[1,3,1024,1024]{3,2,1,0:T(8,128)} %panels.5), custom_call_target="tpu_custom_call" | custom-call | flops 24 | bytes 4194304 | tf_op jit(solution)/shard_map/pallas_call | solution.py:370
  69.0 4.6 %collective-permute-done.8.refs_1_ = f32[64,1024]{1,0:T(8,128)S(1)} collective-permute-done((f32[64,1024]{1,0:T(8,128)S(1)}, f32[64,1024]{1,0:T(8,128)S(1)}, u32[]{:S(2)}, u32[]{:S(2)}) %collective-permute-start.8) | collective-permute-done | bytes 262176 | tf_op jit(solution)/shard_map/ppermute | solution.py:623
  73.5 2.2 %shard_map.115 = (f32[64,1024]{1,0:T(8,128)S(1)}, f32[64,1024]{1,0:T(8,128)S(1)}) custom-call(s32[3]{0:T(128)S(1)} %pad_add_fusion.place.where, f32[64,1024]{1,0:T(8,128)S(1)} %bitcast.21, bf16[4,1024,1024]{2,1,0:T(8,128)(2,1)S(1)} %get-tuple-element.84.halves, f32[64,1024]{1,0:T(8,128)S(1)} %add.77.refs_0_, f32[64,1024]{1,0:T(8,128)S(1)} %collective-permute-done.8.refs_1_), custom_call_target="tpu_custom_call" | custom-call | flops 1610612736 | bytes 4194304 | tf_op jit(solution)/shard_map/pallas_call | solution.py:418
  76.6 1.8 %collective-permute-start.13 = (f32[64,1024]{1,0:T(8,128)S(1)}, f32[64,1024]{1,0:T(8,128)S(1)}, u32[]{:S(2)}, u32[]{:S(2)}) collective-permute-start(f32[64,1024]{1,0:T(8,128)S(1)} %slice.22), channel_id=1, source_target_pairs={{0,2},{1,3},{2,0},{3,1},{4,6},{5,7},{6,4},{7,5},{8,10},{9,11},{10,... | collective-permute-start | bytes 786440 | tf_op jit(solution)/shard_map/ppermute | solution.py:629
  80.1 3.3 %shard_map.116 = (f32[64,1024]{1,0:T(8,128)S(1)}, f32[8,128]{1,0:T(8,128)S(1)}, f32[1024,128]{1,0:T(8,128)S(1)}, f32[64,1024]{1,0:T(8,128)S(1)}) custom-call(s32[3]{0:T(128)S(1)} %pad_add_fusion.place.where, f32[64,1024]{1,0:T(8,128)S(1)} %get-tuple-element.108.left, bf16[4,1024,1024]{2,1,0:T(8,128)(2,1)S(1)} %get-tuple-element.84.halves, ...), custom_call_target="tpu_custom_call" | custom-call | flops 24 | bytes 4194304 | tf_op jit(solution)/shard_map/pallas_call | solution.py:468
  86.0 1.8 %collective-permute-start.18 = (f32[72,1024]{1,0:T(8,128)S(1)}, f32[72,1024]{1,0:T(8,128)S(1)}, u32[]{:S(2)}, u32[]{:S(2)}) collective-permute-start(f32[72,1024]{1,0:T(8,128)S(1)} %slice.24), channel_id=1, source_target_pairs={{0,2},{1,3},{2,0},{3,1},{4,6},{5,7},{6,4},{7,5},{8,10},{9,11},{10,... | collective-permute-start | bytes 884744 | tf_op jit(solution)/shard_map/ppermute | solution.py:629
  87.9 3.7 %shard_map.117 = f32[72,1024]{1,0:T(8,128)S(1)} custom-call(s32[3]{0:T(128)S(1)} %pad_add_fusion.place.where, f32[1024,128]{1,0:T(8,128)S(1)} %get-tuple-element.113.value, f32[8,128]{1,0:T(8,128)S(1)} %get-tuple-element.114.squares, f32[1,3,1024,1024]{3,2,1,0:T(8,128)} %panels.5), custom_call_target="tpu_custom_call" | custom-call | flops 24 | bytes 4194304 | tf_op jit(solution)/shard_map/pallas_call | solution.py:499
  93.9 2.9 %collective-permute-start.19 = (f32[72,1024]{1,0:T(8,128)S(1)}, f32[72,1024]{1,0:T(8,128)S(1)}, u32[]{:S(2)}, u32[]{:S(2)}) collective-permute-start(f32[72,1024]{1,0:T(8,128)S(1)} %fusion.1), channel_id=1, source_target_pairs={{0,4},{8,12},{16,20},{24,28},{1,5},{9,13},{17,21},{25,29},{2,6},{1... | collective-permute-start | bytes 884744 | tf_op jit(solution)/shard_map/ppermute | solution.py:656
  110.4 26.8 %collective-permute-done.25 = f32[8,128]{1,0:T(8,128)S(1)} collective-permute-done((f32[8,128]{1,0:T(8,128)S(1)}, f32[8,128]{1,0:T(8,128)S(1)}, u32[]{:S(2)}, u32[]{:S(2)}) %collective-permute-start.25) | collective-permute-done | bytes 4128 | tf_op jit(solution)/shard_map/ppermute | solution.py:698
  (82 shorter events, 32.2 us)
Async XLA Ops:
  3.3 22.9 %all-to-all-start = ((f32[32,16,256]{2,1,0:T(8,128)}), f32[32,16,256]{2,1,0:T(8,128)S(1)}, u32[]{:S(2)}, u32[]{:S(2)}) async-start(f32[32,16,256]{2,1,0:T(8,128)} %bitcast.4), calls=%async_computation | async-start | bytes 1048576 | tf_op jit(solution)/shard_map/all_to_all | solution.py:581
  29.8 3.8 %collective-permute-start = (f32[512,256]{1,0:T(8,128)S(1)}, f32[512,256]{1,0:T(8,128)S(1)}, u32[]{:S(2)}, u32[]{:S(2)}) collective-permute-start(f32[512,256]{1,0:T(8,128)S(1)} %get-tuple-element.74), channel_id=1, source_target_pairs={{0,1},{1,0},{2,3},{4,5},{5,4},{6,7},{8,9},{9,8},{10,11},{12,13},{1... | collective-permute-start | bytes 1572872 | tf_op jit(solution)/shard_map/ppermute | solution.py:595
  33.7 14.6 %collective-permute-start.1 = (f32[512,256]{1,0:T(8,128)S(1)}, f32[512,256]{1,0:T(8,128)S(1)}, u32[]{:S(2)}, u32[]{:S(2)}) collective-permute-start(f32[512,256]{1,0:T(8,128)S(1)} %add.75), channel_id=1, source_target_pairs={{0,2},{1,3},{4,6},{5,7},{8,10},{9,11},{12,14},{13,15},{16,18},{17,... | collective-permute-start | bytes 1572872 | tf_op jit(solution)/shard_map/ppermute | solution.py:598
  38.2 9.3 %collective-permute-start.2 = (f32[256,256]{1,0:T(8,128)S(1)}, f32[256,256]{1,0:T(8,128)S(1)}, u32[]{:S(2)}, u32[]{:S(2)}) collective-permute-start(f32[256,256]{1,0:T(8,128)S(1)} %get-tuple-element.79.top), channel_id=1, source_target_pairs={{0,1},{4,5},{8,9},{12,13},{16,17},{20,21},{24,25},{28,29}} | collective-permute-start | bytes 786440 | tf_op jit(solution)/shard_map/ppermute | solution.py:600
  40.2 7.4 %collective-permute-start.3 = (f32[256,256]{1,0:T(8,128)S(1)}, f32[256,256]{1,0:T(8,128)S(1)}, u32[]{:S(2)}, u32[]{:S(2)}) collective-permute-start(f32[256,256]{1,0:T(8,128)S(1)} %get-tuple-element.80.bottom), channel_id=1, source_target_pairs={{0,1},{4,5},{8,9},{12,13},{16,17},{20,21},{24,25},{28,29}} | collective-permute-start | bytes 786440 | tf_op jit(solution)/shard_map/ppermute | solution.py:600
  50.8 1.9 %collective-permute-start.4 = (f32[2,64,1024]{2,1,0:T(8,128)S(1)}, f32[2,64,1024]{2,1,0:T(8,128)S(1)}, u32[]{:S(2)}, u32[]{:S(2)}) collective-permute-start(f32[2,64,1024]{2,1,0:T(8,128)S(1)} %get-tuple-element.88), channel_id=1, source_target_pairs={{0,1},{1,0},{2,3},{3,2},{4,5},{5,4},{6,7},{7,6},{8,9},{9,8},{10,11... | collective-permute-start | bytes 1572872 | tf_op jit(solution)/shard_map/ppermute | solution.py:608
  53.3 5.7 %collective-permute-start.5 = (f32[2,64,1024]{2,1,0:T(8,128)S(1)}, f32[2,64,1024]{2,1,0:T(8,128)S(1)}, u32[]{:S(2)}, u32[]{:S(2)}) collective-permute-start(f32[2,64,1024]{2,1,0:T(8,128)S(1)} %get-tuple-element.91), channel_id=1, source_target_pairs={{0,1},{1,0},{2,3},{3,2},{4,5},{5,4},{6,7},{7,6},{8,9},{9,8},{10,11... | collective-permute-start | bytes 1572872 | tf_op jit(solution)/shard_map/ppermute | solution.py:613
  53.7 9.2 %collective-permute-start.6 = (f32[64,1024]{1,0:T(8,128)S(1)}, f32[64,1024]{1,0:T(8,128)S(1)}, u32[]{:S(2)}, u32[]{:S(2)}) collective-permute-start(f32[64,1024]{1,0:T(8,128)S(1)} %get-tuple-element.93), channel_id=1, source_target_pairs={{0,2},{1,3},{2,0},{3,1},{4,6},{5,7},{6,4},{7,5},{8,10},{9,11},{10,... | collective-permute-start | bytes 786440 | tf_op jit(solution)/shard_map/ppermute | solution.py:612
  62.9 3.2 %collective-permute-start.9 = (f32[2,136,1024]{2,1,0:T(8,128)S(1)}, f32[2,136,1024]{2,1,0:T(8,128)S(1)}, u32[]{:S(2)}, u32[]{:S(2)}) collective-permute-start(f32[2,136,1024]{2,1,0:T(8,128)S(1)} %get-tuple-element.102), channel_id=1, source_target_pairs={{0,1},{1,0},{2,3},{3,2},{4,5},{5,4},{6,7},{7,6},{8,9},{9,8},{10,11... | collective-permute-start | bytes 3342344 | tf_op jit(solution)/shard_map/ppermute | solution.py:618
  62.9 10.6 %collective-permute-start.8 = (f32[64,1024]{1,0:T(8,128)S(1)}, f32[64,1024]{1,0:T(8,128)S(1)}, u32[]{:S(2)}, u32[]{:S(2)}) collective-permute-start(f32[64,1024]{1,0:T(8,128)S(1)} %add.77.refs_0_), channel_id=1, source_target_pairs={{4,0},{12,8},{20,16},{28,24},{5,1},{13,9},{21,17},{29,25},{6,2},{1... | collective-permute-start | bytes 786440 | tf_op jit(solution)/shard_map/ppermute | solution.py:623
  64.2 11.5 %collective-permute-start.7 = (f32[64,1024]{1,0:T(8,128)S(1)}, f32[64,1024]{1,0:T(8,128)S(1)}, u32[]{:S(2)}, u32[]{:S(2)}) collective-permute-start(f32[64,1024]{1,0:T(8,128)S(1)} %get-tuple-element.98), channel_id=1, source_target_pairs={{0,2},{1,3},{2,0},{3,1},{4,6},{5,7},{6,4},{7,5},{8,10},{9,11},{10,... | collective-permute-start | bytes 786440 | tf_op jit(solution)/shard_map/ppermute | solution.py:617
  75.8 7.6 %collective-permute-start.10 = (f32[64,1024]{1,0:T(8,128)S(1)}, f32[64,1024]{1,0:T(8,128)S(1)}, u32[]{:S(2)}, u32[]{:S(2)}) collective-permute-start(f32[64,1024]{1,0:T(8,128)S(1)} %get-tuple-element.133), channel_id=1, source_target_pairs={{8,12},{24,28},{9,13},{25,29},{10,14},{26,30},{11,15},{27,31}} | collective-permute-start | bytes 786440 | tf_op jit(solution)/shard_map/ppermute | solution.py:664
  76.6 8.0 %collective-permute-start.13 = (f32[64,1024]{1,0:T(8,128)S(1)}, f32[64,1024]{1,0:T(8,128)S(1)}, u32[]{:S(2)}, u32[]{:S(2)}) collective-permute-start(f32[64,1024]{1,0:T(8,128)S(1)} %slice.22), channel_id=1, source_target_pairs={{0,2},{1,3},{2,0},{3,1},{4,6},{5,7},{6,4},{7,5},{8,10},{9,11},{10,... | collective-permute-start | bytes 786440 | tf_op jit(solution)/shard_map/ppermute | solution.py:629
  78.5 9.4 %collective-permute-start.12 = (f32[64,1024]{1,0:T(8,128)S(1)}, f32[64,1024]{1,0:T(8,128)S(1)}, u32[]{:S(2)}, u32[]{:S(2)}) collective-permute-start(f32[64,1024]{1,0:T(8,128)S(1)} %get-tuple-element.133), channel_id=1, source_target_pairs={{0,4},{16,20},{1,5},{17,21},{2,6},{18,22},{3,7},{19,23}} | collective-permute-start | bytes 786440 | tf_op jit(solution)/shard_map/ppermute | solution.py:662
  83.4 8.2 %collective-permute-start.11 = (f32[64,1024]{1,0:T(8,128)S(1)}, f32[64,1024]{1,0:T(8,128)S(1)}, u32[]{:S(2)}, u32[]{:S(2)}) collective-permute-start(f32[64,1024]{1,0:T(8,128)S(1)} %add.79), channel_id=1, source_target_pairs={{12,4},{28,20},{13,5},{29,21},{14,6},{30,22},{15,7},{31,23}} | collective-permute-start | bytes 786440 | tf_op jit(solution)/shard_map/ppermute | solution.py:665
  84.7 7.5 %collective-permute-start.14 = (f32[64,1024]{1,0:T(8,128)S(1)}, f32[64,1024]{1,0:T(8,128)S(1)}, u32[]{:S(2)}, u32[]{:S(2)}) collective-permute-start(f32[64,1024]{1,0:T(8,128)S(1)} %fusion.3), channel_id=1, source_target_pairs={{0,4},{8,12},{16,20},{24,28},{1,5},{9,13},{17,21},{25,29},{2,6},{1... | collective-permute-start | bytes 786440 | tf_op jit(solution)/shard_map/ppermute | solution.py:670
  86.0 7.8 %collective-permute-start.18 = (f32[72,1024]{1,0:T(8,128)S(1)}, f32[72,1024]{1,0:T(8,128)S(1)}, u32[]{:S(2)}, u32[]{:S(2)}) collective-permute-start(f32[72,1024]{1,0:T(8,128)S(1)} %slice.24), channel_id=1, source_target_pairs={{0,2},{1,3},{2,0},{3,1},{4,6},{5,7},{6,4},{7,5},{8,10},{9,11},{10,... | collective-permute-start | bytes 884744 | tf_op jit(solution)/shard_map/ppermute | solution.py:629
  93.9 7.5 %collective-permute-start.19 = (f32[72,1024]{1,0:T(8,128)S(1)}, f32[72,1024]{1,0:T(8,128)S(1)}, u32[]{:S(2)}, u32[]{:S(2)}) collective-permute-start(f32[72,1024]{1,0:T(8,128)S(1)} %fusion.1), channel_id=1, source_target_pairs={{0,4},{8,12},{16,20},{24,28},{1,5},{9,13},{17,21},{25,29},{2,6},{1... | collective-permute-start | bytes 884744 | tf_op jit(solution)/shard_map/ppermute | solution.py:656
  96.9 5.3 %collective-permute-start.16 = (f32[64,1024]{1,0:T(8,128)S(1)}, f32[64,1024]{1,0:T(8,128)S(1)}, u32[]{:S(2)}, u32[]{:S(2)}) collective-permute-start(f32[64,1024]{1,0:T(8,128)S(1)} %add.83), channel_id=1, source_target_pairs={{4,12},{5,13},{6,14},{7,15}} | collective-permute-start | bytes 786440 | tf_op jit(solution)/shard_map/ppermute | solution.py:662
  97.6 4.6 %collective-permute-start.17 = (f32[64,1024]{1,0:T(8,128)S(1)}, f32[64,1024]{1,0:T(8,128)S(1)}, u32[]{:S(2)}, u32[]{:S(2)}) collective-permute-start(f32[64,1024]{1,0:T(8,128)S(1)} %add.83), channel_id=1, source_target_pairs={{20,12},{21,13},{22,14},{23,15}} | collective-permute-start | bytes 786440 | tf_op jit(solution)/shard_map/ppermute | solution.py:668
  98.2 4.0 %collective-permute-start.15 = (f32[64,1024]{1,0:T(8,128)S(1)}, f32[64,1024]{1,0:T(8,128)S(1)}, u32[]{:S(2)}, u32[]{:S(2)}) collective-permute-start(f32[64,1024]{1,0:T(8,128)S(1)} %fusion.2.refs_0_), channel_id=1, source_target_pairs={{28,12},{29,13},{30,14},{31,15}} | collective-permute-start | bytes 786440 | tf_op jit(solution)/shard_map/ppermute | solution.py:667
  101.5 1.3 collective-permute-start.20
  102.9 3.0 %collective-permute-start.22 = (f32[64,1024]{1,0:T(8,128)S(1)}, f32[64,1024]{1,0:T(8,128)S(1)}, u32[]{:S(2)}, u32[]{:S(2)}) collective-permute-start(f32[64,1024]{1,0:T(8,128)S(1)} %get-tuple-element.135), channel_id=1, source_target_pairs={{12,28},{13,29},{14,30},{15,31}} | collective-permute-start | bytes 786440 | tf_op jit(solution)/shard_map/ppermute | solution.py:681
  107.8 29.4 %collective-permute-start.25 = (f32[8,128]{1,0:T(8,128)S(1)}, f32[8,128]{1,0:T(8,128)S(1)}, u32[]{:S(2)}, u32[]{:S(2)}) collective-permute-start(f32[8,128]{1,0:T(8,128)S(1)} %add.92), channel_id=1, source_target_pairs={{4,0},{12,8},{20,16},{28,24},{5,1},{13,9},{21,17},{29,25},{6,2},{1... | collective-permute-start | bytes 12296 | tf_op jit(solution)/shard_map/ppermute | solution.py:698
  (7 other events, 27.1 us)

commit v5 on v4

--- a/solution.py
+++ b/solution.py
@@ -401,6 +401,21 @@
     for part in parts[1:]:
         total = total + part[...]
     return own_rhs[...] - total
+
+
+def sum_kernel(first, second, out):
+    out[...] = first[...] + second[...]
+
+
+def pending_sum(first, second):
+    return pl.pallas_call(
+        sum_kernel,
+        out_shape=shaped(*first.shape),
+        in_specs=[VMEM, VMEM],
+        out_specs=VMEM,
+        cost_estimate=cost(first.shape[1] ** 2 * 256),
+        compiler_params=limit(4),
+    )(first, second)
 
 
 def direct_kernel(tier, count, where, own_rhs, halves, *refs):
@@ -666,7 +681,7 @@
             else:
                 next_early = lax.ppermute(following, "leaf", early)
                 from_right = lax.ppermute(term, "leaf", direct_right)
-                parts = [following, next_early, from_left, from_right]
+                parts = [pending_sum(following, next_early), from_left, from_right]
             following = rest[0] + lax.ppermute(rest[0] + tail, "leaf", onward)
             rest = rest[1:]
             waiting = []

time: 138 us -> 139 us (level)
  no operation moved by 1% of the time
where the time goes in v5:
time: 139 us; the launch traced here: 138 us
  waiting for transfers between devices  48.4 us (35%)
  Pallas kernels  46.3 us (33%)
  starting transfers between devices  39 us (28%)
  local copies, waits for them, and re-layouts  2.85 us (2%)
    ppermute x3, waiting for transfers between devices, local(): widths = widths + lax.ppermute(widths, 'leaf', steps)  27.4 us
    pallas_call x1, Pallas kernels, prepared(): pl.pallas_call(prepare_kernel, out_shape=pltpu.HBM((4, rows, rows), jnp.b...  8.44 us
    all_to_all x1, starting transfers between devices, local(): lax.all_to_all(picked.reshape(block_count, block_rows // block_count, col...  7.3 us
    all_to_all x1, waiting for transfers between devices, local(): lax.all_to_all(picked.reshape(block_count, block_rows // block_count, col...  7.1 us
    pallas_call x3, Pallas kernels, solve(): pl.pallas_call(functools.partial(solve_kernel, tier, last, with_tail), ou...  6.28 us
    pallas_call x1, Pallas kernels, loaded(): pl.pallas_call(load_kernel, out_shape=(pltpu.VMEM(halves.shape, jnp.bfloa...  5.92 us
    ppermute x1, waiting for transfers between devices, local(): lax.ppermute(mine, 'leaf', pairs)  4.55 us
    pallas_call x1, Pallas kernels, more_tails(): pl.pallas_call(functools.partial(tails_kernel, tier), out_shape=[shaped(*...  3.73 us
  transfers between devices with their start and end apart: 27, of which 10 were waited for; matrix products, arithmetic and copies ran while one was open for 0% of the time, Pallas kernels for 28%

profile of v5, /device:TPU:0, one launch (start us, length us, event | category | flops | bytes accessed | tf_op | source)
XLA Modules:
  0.0 138.3 jit_solution(2746328948268113427)
XLA Ops:
  0.6 2.5 %shard_map.103 = f32[512,256]{1,0:T(8,128)} custom-call(s32[1,512]{1,0:T(1,128)} %bitcast.31, f32[512,256]{1,0:T(8,128)} %rows.1), custom_call_target="tpu_custom_call" | custom-call | flops 1610612736 | bytes 4194304 | tf_op jit(solution)/shard_map/pallas_call | solution.py:79
  3.3 7.3 %all-to-all-start = ((f32[32,16,256]{2,1,0:T(8,128)}), f32[32,16,256]{2,1,0:T(8,128)S(1)}, u32[]{:S(2)}, u32[]{:S(2)}) async-start(f32[32,16,256]{2,1,0:T(8,128)} %bitcast.4), calls=%async_computation | async-start | bytes 1048576 | tf_op jit(solution)/shard_map/all_to_all | solution.py:596
  10.6 8.4 %shard_map.104.halves = bf16[4,1024,1024]{2,1,0:T(8,128)(2,1)} custom-call(f32[1,1024,1024]{2,1,0:T(8,128)} %inverse, f32[1,3,1024,1024]{3,2,1,0:T(8,128)} %panels.5), custom_call_target="tpu_custom_call" | custom-call | flops 25769803776 | bytes 4194304 | tf_op jit(solution)/shard_map/pallas_call | solution.py:318
  19.0 7.1 %all-to-all-done = f32[32,16,256]{2,1,0:T(8,128)S(1)} async-done(((f32[32,16,256]{2,1,0:T(8,128)}), f32[32,16,256]{2,1,0:T(8,128)S(1)}, u32[]{:S(2)}, u32[]{:S(2)}) %all-to-all-start) | async-done | bytes 524320 | tf_op jit(solution)/shard_map/all_to_all | solution.py:596
  26.1 2.2 %copy-done.1 = f32[2048,512]{1,0:T(8,128)S(1)} copy-done((f32[2048,512]{1,0:T(8,128)S(1)}, f32[2048,512]{1,0:T(8,128)}, u32[]{:S(2)}) %copy-start.1) | copy-done | bytes 4194328
  29.8 1.9 %collective-permute-start = (f32[512,256]{1,0:T(8,128)S(1)}, f32[512,256]{1,0:T(8,128)S(1)}, u32[]{:S(2)}, u32[]{:S(2)}) collective-permute-start(f32[512,256]{1,0:T(8,128)S(1)} %get-tuple-element.74), channel_id=1, source_target_pairs={{0,1},{1,0},{2,3},{4,5},{5,4},{6,7},{8,9},{9,8},{10,11},{12,13},{1... | collective-permute-start | bytes 1572872 | tf_op jit(solution)/shard_map/ppermute | solution.py:610
  31.8 1.9 %collective-permute-done.in_chip = f32[512,256]{1,0:T(8,128)S(1)} collective-permute-done((f32[512,256]{1,0:T(8,128)S(1)}, f32[512,256]{1,0:T(8,128)S(1)}, u32[]{:S(2)}, u32[]{:S(2)}) %collective-permute-start) | collective-permute-done | bytes 524320 | tf_op jit(solution)/shard_map/ppermute | solution.py:610
  33.7 2.9 %collective-permute-start.1 = (f32[512,256]{1,0:T(8,128)S(1)}, f32[512,256]{1,0:T(8,128)S(1)}, u32[]{:S(2)}, u32[]{:S(2)}) collective-permute-start(f32[512,256]{1,0:T(8,128)S(1)} %add.75), channel_id=1, source_target_pairs={{0,2},{1,3},{4,6},{5,7},{8,10},{9,11},{12,14},{13,15},{16,18},{17,... | collective-permute-start | bytes 1572872 | tf_op jit(solution)/shard_map/ppermute | solution.py:613
  38.2 2.0 %collective-permute-start.2 = (f32[256,256]{1,0:T(8,128)S(1)}, f32[256,256]{1,0:T(8,128)S(1)}, u32[]{:S(2)}, u32[]{:S(2)}) collective-permute-start(f32[256,256]{1,0:T(8,128)S(1)} %get-tuple-element.79.top), channel_id=1, source_target_pairs={{0,1},{4,5},{8,9},{12,13},{16,17},{20,21},{24,25},{28,29}} | collective-permute-start | bytes 786440 | tf_op jit(solution)/shard_map/ppermute | solution.py:615
  41.6 5.9 %shard_map.107 = (bf16[4,1024,1024]{2,1,0:T(8,128)(2,1)S(1)}, f32[4,1024,512]{2,1,0:T(8,128)S(1)}) custom-call(bf16[4,1024,1024]{2,1,0:T(8,128)(2,1)} %shard_map.104.halves, f32[1,4,1024,512]{3,2,1,0:T(8,128)} %panels.3), custom_call_target="tpu_custom_call" | custom-call | flops 24 | bytes 4194304 | tf_op jit(solution)/shard_map/pallas_call | solution.py:349
  48.3 2.5 %shard_map.108 = (f32[512,256]{1,0:T(8,128)}, f32[256,512]{1,0:T(8,128)S(1)}, f32[8,256]{1,0:T(8,128)S(1)}, f32[2,64,1024]{2,1,0:T(8,128)S(1)}, f32[2,64,1024]{2,1,0:T(8,128)S(1)}) custom-call(s32[3]{0:T(128)S(1)} %pad_add_fusion.place.where, f32[512,256]{1,0:T(8,128)S(1)} %get-tuple-element.73.kept_in, f32[512,256]{1,0:T(8,128)S(1)} %collective-permute-done.in_chip, ...), custom_call_target="tpu_custom_call" | custom-call | flops 3221225472 | bytes 4194304 | tf_op jit(solution)/shard_map/pallas_call | solution.py:178
  53.7 2.5 %collective-permute-start.6 = (f32[64,1024]{1,0:T(8,128)S(1)}, f32[64,1024]{1,0:T(8,128)S(1)}, u32[]{:S(2)}, u32[]{:S(2)}) collective-permute-start(f32[64,1024]{1,0:T(8,128)S(1)} %get-tuple-element.93), channel_id=1, source_target_pairs={{0,2},{1,3},{2,0},{3,1},{4,6},{5,7},{6,4},{7,5},{8,10},{9,11},{10,... | collective-permute-start | bytes 786440 | tf_op jit(solution)/shard_map/ppermute | solution.py:627
  56.2 2.9 %shard_map.112 = (f32[2,136,1024]{2,1,0:T(8,128)S(1)}, f32[2,136,1024]{2,1,0:T(8,128)S(1)}) custom-call(s32[3]{0:T(128)S(1)} %pad_add_fusion.place.where, f32[8,256]{1,0:T(8,128)S(1)} %get-tuple-element.95.squares, f32[256,512]{1,0:T(8,128)S(1)} %get-tuple-element.96.turned, f32[4,512]{1,0:T(4,128)S(1)} %bitcast.29, f32[4,1024,512]{2,1,0:T(8,128)S(1)} %get-tuple-element.82.panels), custom_call_target="tpu_custom_call" | custom-call | flops 24 | bytes 4194304 | tf_op jit(solution)/shard_map/pallas_call | solution.py:232
  59.6 3.2 %collective-permute-done.6 = f32[64,1024]{1,0:T(8,128)S(1)} collective-permute-done((f32[64,1024]{1,0:T(8,128)S(1)}, f32[64,1024]{1,0:T(8,128)S(1)}, u32[]{:S(2)}, u32[]{:S(2)}) %collective-permute-start.6) | collective-permute-done | bytes 262176 | tf_op jit(solution)/shard_map/ppermute | solution.py:627
  64.2 1.8 %collective-permute-start.7 = (f32[64,1024]{1,0:T(8,128)S(1)}, f32[64,1024]{1,0:T(8,128)S(1)}, u32[]{:S(2)}, u32[]{:S(2)}) collective-permute-start(f32[64,1024]{1,0:T(8,128)S(1)} %get-tuple-element.98), channel_id=1, source_target_pairs={{0,2},{1,3},{2,0},{3,1},{4,6},{5,7},{6,4},{7,5},{8,10},{9,11},{10,... | collective-permute-start | bytes 786440 | tf_op jit(solution)/shard_map/ppermute | solution.py:632
  66.7 2.3 %shard_map.114.refs_0_ = f32[1024,1024]{1,0:T(8,128)S(1)} custom-call(f32[1,3,1024,1024]{3,2,1,0:T(8,128)} %panels.5), custom_call_target="tpu_custom_call" | custom-call | flops 24 | bytes 4194304 | tf_op jit(solution)/shard_map/pallas_call | solution.py:370
  69.0 4.6 %collective-permute-done.8.refs_1_ = f32[64,1024]{1,0:T(8,128)S(1)} collective-permute-done((f32[64,1024]{1,0:T(8,128)S(1)}, f32[64,1024]{1,0:T(8,128)S(1)}, u32[]{:S(2)}, u32[]{:S(2)}) %collective-permute-start.8) | collective-permute-done | bytes 262176 | tf_op jit(solution)/shard_map/ppermute | solution.py:638
  73.5 2.2 %shard_map.115 = (f32[64,1024]{1,0:T(8,128)S(1)}, f32[64,1024]{1,0:T(8,128)S(1)}) custom-call(s32[3]{0:T(128)S(1)} %pad_add_fusion.place.where, f32[64,1024]{1,0:T(8,128)S(1)} %bitcast.21, bf16[4,1024,1024]{2,1,0:T(8,128)(2,1)S(1)} %get-tuple-element.84.halves, f32[64,1024]{1,0:T(8,128)S(1)} %add.77.refs_0_, f32[64,1024]{1,0:T(8,128)S(1)} %collective-permute-done.8.refs_1_), custom_call_target="tpu_custom_call" | custom-call | flops 1610612736 | bytes 4194304 | tf_op jit(solution)/shard_map/pallas_call | solution.py:433
  76.7 1.8 %collective-permute-start.13 = (f32[64,1024]{1,0:T(8,128)S(1)}, f32[64,1024]{1,0:T(8,128)S(1)}, u32[]{:S(2)}, u32[]{:S(2)}) collective-permute-start(f32[64,1024]{1,0:T(8,128)S(1)} %slice.22), channel_id=1, source_target_pairs={{0,2},{1,3},{2,0},{3,1},{4,6},{5,7},{6,4},{7,5},{8,10},{9,11},{10,... | collective-permute-start | bytes 786440 | tf_op jit(solution)/shard_map/ppermute | solution.py:644
  80.1 3.3 %shard_map.116 = (f32[64,1024]{1,0:T(8,128)S(1)}, f32[8,128]{1,0:T(8,128)S(1)}, f32[1024,128]{1,0:T(8,128)S(1)}, f32[64,1024]{1,0:T(8,128)S(1)}) custom-call(s32[3]{0:T(128)S(1)} %pad_add_fusion.place.where, f32[64,1024]{1,0:T(8,128)S(1)} %get-tuple-element.108.left, bf16[4,1024,1024]{2,1,0:T(8,128)(2,1)S(1)} %get-tuple-element.84.halves, ...), custom_call_target="tpu_custom_call" | custom-call | flops 24 | bytes 4194304 | tf_op jit(solution)/shard_map/pallas_call | solution.py:483
  86.0 1.8 %collective-permute-start.18 = (f32[72,1024]{1,0:T(8,128)S(1)}, f32[72,1024]{1,0:T(8,128)S(1)}, u32[]{:S(2)}, u32[]{:S(2)}) collective-permute-start(f32[72,1024]{1,0:T(8,128)S(1)} %slice.24), channel_id=1, source_target_pairs={{0,2},{1,3},{2,0},{3,1},{4,6},{5,7},{6,4},{7,5},{8,10},{9,11},{10,... | collective-permute-start | bytes 884744 | tf_op jit(solution)/shard_map/ppermute | solution.py:644
  87.9 3.7 %shard_map.117 = f32[72,1024]{1,0:T(8,128)S(1)} custom-call(s32[3]{0:T(128)S(1)} %pad_add_fusion.place.where, f32[1024,128]{1,0:T(8,128)S(1)} %get-tuple-element.113.value, f32[8,128]{1,0:T(8,128)S(1)} %get-tuple-element.114.squares, f32[1,3,1024,1024]{3,2,1,0:T(8,128)} %panels.5), custom_call_target="tpu_custom_call" | custom-call | flops 24 | bytes 4194304 | tf_op jit(solution)/shard_map/pallas_call | solution.py:514
  93.9 2.9 %collective-permute-start.19 = (f32[72,1024]{1,0:T(8,128)S(1)}, f32[72,1024]{1,0:T(8,128)S(1)}, u32[]{:S(2)}, u32[]{:S(2)}) collective-permute-start(f32[72,1024]{1,0:T(8,128)S(1)} %fusion.1), channel_id=1, source_target_pairs={{0,4},{8,12},{16,20},{24,28},{1,5},{9,13},{17,21},{25,29},{2,6},{1... | collective-permute-start | bytes 884744 | tf_op jit(solution)/shard_map/ppermute | solution.py:671
  110.4 27.4 %collective-permute-done.25 = f32[8,128]{1,0:T(8,128)S(1)} collective-permute-done((f32[8,128]{1,0:T(8,128)S(1)}, f32[8,128]{1,0:T(8,128)S(1)}, u32[]{:S(2)}, u32[]{:S(2)}) %collective-permute-start.25) | collective-permute-done | bytes 4128 | tf_op jit(solution)/shard_map/ppermute | solution.py:713
  (83 shorter events, 32.2 us)
Async XLA Ops:
  3.3 22.9 %all-to-all-start = ((f32[32,16,256]{2,1,0:T(8,128)}), f32[32,16,256]{2,1,0:T(8,128)S(1)}, u32[]{:S(2)}, u32[]{:S(2)}) async-start(f32[32,16,256]{2,1,0:T(8,128)} %bitcast.4), calls=%async_computation | async-start | bytes 1048576 | tf_op jit(solution)/shard_map/all_to_all | solution.py:596
  29.8 3.8 %collective-permute-start = (f32[512,256]{1,0:T(8,128)S(1)}, f32[512,256]{1,0:T(8,128)S(1)}, u32[]{:S(2)}, u32[]{:S(2)}) collective-permute-start(f32[512,256]{1,0:T(8,128)S(1)} %get-tuple-element.74), channel_id=1, source_target_pairs={{0,1},{1,0},{2,3},{4,5},{5,4},{6,7},{8,9},{9,8},{10,11},{12,13},{1... | collective-permute-start | bytes 1572872 | tf_op jit(solution)/shard_map/ppermute | solution.py:610
  33.7 14.6 %collective-permute-start.1 = (f32[512,256]{1,0:T(8,128)S(1)}, f32[512,256]{1,0:T(8,128)S(1)}, u32[]{:S(2)}, u32[]{:S(2)}) collective-permute-start(f32[512,256]{1,0:T(8,128)S(1)} %add.75), channel_id=1, source_target_pairs={{0,2},{1,3},{4,6},{5,7},{8,10},{9,11},{12,14},{13,15},{16,18},{17,... | collective-permute-start | bytes 1572872 | tf_op jit(solution)/shard_map/ppermute | solution.py:613
  38.2 9.3 %collective-permute-start.2 = (f32[256,256]{1,0:T(8,128)S(1)}, f32[256,256]{1,0:T(8,128)S(1)}, u32[]{:S(2)}, u32[]{:S(2)}) collective-permute-start(f32[256,256]{1,0:T(8,128)S(1)} %get-tuple-element.79.top), channel_id=1, source_target_pairs={{0,1},{4,5},{8,9},{12,13},{16,17},{20,21},{24,25},{28,29}} | collective-permute-start | bytes 786440 | tf_op jit(solution)/shard_map/ppermute | solution.py:615
  40.2 7.4 %collective-permute-start.3 = (f32[256,256]{1,0:T(8,128)S(1)}, f32[256,256]{1,0:T(8,128)S(1)}, u32[]{:S(2)}, u32[]{:S(2)}) collective-permute-start(f32[256,256]{1,0:T(8,128)S(1)} %get-tuple-element.80.bottom), channel_id=1, source_target_pairs={{0,1},{4,5},{8,9},{12,13},{16,17},{20,21},{24,25},{28,29}} | collective-permute-start | bytes 786440 | tf_op jit(solution)/shard_map/ppermute | solution.py:615
  50.8 1.9 %collective-permute-start.4 = (f32[2,64,1024]{2,1,0:T(8,128)S(1)}, f32[2,64,1024]{2,1,0:T(8,128)S(1)}, u32[]{:S(2)}, u32[]{:S(2)}) collective-permute-start(f32[2,64,1024]{2,1,0:T(8,128)S(1)} %get-tuple-element.88), channel_id=1, source_target_pairs={{0,1},{1,0},{2,3},{3,2},{4,5},{5,4},{6,7},{7,6},{8,9},{9,8},{10,11... | collective-permute-start | bytes 1572872 | tf_op jit(solution)/shard_map/ppermute | solution.py:623
  53.3 5.7 %collective-permute-start.5 = (f32[2,64,1024]{2,1,0:T(8,128)S(1)}, f32[2,64,1024]{2,1,0:T(8,128)S(1)}, u32[]{:S(2)}, u32[]{:S(2)}) collective-permute-start(f32[2,64,1024]{2,1,0:T(8,128)S(1)} %get-tuple-element.91), channel_id=1, source_target_pairs={{0,1},{1,0},{2,3},{3,2},{4,5},{5,4},{6,7},{7,6},{8,9},{9,8},{10,11... | collective-permute-start | bytes 1572872 | tf_op jit(solution)/shard_map/ppermute | solution.py:628
  53.7 9.2 %collective-permute-start.6 = (f32[64,1024]{1,0:T(8,128)S(1)}, f32[64,1024]{1,0:T(8,128)S(1)}, u32[]{:S(2)}, u32[]{:S(2)}) collective-permute-start(f32[64,1024]{1,0:T(8,128)S(1)} %get-tuple-element.93), channel_id=1, source_target_pairs={{0,2},{1,3},{2,0},{3,1},{4,6},{5,7},{6,4},{7,5},{8,10},{9,11},{10,... | collective-permute-start | bytes 786440 | tf_op jit(solution)/shard_map/ppermute | solution.py:627
  62.9 3.1 %collective-permute-start.9 = (f32[2,136,1024]{2,1,0:T(8,128)S(1)}, f32[2,136,1024]{2,1,0:T(8,128)S(1)}, u32[]{:S(2)}, u32[]{:S(2)}) collective-permute-start(f32[2,136,1024]{2,1,0:T(8,128)S(1)} %get-tuple-element.102), channel_id=1, source_target_pairs={{0,1},{1,0},{2,3},{3,2},{4,5},{5,4},{6,7},{7,6},{8,9},{9,8},{10,11... | collective-permute-start | bytes 3342344 | tf_op jit(solution)/shard_map/ppermute | solution.py:633
  62.9 10.6 %collective-permute-start.8 = (f32[64,1024]{1,0:T(8,128)S(1)}, f32[64,1024]{1,0:T(8,128)S(1)}, u32[]{:S(2)}, u32[]{:S(2)}) collective-permute-start(f32[64,1024]{1,0:T(8,128)S(1)} %add.77.refs_0_), channel_id=1, source_target_pairs={{4,0},{12,8},{20,16},{28,24},{5,1},{13,9},{21,17},{29,25},{6,2},{1... | collective-permute-start | bytes 786440 | tf_op jit(solution)/shard_map/ppermute | solution.py:638
  64.2 11.5 %collective-permute-start.7 = (f32[64,1024]{1,0:T(8,128)S(1)}, f32[64,1024]{1,0:T(8,128)S(1)}, u32[]{:S(2)}, u32[]{:S(2)}) collective-permute-start(f32[64,1024]{1,0:T(8,128)S(1)} %get-tuple-element.98), channel_id=1, source_target_pairs={{0,2},{1,3},{2,0},{3,1},{4,6},{5,7},{6,4},{7,5},{8,10},{9,11},{10,... | collective-permute-start | bytes 786440 | tf_op jit(solution)/shard_map/ppermute | solution.py:632
  75.8 7.6 %collective-permute-start.10 = (f32[64,1024]{1,0:T(8,128)S(1)}, f32[64,1024]{1,0:T(8,128)S(1)}, u32[]{:S(2)}, u32[]{:S(2)}) collective-permute-start(f32[64,1024]{1,0:T(8,128)S(1)} %get-tuple-element.133), channel_id=1, source_target_pairs={{8,12},{24,28},{9,13},{25,29},{10,14},{26,30},{11,15},{27,31}} | collective-permute-start | bytes 786440 | tf_op jit(solution)/shard_map/ppermute | solution.py:679
  76.7 8.0 %collective-permute-start.13 = (f32[64,1024]{1,0:T(8,128)S(1)}, f32[64,1024]{1,0:T(8,128)S(1)}, u32[]{:S(2)}, u32[]{:S(2)}) collective-permute-start(f32[64,1024]{1,0:T(8,128)S(1)} %slice.22), channel_id=1, source_target_pairs={{0,2},{1,3},{2,0},{3,1},{4,6},{5,7},{6,4},{7,5},{8,10},{9,11},{10,... | collective-permute-start | bytes 786440 | tf_op jit(solution)/shard_map/ppermute | solution.py:644
  78.5 9.4 %collective-permute-start.12 = (f32[64,1024]{1,0:T(8,128)S(1)}, f32[64,1024]{1,0:T(8,128)S(1)}, u32[]{:S(2)}, u32[]{:S(2)}) collective-permute-start(f32[64,1024]{1,0:T(8,128)S(1)} %get-tuple-element.133), channel_id=1, source_target_pairs={{0,4},{16,20},{1,5},{17,21},{2,6},{18,22},{3,7},{19,23}} | collective-permute-start | bytes 786440 | tf_op jit(solution)/shard_map/ppermute | solution.py:677
  83.4 8.2 %collective-permute-start.11 = (f32[64,1024]{1,0:T(8,128)S(1)}, f32[64,1024]{1,0:T(8,128)S(1)}, u32[]{:S(2)}, u32[]{:S(2)}) collective-permute-start(f32[64,1024]{1,0:T(8,128)S(1)} %add.79), channel_id=1, source_target_pairs={{12,4},{28,20},{13,5},{29,21},{14,6},{30,22},{15,7},{31,23}} | collective-permute-start | bytes 786440 | tf_op jit(solution)/shard_map/ppermute | solution.py:680
  84.7 7.5 %collective-permute-start.14 = (f32[64,1024]{1,0:T(8,128)S(1)}, f32[64,1024]{1,0:T(8,128)S(1)}, u32[]{:S(2)}, u32[]{:S(2)}) collective-permute-start(f32[64,1024]{1,0:T(8,128)S(1)} %fusion.3), channel_id=1, source_target_pairs={{0,4},{8,12},{16,20},{24,28},{1,5},{9,13},{17,21},{25,29},{2,6},{1... | collective-permute-start | bytes 786440 | tf_op jit(solution)/shard_map/ppermute | solution.py:685
  86.0 7.8 %collective-permute-start.18 = (f32[72,1024]{1,0:T(8,128)S(1)}, f32[72,1024]{1,0:T(8,128)S(1)}, u32[]{:S(2)}, u32[]{:S(2)}) collective-permute-start(f32[72,1024]{1,0:T(8,128)S(1)} %slice.24), channel_id=1, source_target_pairs={{0,2},{1,3},{2,0},{3,1},{4,6},{5,7},{6,4},{7,5},{8,10},{9,11},{10,... | collective-permute-start | bytes 884744 | tf_op jit(solution)/shard_map/ppermute | solution.py:644
  93.9 7.5 %collective-permute-start.19 = (f32[72,1024]{1,0:T(8,128)S(1)}, f32[72,1024]{1,0:T(8,128)S(1)}, u32[]{:S(2)}, u32[]{:S(2)}) collective-permute-start(f32[72,1024]{1,0:T(8,128)S(1)} %fusion.1), channel_id=1, source_target_pairs={{0,4},{8,12},{16,20},{24,28},{1,5},{9,13},{17,21},{25,29},{2,6},{1... | collective-permute-start | bytes 884744 | tf_op jit(solution)/shard_map/ppermute | solution.py:671
  96.9 5.3 %collective-permute-start.15 = (f32[64,1024]{1,0:T(8,128)S(1)}, f32[64,1024]{1,0:T(8,128)S(1)}, u32[]{:S(2)}, u32[]{:S(2)}) collective-permute-start(f32[64,1024]{1,0:T(8,128)S(1)} %fusion.2.first), channel_id=1, source_target_pairs={{28,12},{29,13},{30,14},{31,15}} | collective-permute-start | bytes 786440 | tf_op jit(solution)/shard_map/ppermute | solution.py:682
  97.6 4.7 %collective-permute-start.16 = (f32[64,1024]{1,0:T(8,128)S(1)}, f32[64,1024]{1,0:T(8,128)S(1)}, u32[]{:S(2)}, u32[]{:S(2)}) collective-permute-start(f32[64,1024]{1,0:T(8,128)S(1)} %add.83), channel_id=1, source_target_pairs={{4,12},{5,13},{6,14},{7,15}} | collective-permute-start | bytes 786440 | tf_op jit(solution)/shard_map/ppermute | solution.py:677
  98.3 4.0 %collective-permute-start.17 = (f32[64,1024]{1,0:T(8,128)S(1)}, f32[64,1024]{1,0:T(8,128)S(1)}, u32[]{:S(2)}, u32[]{:S(2)}) collective-permute-start(f32[64,1024]{1,0:T(8,128)S(1)} %add.83), channel_id=1, source_target_pairs={{20,12},{21,13},{22,14},{23,15}} | collective-permute-start | bytes 786440 | tf_op jit(solution)/shard_map/ppermute | solution.py:683
  101.5 1.3 collective-permute-start.20
  103.0 3.0 %collective-permute-start.22 = (f32[64,1024]{1,0:T(8,128)S(1)}, f32[64,1024]{1,0:T(8,128)S(1)}, u32[]{:S(2)}, u32[]{:S(2)}) collective-permute-start(f32[64,1024]{1,0:T(8,128)S(1)} %get-tuple-element.135), channel_id=1, source_target_pairs={{12,28},{13,29},{14,30},{15,31}} | collective-permute-start | bytes 786440 | tf_op jit(solution)/shard_map/ppermute | solution.py:696
  107.9 30.0 %collective-permute-start.25 = (f32[8,128]{1,0:T(8,128)S(1)}, f32[8,128]{1,0:T(8,128)S(1)}, u32[]{:S(2)}, u32[]{:S(2)}) collective-permute-start(f32[8,128]{1,0:T(8,128)S(1)} %add.92), channel_id=1, source_target_pairs={{4,0},{12,8},{20,16},{28,24},{5,1},{13,9},{21,17},{29,25},{6,2},{1... | collective-permute-start | bytes 12296 | tf_op jit(solution)/shard_map/ppermute | solution.py:713
  (7 other events, 27.1 us)
